TPU v7x, 32 devices: a whole 2x2x4 slice. The times are simulated.
32 devices in a mesh: px: 8 (over z, x), py: 4 (over y, core).
Axes of the slice: x: 2, y: 2, z: 4, core: 2. Of those that a mesh axis runs over, the one named last changes fastest.
Arguments:
- displacement: float32 [3, 32, 64, 128], P(None, 'px', 'py'), may hold values from -6 to 6
- velocity: float32 [3, 32, 64, 128], P(None, 'px', 'py'), may hold values from -6 to 6
- inverse_mass: float32 [32, 64, 128], P('px', 'py'), may hold values from 0.5 to 2
- lame_first: float32 [5, 5, 5, 8, 512], P(None, None, None, 'px', 'py'), may hold values from 0.5 to 2
- lame_second: float32 [5, 5, 5, 8, 512], P(None, None, None, 'px', 'py'), may hold values from 0.5 to 2
- level_map: int32 [8, 512], P('px', 'py'), may hold values from 0 to 2, as said below
Outputs:
- new_displacement: float32 [3, 32, 64, 128], P(None, 'px', 'py')
- new_velocity: float32 [3, 32, 64, 128], P(None, 'px', 'py')
Inputs may be any that keep to these rules, and one draw needn't show every extreme that they name: `level_map`: level 2 is the finest. The device whose blocks hold the most finest-level elements holds exactly 96 of them; no device holds more.
All inputs are finite; a program needn't handle non-finite values.
Results may differ from a plain program's by a relative error of at most 0.0003.
Values sent between devices are 32-bit elements; how exact they have to be, the bound alone decides.
No kernel may reach another device: no remote copies, remote signals or barrier semaphores. Data moves between devices by JAX's collectives and lax.ppermute only.
A program may use at most 64 MiB of HBM per device.

v0:
```python
import functools

import jax
import jax.numpy as jnp
import numpy as np
from jax import lax
from jax.experimental import pallas as pl
from jax.experimental.pallas import tpu as pltpu
from jax.sharding import PartitionSpec as P

time_step = 0.1
LEVELS = 3
F32 = jnp.float32
BF16 = jnp.bfloat16


def gll_tables():
    points = np.array([-1.0, -np.sqrt(3.0 / 7.0), 0.0, np.sqrt(3.0 / 7.0), 1.0])
    weights = np.array([0.1, 49.0 / 90.0, 32.0 / 45.0, 49.0 / 90.0, 0.1])
    legendre = (35.0 * points**4 - 30.0 * points**2 + 3.0) / 8.0
    derivative = np.zeros((5, 5))
    for row_index in range(5):
        for col_index in range(5):
            if row_index != col_index:
                derivative[row_index, col_index] = legendre[row_index] / (
                    legendre[col_index] * (points[row_index] - points[col_index])
                )
    derivative[0, 0] = -5.0
    derivative[4, 4] = 5.0
    return (derivative, weights)


D, W = gll_tables()


def split(table):
    high = np.asarray(table, np.float32).astype(BF16)
    low = (np.asarray(table, np.float64) - high.astype(np.float64)).astype(BF16)
    return high, low


def depth_tables(depth):
    lanes = 4 * depth
    table = np.zeros((lanes, 2 * lanes))
    for c in range(depth):
        for i in range(5):
            if 4 * c + i < lanes:
                for k in range(4):
                    table[4 * c + i, 4 * c + k] = D[k, i]
                table[4 * c + i, lanes + (4 * (c + 1)) % lanes] = D[4, i]
    high, low = split(table)
    gradient = np.concatenate([high, high, low], axis=0)
    divergence = np.concatenate([high.T, high.T, low.T], axis=0)
    return gradient, divergence


def weight_table(depth):
    lanes = 4 * depth
    pair = (W[:, None] * W[None, :]).reshape(25, 1)
    main = pair * np.tile(W[:4], depth)[None, :]
    last = pair * np.where(np.arange(lanes) % 4 == 0, W[4], 0.0)[None, :]
    return np.concatenate([main, last], axis=0).astype(np.float32)


def apply5(matrix, x):
    s0, s1 = x[0] + x[4], x[1] + x[3]
    d0, d1 = x[0] - x[4], x[1] - x[3]

    def even(a):
        p, q = (matrix[a, 0] - matrix[a, 4]) / 2, (matrix[a, 1] - matrix[a, 3]) / 2
        return d0 * float(p) + d1 * float(q)

    def odd(a):
        p, q = (matrix[a, 0] + matrix[a, 4]) / 2, (matrix[a, 1] + matrix[a, 3]) / 2
        return s0 * float(p) + s1 * float(q) + x[2] * float(matrix[a, 2])

    e0, e1, e2 = even(0), even(1), even(2)
    o0, o1 = odd(0), odd(1)
    return [e0 + o0, e1 + o1, e2, e1 - o1, e0 - o0]


def halves(x):
    high = x.astype(BF16)
    return high, (x - high.astype(F32)).astype(BF16)


def rolled(x, by):
    return pltpu.roll(x, by % x.shape[0], 0)


def swap_pairs(nx, ny, along_x, odd):
    pairs = []
    for i in range(nx):
        for j in range(ny):
            here, size = (i, nx) if along_x else (j, ny)
            there = here + 1 if (here % 2 == 1) == odd else here - 1
            if 0 <= there < size:
                target = (there, j) if along_x else (i, there)
            else:
                target = (i, j ^ 1) if along_x else (i ^ 1, j)
            if target[0] < nx and target[1] < ny:
                pairs.append((i * ny + j, target[0] * ny + target[1]))
    return pairs


def swap(mesh_sizes, along_x, odd, x):
    return lax.ppermute(x, ("px", "py"), swap_pairs(*mesh_sizes, along_x, odd))


def place(axis, size):
    here = lax.axis_index(axis)
    return lax.rem(here, 2) == 0, here == 0, here == size - 1


def prep_kernel(sizes, rows, own_ref, e_ref, o_ref, weight_ref, u_ref, v_ref, m_ref, lame_ref, level_ref, sel):
    ny, ey, lanes = sizes
    even, first, last = place("py", ny)
    base_v, base_m, base_first, base_second, base_level, total = rows
    tall = 4 * ey

    def left(at):
        return jnp.where(first, 0.0, jnp.where(even, o_ref[at], e_ref[at]))

    def right(at):
        return jnp.where(last, 0.0, jnp.where(even, e_ref[at], o_ref[at]))

    def spread(base, out):
        for j in range(4):
            at = pl.ds(base + j, ey, stride=4)
            out[j, 0:ey, :] = left((at, slice(None)))
            out[j, ey : 2 * ey, :] = own_ref[at, :]
            out[j, 2 * ey : 3 * ey, :] = right((at, slice(None)))
            out[j, 3 * ey :, :] = jnp.zeros((ey, lanes), F32)

    for c in range(3):
        for i in range(4):
            spread((c * 4 + i) * tall, u_ref.at[c, i])
            spread(base_v + (c * 4 + i) * tall, v_ref.at[c, i])
    for i in range(4):
        spread(base_m + i * tall, m_ref.at[i])

    tail = slice(base_first, total)
    sel[0] = left((tail, slice(None)))
    sel[1] = own_ref[tail, :]
    sel[2] = right((tail, slice(None)))

    shape = (2 * ey, lanes)
    sub = lax.broadcasted_iota(jnp.int32, shape, 0)
    lane = lax.broadcasted_iota(jnp.int32, shape, 1)
    ez = lanes // 4
    column = lax.rem(sub, ey) * ez
    main_at = column + lane // 4
    last_at = column + lax.rem(lane // 4 + ez - 1, ez)
    point = lax.rem(lane, 4)
    upper = sub < ey

    def both(row):
        zero = jnp.zeros(shape, F32)
        a = jnp.broadcast_to(sel[0, pl.ds(row, 1), :], shape)
        b = jnp.broadcast_to(sel[1, pl.ds(row, 1), :], shape)
        c = jnp.broadcast_to(sel[2, pl.ds(row, 1), :], shape)
        return jnp.where(upper, a, b), jnp.where(upper, c, zero)

    def gather(x, at):
        return jnp.take_along_axis(x, at, axis=1, mode="promise_in_bounds")

    def body(ij, carry):
        weight = jnp.broadcast_to(weight_ref[pl.ds(ij, 1), :], shape)
        weight_last = jnp.broadcast_to(weight_ref[pl.ds(25 + ij, 1), :], shape)
        for p in range(2):
            start = (base_second - base_first) * p + ij * 5
            points = [both(start + k) for k in range(5)]
            for h in range(2):
                got = [gather(points[k][h], main_at) for k in range(4)]
                main = jnp.where(
                    point < 2, jnp.where(point == 0, got[0], got[1]), jnp.where(point == 2, got[2], got[3])
                )
                lame_ref[p, 0, ij, 2 * ey * h : 2 * ey * (h + 1), :] = main * weight
                lame_ref[p, 1, ij, 2 * ey * h : 2 * ey * (h + 1), :] = gather(points[4][h], last_at) * weight_last
        return carry

    lax.fori_loop(0, 25, body, 0)
    levels = both(base_level - base_first)
    for h in range(2):
        level_ref[0, 2 * ey * h : 2 * ey * (h + 1), :] = gather(levels[h], main_at)
        level_ref[1, 2 * ey * h : 2 * ey * (h + 1), :] = gather(levels[h], last_at)


def forces(tall, windows, keep, us, lame, level, old, new, grad_ref, div_ref, gx, gz, flux_x, flux_z, qy, qz, out):
    lanes = us.shape[-1]
    flat = us[...].reshape(75 * tall, lanes)
    high, low = halves(flat)
    lhs = jnp.concatenate([high, low, high], axis=1)
    gz[...] = jnp.dot(lhs, grad_ref[...], preferred_element_type=F32).reshape(3, 25, tall, 2 * lanes)
    for c in range(3):
        for j in range(5):
            y = apply5(D, [us[c, i, j] for i in range(5)])
            for i in range(5):
                gx[c, 5 * i + j] = y[i]

    inner = (lax.broadcasted_iota(jnp.int32, (8, lanes), 1) > 0).astype(F32)

    def body(i, carry):
        for h in range(tall // 8):
            at = slice(8 * h, 8 * h + 8)
            table = slice(windows[0] + 8 * h, windows[0] + 8 * h + 8)
            stored = slice(windows[1] + 8 * h, windows[1] + 8 * h + 8)
            gy = [apply5(D, [us[c, i, j, at, :] for j in range(5)]) for c in range(3)]
            if keep is not None:
                fresh = [keep(level[e, table, :]) for e in range(2)]
            across = [[], [], []]
            for j in range(5):
                p = 5 * i + j
                grads_x = [gx[c, p, at, :] for c in range(3)]
                grads_y = [gy[c][j] for c in range(3)]
                sums = []
                for e in range(2):
                    grads_z = [gz[c, p, at, e * lanes : (e + 1) * lanes] for c in range(3)]
                    if e == 1:
                        grads_x = [g * inner for g in grads_x]
                        grads_y = [g * inner for g in grads_y]
                    first, second = lame[0, e, p, table, :], lame[1, e, p, table, :]
                    trace = first * (grads_x[0] + grads_y[1] + grads_z[2])
                    twice = second + second
                    stress = [
                        trace + twice * grads_x[0],
                        trace + twice * grads_y[1],
                        second * (grads_y[0] + grads_x[1]),
                        second * (grads_z[0] + grads_x[2]),
                        second * (grads_z[1] + grads_y[2]),
                        trace + twice * grads_z[2],
                    ]
                    if keep is not None:
                        stress = [
                            jnp.where(fresh[e], stress[n], old[n, e, p, stored, :]) for n in range(6)
                        ]
                    if new is not None:
                        for n in range(6):
                            new[n, e, p, at, :] = stress[n]
                    if flux_z is not None:
                        for n in range(3):
                            flux_z[n, e, p, at, :] = stress[3 + n]
                    if e == 1:
                        stress = [x * inner for x in stress[:5]]
                    sums.append(stress)
                xx, yy, xy, xz, yz = [sums[0][n] + sums[1][n] for n in range(5)]
                for c, value in enumerate((xx, xy, xz)):
                    flux_x[c, p, at, :] = value
                for c, value in enumerate((xy, yy, yz)):
                    across[c].append(value)
            for c in range(3):
                y = apply5(D.T, across[c])
                for j in range(5):
                    qy[c, 5 * i + j, at, :] = y[j]
        return carry

    lax.fori_loop(0, 5, body, 0)
    if flux_z is None:
        flux_z = new.at[3:6]
    high0, low0 = halves(flux_z[:, 0].reshape(75 * tall, lanes))
    high1, low1 = halves(flux_z[:, 1].reshape(75 * tall, lanes))
    lhs = jnp.concatenate([high0, high1, low0, low1, high0, high1], axis=1)
    qz[...] = jnp.dot(lhs, div_ref[...], preferred_element_type=F32).reshape(3, 25, tall, lanes)
    for c in range(3):
        ends = None
        for j in (4, 0, 1, 2, 3):
            x = apply5(D.T, [flux_x[c, 5 * i + j] for i in range(5)])
            x = [x[i] + (qy[c, 5 * i + j] + qz[c, 5 * i + j]) for i in range(5)]
            if j == 4:
                ends = [rolled(v, 1) for v in x]
                continue
            for i in range(5):
                out[c, i, j] = x[i] + ends[i] if j == 0 else x[i]


def fill_points(us, c, i, values):
    for j in range(4):
        us[c, i, j] = values[j]
    us[c, i, 4] = rolled(values[0], -1)


def start_kernel(sizes, u_ref, v_ref, m_ref, lame, level, a_ref, b_ref, grad_ref, div_ref,
                 rim_ref, old_ref, total_ref, send_a, send_b, us, gx, gz, flux_x, qy, qz):
    nx, ey, lanes = sizes
    even, _, last = place("px", nx)
    tall = 4 * ey
    wide = 3 * ey
    for c in range(3):
        for i in range(4):
            fill_points(us, c, i, [u_ref[c, i, j] for j in range(4)])
        for j in range(4):
            at = pl.ds(j, wide, stride=4)
            rim = jnp.where(last, 0.0, jnp.where(even, a_ref[c, at, :], b_ref[c, at, :]))
            rim_ref[c, j, 0:wide, :] = rim
            rim_ref[c, j, wide:, :] = jnp.zeros((tall - wide, lanes), F32)
        fill_points(us, c, 4, [rim_ref[c, j] for j in range(4)])
    forces(tall, (0, 0), None, us, lame, level, None, old_ref, grad_ref, div_ref, gx, gz, flux_x, None, qy, qz, total_ref)
    count = wide - 2
    for j in range(4):
        at = slice(j * count, (j + 1) * count)
        mass = m_ref[0, j, 1 : 1 + count, :]
        for c in range(3):
            back = v_ref[c, 0, j, 1 : 1 + count, :] - time_step * mass * total_ref[c, 0, j, 1 : 1 + count, :]
            ahead = total_ref[c, 4, j, 1 : 1 + count, :]
            send_a[c, at, :] = jnp.where(even, ahead, back)
            send_b[c, at, :] = jnp.where(even, back, ahead)
        send_a[3, at, :] = mass
        send_b[3, at, :] = mass


def second_kernel(sizes, u_ref, rim_ref, v_ref, m_ref, total_ref, a_ref, b_ref, old, lame, level, grad_ref, div_ref,
                  u_out, v_out, m_out, total_out, send_a, send_b,
                  got, us, gx, gz, flux_x, flux_z, qy, qz, total):
    nx, ey, lanes = sizes
    even, first, last = place("px", nx)
    tall, count = 4 * ey, 3 * ey - 2
    low, high = ey - 2, 3 * ey - 2
    got[...] = jnp.zeros(got.shape, F32)
    for j in range(4):
        at = slice(j * count, (j + 1) * count)
        for c in range(4):
            got[0, c, j, 1 : 1 + count, :] = jnp.where(last, 0.0, jnp.where(even, a_ref[c, at, :], b_ref[c, at, :]))
        for c in range(3):
            got[1, c, j, 1 : 1 + count, :] = jnp.where(first, 0.0, jnp.where(even, b_ref[c, at, :], a_ref[c, at, :]))
    for c in range(3):
        for i in range(5):
            values = []
            for j in range(4):
                force = total_ref[c, i, j]
                mass = m_ref[i, j] if i < 4 else got[0, 3, j]
                if i == 0:
                    force = force + got[1, c, j]
                before = v_ref[c, i, j] if i < 4 else got[0, c, j]
                position = u_ref[c, i, j] if i < 4 else rim_ref[c, j]
                speed = before - time_step * mass * force
                position = position + time_step * speed
                u_out[c, i, j] = position[low:high]
                v_out[c, i, j] = speed[low:high]
                if c == 0:
                    m_out[i, j] = mass[low:high]
                values.append(position)
            fill_points(us, c, i, values)
    forces(tall, (0, 0), lambda level_of: level_of > 1.5, us, lame, level, old, None, grad_ref, div_ref,
           gx, gz, flux_x, flux_z, qy, qz, total)
    for c in range(3):
        for i in range(5):
            for j in range(4):
                total_out[c, i, j] = total[c, i, j, low:high, :]
        for j in range(4):
            back, ahead = total_out[c, 0, j], total_out[c, 4, j]
            send_a[c, j] = jnp.where(even, ahead, back)
            send_b[c, j] = jnp.where(even, back, ahead)


def later_kernel(sizes, final, u_ref, v_ref, m_ref, total_ref, a_ref, b_ref, old, lame, level, grad_ref, div_ref, *refs):
    nx, ey, lanes = sizes
    if final:
        u_out, v_out, total_out, send_a, send_b, us, gx, gz, flux_x, flux_z, qy, qz = refs
        new, keep, windows = None, lambda level_of: level_of > 1.5, (ey - 2, 0)
    else:
        u_out, v_out, new, total_out, send_a, send_b, us, gx, gz, flux_x, qy, qz = refs
        flux_z, keep, windows = None, lambda level_of: level_of > 0.5, (ey - 2, ey - 2)
    even, first, last = place("px", nx)
    for c in range(3):
        for i in range(5):
            values = []
            for j in range(4):
                force = total_ref[c, i, j]
                if i == 0:
                    force = force + jnp.where(first, 0.0, jnp.where(even, b_ref[c, j], a_ref[c, j]))
                if i == 4:
                    force = force + jnp.where(last, 0.0, jnp.where(even, a_ref[c, j], b_ref[c, j]))
                speed = v_ref[c, i, j] - time_step * m_ref[i, j] * force
                position = u_ref[c, i, j] + time_step * speed
                u_out[c, i, j] = position
                v_out[c, i, j] = speed
                values.append(position)
            fill_points(us, c, i, values)
    forces(2 * ey, windows, keep, us, lame, level, old, new, grad_ref, div_ref,
           gx, gz, flux_x, flux_z, qy, qz, total_out)
    for c in range(3):
        for j in range(4):
            if final:
                at = slice(j * ey, (j + 1) * ey)
                send_a[c, at, :] = total_out[c, 4, j, 2 : 2 + ey, :]
                send_b[c, at, :] = send_a[c, at, :]
            else:
                back, ahead = total_out[c, 0, j], total_out[c, 4, j]
                send_a[c, j] = jnp.where(even, ahead, back)
                send_b[c, j] = jnp.where(even, back, ahead)


def end_kernel(sizes, u_ref, v_ref, m_ref, total_ref, a_ref, b_ref, u_out, v_out):
    nx, ey, lanes = sizes
    even, first, _ = place("px", nx)
    mine = slice(2, 2 + ey)
    for c in range(3):
        for i in range(4):
            for j in range(4):
                force = total_ref[c, i, j, mine, :]
                if i == 0:
                    at = slice(j * ey, (j + 1) * ey)
                    force = force + jnp.where(first, 0.0, jnp.where(even, b_ref[c, at, :], a_ref[c, at, :]))
                speed = v_ref[c, i, j, mine, :] - time_step * m_ref[i, j, mine, :] * force
                v_out[c, i, pl.ds(j, ey, stride=4), :] = speed
                u_out[c, i, pl.ds(j, ey, stride=4), :] = u_ref[c, i, j, mine, :] + time_step * speed


def call(kernel, name, outs, scratch, *args):
    shapes = [jax.ShapeDtypeStruct(s, F32) for s in outs]
    return pl.pallas_call(
        kernel,
        out_shape=shapes,
        scratch_shapes=[pltpu.VMEM(s, F32) for s in scratch],
        compiler_params=pltpu.CompilerParams(vmem_limit_bytes=32 * 1024 * 1024),
        name=name,
    )(*args)


def shards(sizes, displacement, velocity, inverse_mass, lame_first, lame_second, level_map):
    nx, ny = sizes
    _, ex4, ey4, lanes = displacement.shape
    ey = ey4 // 4
    tall, wide, short = 4 * ey, 3 * ey, 2 * ey
    move = functools.partial(swap, sizes)

    def rows_of(x, pad):
        x = x.reshape(-1, lanes).astype(F32)
        return jnp.pad(x, ((0, pad), (0, 0))) if pad else x

    pieces = [rows_of(displacement, 0), rows_of(velocity, 0), rows_of(inverse_mass, 0),
              rows_of(lame_first, 3), rows_of(lame_second, 3), rows_of(level_map, 7)]
    bounds = np.cumsum([0] + [p.shape[0] for p in pieces])
    own = jnp.concatenate(pieces, axis=0)
    from_e = move(False, False, own)
    from_o = move(False, True, own)
    here = lax.axis_index("py")
    even_y = here % 2 == 0

    def layer(x):
        return x[: bounds[1]].reshape(3, 4, ey4, lanes)[:, 0]

    layer_left = jnp.where(here == 0, 0.0, jnp.where(even_y, layer(from_o), layer(from_e)))
    layer_right = jnp.where(here == ny - 1, 0.0, jnp.where(even_y, layer(from_e), layer(from_o)))
    rim = jnp.concatenate([layer_left, displacement[:, 0], layer_right], axis=1)
    rim_a = move(True, False, rim)
    rim_b = move(True, True, rim)

    weights = jnp.asarray(weight_table(lanes // 4))
    gradient, divergence = (jnp.asarray(t) for t in depth_tables(lanes // 4))
    field = (3, 4, 4, tall, lanes)
    u, v, m, lame, level = call(
        functools.partial(prep_kernel, (ny, ey, lanes), tuple(int(b) for b in bounds[1:])), "prep",
        [field, field, field[1:], (2, 2, 25, tall, lanes), (2, tall, lanes)],
        [(3, int(bounds[6] - bounds[3]), lanes)],
        own, from_e, from_o, weights,
    )

    def scratch(rows, with_flux):
        points = (3, 25, rows, lanes)
        flux = [(3, 2, 25, rows, lanes)] if with_flux else []
        return [(3, 5, 5, rows, lanes), points, (3, 25, rows, 2 * lanes), points] + flux + [points, points]

    sizes_x = (nx, ey, lanes)
    count = wide - 2
    rim_u, old, total, send_a, send_b = call(
        functools.partial(start_kernel, sizes_x), "substep0",
        [(3, 4, tall, lanes), (6, 2, 25, tall, lanes), (3, 5, 4, tall, lanes), (4, 4 * count, lanes), (4, 4 * count, lanes)],
        scratch(tall, False),
        u, v, m, lame, level, rim_a, rim_b, gradient, divergence,
    )
    got_a, got_b = move(True, False, send_a), move(True, True, send_b)

    state = (3, 5, 4, short, lanes)
    message = (3, 4, short, lanes)
    u, v, m, total, send_a, send_b = call(
        functools.partial(second_kernel, sizes_x), "substep1",
        [state, state, state[1:], state, message, message],
        [(2, 4, 4, tall, lanes)] + scratch(tall, True) + [(3, 5, 4, tall, lanes)],
        u, rim_u, v, m, total, got_a, got_b, old, lame, level, gradient, divergence,
    )
    got_a, got_b = move(True, False, send_a), move(True, True, send_b)

    u, v, old, total, send_a, send_b = call(
        functools.partial(later_kernel, sizes_x, False), "substep2",
        [state, state, (6, 2, 25, short, lanes), state, message, message],
        scratch(short, False),
        u, v, m, total, got_a, got_b, old, lame, level, gradient, divergence,
    )
    got_a, got_b = move(True, False, send_a), move(True, True, send_b)

    u, v, total, send_a, send_b = call(
        functools.partial(later_kernel, sizes_x, True), "substep3",
        [state, state, state, (3, 4 * ey, lanes), (3, 4 * ey, lanes)],
        scratch(short, True),
        u, v, m, total, got_a, got_b, old, lame, level, gradient, divergence,
    )
    got_a, got_b = move(True, False, send_a), move(True, True, send_b)

    return tuple(call(
        functools.partial(end_kernel, sizes_x), "end",
        [displacement.shape, velocity.shape], [],
        u, v, m, total, got_a, got_b,
    ))


def solution(mesh):
    sizes = (mesh.shape["px"], mesh.shape["py"])
    in_specs = (
        P(None, "px", "py", None),
        P(None, "px", "py", None),
        P("px", "py", None),
        P(None, None, None, "px", "py"),
        P(None, None, None, "px", "py"),
        P("px", "py"),
    )
    out_specs = (P(None, "px", "py", None), P(None, "px", "py", None))
    return jax.shard_map(
        functools.partial(shards, sizes), mesh=mesh, in_specs=in_specs, out_specs=out_specs, check_vma=False
    )
```

profile of v0, /device:TPU:16, one launch (start us, length us, event | category | flops | bytes accessed | tf_op | source)
XLA Modules:
  0.0 52.1 jit_solution(11899576960355427439)
XLA Ops:
  0.7 0.7 %convert_element_type.8 = f32[1,128]{1,0:T(1,128)S(1)} convert(s32[1,128]{1,0:T(1,128)} %param.14) | non-fusion elementwise | flops 128 | bytes 1024 | tf_op jit(solution)/shard_map/convert_element_type | solution.py:428
  1.4 1.0 %reduce = f32[5,5,5,128]{3,2,1,0:T(8,128)S(1)} reduce(f32[5,5,5,1,128]{4,3,2,1,0:T(1,128)} %param.12, f32[]{:T(128)} %constant.44), dimensions={3}, to_apply=%param.12.reduce_sub_computation | reduce | bytes 128004 | tf_op args[3]
  2.4 1.0 %reduce.1 = f32[5,5,5,128]{3,2,1,0:T(8,128)S(1)} reduce(f32[5,5,5,1,128]{4,3,2,1,0:T(1,128)} %param.13, f32[]{:T(128)} %constant.44), dimensions={3}, to_apply=%param.13.reduce_sub_computation | reduce | bytes 128004 | tf_op args[4]
  3.4 0.9 %constant_dynamic-update-slice_fusion.3 = f32[712,128]{1,0:T(8,128)S(1)} fusion(f32[192,128]{1,0:T(8,128)} %bitcast.25), kind=kLoop, calls=%fused_computation.11 | loop fusion | bytes 196608
  4.3 0.9 %constant_dynamic-update-slice_fusion.2 = f32[712,128]{1,0:T(8,128)S(1)} fusion(f32[712,128]{1,0:T(8,128)S(1)} %constant_dynamic-update-slice_fusion.3, f32[192,128]{1,0:T(8,128)} %bitcast.28), kind=kLoop, calls=%fused_computation.10 | loop fusion | bytes 196608
  5.2 0.8 %constant_dynamic-update-slice_fusion.1 = f32[712,128]{1,0:T(8,128)S(1)} fusion(f32[712,128]{1,0:T(8,128)S(1)} %constant_dynamic-update-slice_fusion.2, f32[64,128]{1,0:T(8,128)} %bitcast.29), kind=kLoop, calls=%fused_computation.9 | loop fusion | bytes 65536
  6.0 1.6 %collective-permute-start.1 = (f32[712,128]{1,0:T(8,128)S(1)}, f32[712,128]{1,0:T(8,128)S(1)}, u32[]{:S(2)}, u32[]{:S(2)}) collective-permute-start(f32[712,128]{1,0:T(8,128)S(1)} %constant_dynamic-update-slice_fusion.own_ref), channel_id=1, source_target_pairs={{0,4},{1,2},{2,1},{3,7},{4,0},{5,6},{6,5},{7,3},{8,12},{9,10},{10,... | collective-permute-start | bytes 1093640 | tf_op jit(solution)/shard_map/ppermute | solution.py:107
  7.7 0.7 %slice_bitcast_fusion.2 = f32[3,16,128]{2,1,0:T(8,128)S(1)} fusion(f32[3,4,16,128]{3,2,1,0:T(8,128)} %param.9), kind=kLoop, calls=%fused_computation.6 | loop fusion | bytes 49152 | tf_op jit(solution)/shard_map/squeeze | solution.py:445
  8.4 5.1 %collective-permute-done.1.o_ref = f32[712,128]{1,0:T(8,128)S(1)} collective-permute-done((f32[712,128]{1,0:T(8,128)S(1)}, f32[712,128]{1,0:T(8,128)S(1)}, u32[]{:S(2)}, u32[]{:S(2)}) %collective-permute-start.1) | collective-permute-done | bytes 364576 | tf_op jit(solution)/shard_map/ppermute | solution.py:107
  13.6 1.4 %collective-permute-start.3 = (f32[3,48,128]{2,1,0:T(8,128)S(1)}, f32[3,48,128]{2,1,0:T(8,128)S(1)}, u32[]{:S(2)}, u32[]{:S(2)}) collective-permute-start(f32[3,48,128]{2,1,0:T(8,128)S(1)} %pad_maximum_fusion), channel_id=1, source_target_pairs={{0,1},{1,0},{2,3},{3,2},{4,8},{5,9},{6,10},{7,11},{8,4},{9,5},{10,... | collective-permute-start | bytes 221192 | tf_op jit(solution)/shard_map/ppermute | solution.py:107
  15.0 1.7 %collective-permute-start.2 = (f32[3,48,128]{2,1,0:T(8,128)S(1)}, f32[3,48,128]{2,1,0:T(8,128)S(1)}, u32[]{:S(2)}, u32[]{:S(2)}) collective-permute-start(f32[3,48,128]{2,1,0:T(8,128)S(1)} %pad_maximum_fusion), channel_id=1, source_target_pairs={{0,4},{1,5},{2,6},{3,7},{4,0},{5,1},{6,2},{7,3},{8,12},{9,13},{10,... | collective-permute-start | bytes 221192 | tf_op jit(solution)/shard_map/ppermute | solution.py:107
  16.7 0.7 %copy-done.2 = f32[50,128]{1,0:T(8,128)S(1)} copy-done((f32[50,128]{1,0:T(8,128)S(1)}, f32[50,128]{1,0:T(8,128)}, u32[]{:S(2)}) %copy-start.2) | copy-done | bytes 25624
  17.4 2.6 %prep.1 = (f32[3,4,4,16,128]{4,3,2,1,0:T(8,128)S(1)}, f32[3,4,4,16,128]{4,3,2,1,0:T(8,128)S(1)}, f32[4,4,16,128]{3,2,1,0:T(8,128)S(1)}, f32[2,2,25,16,128]{4,3,2,1,0:T(8,128)S(1)}, f32[2,16,128]{2,1,0:T(8,128)S(1)}) custom-call(f32[712,128]{1,0:T(8,128)S(1)} %constant_dynamic-update-slice_fusion.own_ref, f32[712,128]{1,0:T(8,128)S(1)} %collective-permute-done.e_ref, ...), custom_call_target="tpu_custom_call" | custom-call | tf_op jit(solution)/shard_map/prep/pallas_call | solution.py:411
  20.1 2.1 %substep0.1 = (f32[3,4,16,128]{3,2,1,0:T(8,128)S(1)}, f32[6,2,25,16,128]{4,3,2,1,0:T(8,128)S(1)}, f32[3,5,4,16,128]{4,3,2,1,0:T(8,128)S(1)}, f32[4,40,128]{2,1,0:T(8,128)S(1)}, f32[4,40,128]{2,1,0:T(8,128)S(1)}) custom-call(f32[3,4,4,16,128]{4,3,2,1,0:T(8,128)S(1)} %get-tuple-element.29.u_ref, f32[3,4,4,16,128]{4,3,2,1,0:T(8,128)S(1)} %get-tuple-element.30.v_ref, ...), custom_call_target="tpu_custom_call" | custom-call | tf_op jit(solution)/shard_map/substep0/pallas_call | solution.py:411
  22.2 1.4 %collective-permute-start.4 = (f32[4,40,128]{2,1,0:T(8,128)S(1)}, f32[4,40,128]{2,1,0:T(8,128)S(1)}, u32[]{:S(2)}, u32[]{:S(2)}) collective-permute-start(f32[4,40,128]{2,1,0:T(8,128)S(1)} %get-tuple-element.36), channel_id=1, source_target_pairs={{0,4},{1,5},{2,6},{3,7},{4,0},{5,1},{6,2},{7,3},{8,12},{9,13},{10,... | collective-permute-start | bytes 245768 | tf_op jit(solution)/shard_map/ppermute | solution.py:107
  24.2 3.4 %collective-permute-done.4.a_ref = f32[4,40,128]{2,1,0:T(8,128)S(1)} collective-permute-done((f32[4,40,128]{2,1,0:T(8,128)S(1)}, f32[4,40,128]{2,1,0:T(8,128)S(1)}, u32[]{:S(2)}, u32[]{:S(2)}) %collective-permute-start.4) | collective-permute-done | bytes 81952 | tf_op jit(solution)/shard_map/ppermute | solution.py:107
  27.6 1.4 %collective-permute-done.5.b_ref = f32[4,40,128]{2,1,0:T(8,128)S(1)} collective-permute-done((f32[4,40,128]{2,1,0:T(8,128)S(1)}, f32[4,40,128]{2,1,0:T(8,128)S(1)}, u32[]{:S(2)}, u32[]{:S(2)}) %collective-permute-start.5) | collective-permute-done | bytes 81952 | tf_op jit(solution)/shard_map/ppermute | solution.py:107
  28.9 2.3 %substep1.1 = (f32[3,5,4,8,128]{4,3,2,1,0:T(8,128)S(1)}, f32[3,5,4,8,128]{4,3,2,1,0:T(8,128)S(1)}, f32[5,4,8,128]{3,2,1,0:T(8,128)S(1)}, f32[3,5,4,8,128]{4,3,2,...) custom-call(f32[3,4,4,16,128]{4,3,2,1,0:T(8,128)S(1)} %get-tuple-element.29.u_ref, ...), custom_call_target="tpu_custom_call" | custom-call | tf_op jit(solution)/shard_map/substep1/pallas_call | solution.py:411
  31.2 0.8 %collective-permute-start.6 = (f32[3,4,8,128]{3,2,1,0:T(8,128)S(1)}, f32[3,4,8,128]{3,2,1,0:T(8,128)S(1)}, u32[]{:S(2)}, u32[]{:S(2)}) collective-permute-start(f32[3,4,8,128]{3,2,1,0:T(8,128)S(1)} %get-tuple-element.43), channel_id=1, source_target_pairs={{0,4},{1,5},{2,6},{3,7},{4,0},{5,1},{6,2},{7,3},{8,12},{9,13},{10,... | collective-permute-start | bytes 147464 | tf_op jit(solution)/shard_map/ppermute | solution.py:107
  32.0 1.2 %collective-permute-start.7 = (f32[3,4,8,128]{3,2,1,0:T(8,128)S(1)}, f32[3,4,8,128]{3,2,1,0:T(8,128)S(1)}, u32[]{:S(2)}, u32[]{:S(2)}) collective-permute-start(f32[3,4,8,128]{3,2,1,0:T(8,128)S(1)} %get-tuple-element.44), channel_id=1, source_target_pairs={{0,1},{1,0},{2,3},{3,2},{4,8},{5,9},{6,10},{7,11},{8,4},{9,5},{10,... | collective-permute-start | bytes 147464 | tf_op jit(solution)/shard_map/ppermute | solution.py:107
  33.2 2.2 %collective-permute-done.6.a_ref = f32[3,4,8,128]{3,2,1,0:T(8,128)S(1)} collective-permute-done((f32[3,4,8,128]{3,2,1,0:T(8,128)S(1)}, f32[3,4,8,128]{3,2,1,0:T(8,128)S(1)}, u32[]{:S(2)}, u32[]{:S(2)}) %collective-permute-start.6) | collective-permute-done | bytes 49184 | tf_op jit(solution)/shard_map/ppermute | solution.py:107
  35.4 1.6 %collective-permute-done.7.b_ref = f32[3,4,8,128]{3,2,1,0:T(8,128)S(1)} collective-permute-done((f32[3,4,8,128]{3,2,1,0:T(8,128)S(1)}, f32[3,4,8,128]{3,2,1,0:T(8,128)S(1)}, u32[]{:S(2)}, u32[]{:S(2)}) %collective-permute-start.7) | collective-permute-done | bytes 49184 | tf_op jit(solution)/shard_map/ppermute | solution.py:107
  37.0 1.2 %substep2.1 = (f32[3,5,4,8,128]{4,3,2,1,0:T(8,128)S(1)}, f32[3,5,4,8,128]{4,3,2,1,0:T(8,128)S(1)}, f32[6,2,25,8,128]{4,3,2,1,0:T(8,128)S(1)}, f32[3,5,4,8,128]{4...) custom-call(f32[3,5,4,8,128]{4,3,2,1,0:T(8,128)S(1)} %get-tuple-element.39.u_ref, ...), custom_call_target="tpu_custom_call" | custom-call | tf_op jit(solution)/shard_map/substep2/pallas_call | solution.py:411
  38.2 1.4 %collective-permute-start.8 = (f32[3,4,8,128]{3,2,1,0:T(8,128)S(1)}, f32[3,4,8,128]{3,2,1,0:T(8,128)S(1)}, u32[]{:S(2)}, u32[]{:S(2)}) collective-permute-start(f32[3,4,8,128]{3,2,1,0:T(8,128)S(1)} %get-tuple-element.48), channel_id=1, source_target_pairs={{0,4},{1,5},{2,6},{3,7},{4,0},{5,1},{6,2},{7,3},{8,12},{9,13},{10,... | collective-permute-start | bytes 147464 | tf_op jit(solution)/shard_map/ppermute | solution.py:107
  40.2 2.2 %collective-permute-done.8.a_ref = f32[3,4,8,128]{3,2,1,0:T(8,128)S(1)} collective-permute-done((f32[3,4,8,128]{3,2,1,0:T(8,128)S(1)}, f32[3,4,8,128]{3,2,1,0:T(8,128)S(1)}, u32[]{:S(2)}, u32[]{:S(2)}) %collective-permute-start.8) | collective-permute-done | bytes 49184 | tf_op jit(solution)/shard_map/ppermute | solution.py:107
  42.4 2.2 %collective-permute-done.9.b_ref = f32[3,4,8,128]{3,2,1,0:T(8,128)S(1)} collective-permute-done((f32[3,4,8,128]{3,2,1,0:T(8,128)S(1)}, f32[3,4,8,128]{3,2,1,0:T(8,128)S(1)}, u32[]{:S(2)}, u32[]{:S(2)}) %collective-permute-start.9) | collective-permute-done | bytes 49184 | tf_op jit(solution)/shard_map/ppermute | solution.py:107
  44.6 1.3 %substep3.1 = (f32[3,5,4,8,128]{4,3,2,1,0:T(8,128)S(1)}, f32[3,5,4,8,128]{4,3,2,1,0:T(8,128)S(1)}, f32[3,5,4,8,128]{4,3,2,1,0:T(8,128)S(1)}, f32[3,16,128]{2,1,0:T(8,128)S(1)}, f32[3,16,128]{2,1,0:T(8,128)S(1)}) custom-call(f32[3,5,4,8,128]{4,3,2,1,0:T(8,128)S(1)} %get-tuple-element.45.u_ref, f32[3,5,4,8,128]{4,3,2,1,0:T(8,128)S(1)} %get-tuple-element.46.v_ref, ...), custom_call_target="tpu_custom_call" | custom-call | tf_op jit(solution)/shard_map/substep3/pallas_call | solution.py:411
  45.8 0.8 %collective-permute-start.10 = (f32[3,16,128]{2,1,0:T(8,128)S(1)}, f32[3,16,128]{2,1,0:T(8,128)S(1)}, u32[]{:S(2)}, u32[]{:S(2)}) collective-permute-start(f32[3,16,128]{2,1,0:T(8,128)S(1)} %get-tuple-element.54), channel_id=1, source_target_pairs={{0,4},{1,5},{2,6},{3,7},{4,0},{5,1},{6,2},{7,3},{8,12},{9,13},{10,... | collective-permute-start | bytes 73736 | tf_op jit(solution)/shard_map/ppermute | solution.py:107
  46.6 1.2 %collective-permute-start.11 = (f32[3,16,128]{2,1,0:T(8,128)S(1)}, f32[3,16,128]{2,1,0:T(8,128)S(1)}, u32[]{:S(2)}, u32[]{:S(2)}) collective-permute-start(f32[3,16,128]{2,1,0:T(8,128)S(1)} %get-tuple-element.55), channel_id=1, source_target_pairs={{0,1},{1,0},{2,3},{3,2},{4,8},{5,9},{6,10},{7,11},{8,4},{9,5},{10,... | collective-permute-start | bytes 73736 | tf_op jit(solution)/shard_map/ppermute | solution.py:107
  47.8 1.9 %collective-permute-done.10.a_ref = f32[3,16,128]{2,1,0:T(8,128)S(1)} collective-permute-done((f32[3,16,128]{2,1,0:T(8,128)S(1)}, f32[3,16,128]{2,1,0:T(8,128)S(1)}, u32[]{:S(2)}, u32[]{:S(2)}) %collective-permute-start.10) | collective-permute-done | bytes 24608 | tf_op jit(solution)/shard_map/ppermute | solution.py:107
  49.7 1.6 %collective-permute-done.11.b_ref = f32[3,16,128]{2,1,0:T(8,128)S(1)} collective-permute-done((f32[3,16,128]{2,1,0:T(8,128)S(1)}, f32[3,16,128]{2,1,0:T(8,128)S(1)}, u32[]{:S(2)}, u32[]{:S(2)}) %collective-permute-start.11) | collective-permute-done | bytes 24608 | tf_op jit(solution)/shard_map/ppermute | solution.py:107
  51.3 0.8 %end.1 = (f32[3,4,16,128]{3,2,1,0:T(8,128)}, f32[3,4,16,128]{3,2,1,0:T(8,128)}) custom-call(f32[3,5,4,8,128]{4,3,2,1,0:T(8,128)S(1)} %get-tuple-element.51.u_ref, f32[3,5,4,8,128]{4,3,2,1,0:T(8,128)S(1)} %get-tuple-element.52.v_ref, f32[5,4,8,128]{3,2,1,0:T(8,128)S(1)} %get-tuple-element.41.m_ref, f32[3,5,4,8,128]{4,3,2,1,0:T(8,128)S(1)} %get-tuple-element.53.total_ref, ...), custom_call_target="tpu_custom_call" | custom-call | tf_op jit(solution)/shard_map/end/pallas_call | solution.py:411
  (20 shorter events, 1.4 us)
Async XLA Ops:
  0.6 19.4 %copy-start = (bf16[768,128]{1,0:T(8,128)(2,1)S(1)}, bf16[768,128]{1,0:T(8,128)(2,1)}, u32[]{:S(2)}) copy-start(bf16[768,128]{1,0:T(8,128)(2,1)} %constant.31.clone.div_ref) | copy-start | bytes 589828
  0.6 19.4 %copy-start.1 = (bf16[384,256]{1,0:T(8,128)(2,1)S(1)}, bf16[384,256]{1,0:T(8,128)(2,1)}, u32[]{:S(2)}) copy-start(bf16[384,256]{1,0:T(8,128)(2,1)} %constant.30.clone.grad_ref) | copy-start | bytes 589828
  6.0 7.5 %collective-permute-start.1 = (f32[712,128]{1,0:T(8,128)S(1)}, f32[712,128]{1,0:T(8,128)S(1)}, u32[]{:S(2)}, u32[]{:S(2)}) collective-permute-start(f32[712,128]{1,0:T(8,128)S(1)} %constant_dynamic-update-slice_fusion.own_ref), channel_id=1, source_target_pairs={{0,4},{1,2},{2,1},{3,7},{4,0},{5,6},{6,5},{7,3},{8,12},{9,10},{10,... | collective-permute-start | bytes 1093640 | tf_op jit(solution)/shard_map/ppermute | solution.py:107
  7.5 6.0 %collective-permute-start = (f32[712,128]{1,0:T(8,128)S(1)}, f32[712,128]{1,0:T(8,128)S(1)}, u32[]{:S(2)}, u32[]{:S(2)}) collective-permute-start(f32[712,128]{1,0:T(8,128)S(1)} %constant_dynamic-update-slice_fusion.own_ref), channel_id=1, source_target_pairs={{0,1},{1,0},{2,3},{3,2},{4,5},{5,4},{6,7},{7,6},{8,9},{9,8},{10,11... | collective-permute-start | bytes 1093640 | tf_op jit(solution)/shard_map/ppermute | solution.py:107
  13.6 6.5 %collective-permute-start.3 = (f32[3,48,128]{2,1,0:T(8,128)S(1)}, f32[3,48,128]{2,1,0:T(8,128)S(1)}, u32[]{:S(2)}, u32[]{:S(2)}) collective-permute-start(f32[3,48,128]{2,1,0:T(8,128)S(1)} %pad_maximum_fusion), channel_id=1, source_target_pairs={{0,1},{1,0},{2,3},{3,2},{4,8},{5,9},{6,10},{7,11},{8,4},{9,5},{10,... | collective-permute-start | bytes 221192 | tf_op jit(solution)/shard_map/ppermute | solution.py:107
  15.0 5.0 %collective-permute-start.2 = (f32[3,48,128]{2,1,0:T(8,128)S(1)}, f32[3,48,128]{2,1,0:T(8,128)S(1)}, u32[]{:S(2)}, u32[]{:S(2)}) collective-permute-start(f32[3,48,128]{2,1,0:T(8,128)S(1)} %pad_maximum_fusion), channel_id=1, source_target_pairs={{0,4},{1,5},{2,6},{3,7},{4,0},{5,1},{6,2},{7,3},{8,12},{9,13},{10,... | collective-permute-start | bytes 221192 | tf_op jit(solution)/shard_map/ppermute | solution.py:107
  16.7 0.7 %copy-start.2 = (f32[50,128]{1,0:T(8,128)S(1)}, f32[50,128]{1,0:T(8,128)}, u32[]{:S(2)}) copy-start(f32[50,128]{1,0:T(8,128)} %constant.29.clone.weight_ref) | copy-start | bytes 76804
  22.2 5.4 %collective-permute-start.4 = (f32[4,40,128]{2,1,0:T(8,128)S(1)}, f32[4,40,128]{2,1,0:T(8,128)S(1)}, u32[]{:S(2)}, u32[]{:S(2)}) collective-permute-start(f32[4,40,128]{2,1,0:T(8,128)S(1)} %get-tuple-element.36), channel_id=1, source_target_pairs={{0,4},{1,5},{2,6},{3,7},{4,0},{5,1},{6,2},{7,3},{8,12},{9,13},{10,... | collective-permute-start | bytes 245768 | tf_op jit(solution)/shard_map/ppermute | solution.py:107
  23.6 5.3 %collective-permute-start.5 = (f32[4,40,128]{2,1,0:T(8,128)S(1)}, f32[4,40,128]{2,1,0:T(8,128)S(1)}, u32[]{:S(2)}, u32[]{:S(2)}) collective-permute-start(f32[4,40,128]{2,1,0:T(8,128)S(1)} %get-tuple-element.37), channel_id=1, source_target_pairs={{0,1},{1,0},{2,3},{3,2},{4,8},{5,9},{6,10},{7,11},{8,4},{9,5},{10,... | collective-permute-start | bytes 245768 | tf_op jit(solution)/shard_map/ppermute | solution.py:107
  31.2 4.2 %collective-permute-start.6 = (f32[3,4,8,128]{3,2,1,0:T(8,128)S(1)}, f32[3,4,8,128]{3,2,1,0:T(8,128)S(1)}, u32[]{:S(2)}, u32[]{:S(2)}) collective-permute-start(f32[3,4,8,128]{3,2,1,0:T(8,128)S(1)} %get-tuple-element.43), channel_id=1, source_target_pairs={{0,4},{1,5},{2,6},{3,7},{4,0},{5,1},{6,2},{7,3},{8,12},{9,13},{10,... | collective-permute-start | bytes 147464 | tf_op jit(solution)/shard_map/ppermute | solution.py:107
  32.0 5.0 %collective-permute-start.7 = (f32[3,4,8,128]{3,2,1,0:T(8,128)S(1)}, f32[3,4,8,128]{3,2,1,0:T(8,128)S(1)}, u32[]{:S(2)}, u32[]{:S(2)}) collective-permute-start(f32[3,4,8,128]{3,2,1,0:T(8,128)S(1)} %get-tuple-element.44), channel_id=1, source_target_pairs={{0,1},{1,0},{2,3},{3,2},{4,8},{5,9},{6,10},{7,11},{8,4},{9,5},{10,... | collective-permute-start | bytes 147464 | tf_op jit(solution)/shard_map/ppermute | solution.py:107
  38.2 4.2 %collective-permute-start.8 = (f32[3,4,8,128]{3,2,1,0:T(8,128)S(1)}, f32[3,4,8,128]{3,2,1,0:T(8,128)S(1)}, u32[]{:S(2)}, u32[]{:S(2)}) collective-permute-start(f32[3,4,8,128]{3,2,1,0:T(8,128)S(1)} %get-tuple-element.48), channel_id=1, source_target_pairs={{0,4},{1,5},{2,6},{3,7},{4,0},{5,1},{6,2},{7,3},{8,12},{9,13},{10,... | collective-permute-start | bytes 147464 | tf_op jit(solution)/shard_map/ppermute | solution.py:107
  39.6 5.0 %collective-permute-start.9 = (f32[3,4,8,128]{3,2,1,0:T(8,128)S(1)}, f32[3,4,8,128]{3,2,1,0:T(8,128)S(1)}, u32[]{:S(2)}, u32[]{:S(2)}) collective-permute-start(f32[3,4,8,128]{3,2,1,0:T(8,128)S(1)} %get-tuple-element.49), channel_id=1, source_target_pairs={{0,1},{1,0},{2,3},{3,2},{4,8},{5,9},{6,10},{7,11},{8,4},{9,5},{10,... | collective-permute-start | bytes 147464 | tf_op jit(solution)/shard_map/ppermute | solution.py:107
  45.8 3.9 %collective-permute-start.10 = (f32[3,16,128]{2,1,0:T(8,128)S(1)}, f32[3,16,128]{2,1,0:T(8,128)S(1)}, u32[]{:S(2)}, u32[]{:S(2)}) collective-permute-start(f32[3,16,128]{2,1,0:T(8,128)S(1)} %get-tuple-element.54), channel_id=1, source_target_pairs={{0,4},{1,5},{2,6},{3,7},{4,0},{5,1},{6,2},{7,3},{8,12},{9,13},{10,... | collective-permute-start | bytes 73736 | tf_op jit(solution)/shard_map/ppermute | solution.py:107
  46.6 4.7 %collective-permute-start.11 = (f32[3,16,128]{2,1,0:T(8,128)S(1)}, f32[3,16,128]{2,1,0:T(8,128)S(1)}, u32[]{:S(2)}, u32[]{:S(2)}) collective-permute-start(f32[3,16,128]{2,1,0:T(8,128)S(1)} %get-tuple-element.55), channel_id=1, source_target_pairs={{0,1},{1,0},{2,3},{3,2},{4,8},{5,9},{6,10},{7,11},{8,4},{9,5},{10,... | collective-permute-start | bytes 73736 | tf_op jit(solution)/shard_map/ppermute | solution.py:107
where the time goes:
time: 52.6 us; the launch traced here: 52.1 us
  waiting for transfers between devices  21.5 us (41%)
  starting transfers between devices  12.7 us (24%)
  Pallas kernels  10.2 us (19%)
  local copies, waits for them, and re-layouts  4.12 us (8%)
  other arithmetic  2.71 us (5%)
  between operations  0.78 us (1%)
    ppermute x12, waiting for transfers between devices, swap(): return lax.ppermute(x, ('px', 'py'), swap_pairs(*mesh_sizes, along_x, odd))  21.5 us
    ppermute x12, starting transfers between devices, swap(): return lax.ppermute(x, ('px', 'py'), swap_pairs(*mesh_sizes, along_x, odd))  12.7 us
    pallas_call x6, Pallas kernels, call(): pl.pallas_call(kernel, out_shape=shapes, scratch_shapes=[pltpu.VMEM(s, F3...  10.2 us
    unnamed x11, local copies, waits for them, and re-layouts  3.34 us
    unnamed x2, other arithmetic  1.98 us
  transfers between devices with their start and end apart: 12, of which 9 were waited for; matrix products, arithmetic and copies ran while one was open for 1% of the time, Pallas kernels for 5%

commit v1 on v0

--- a/solution.py
+++ b/solution.py
@@ -112,37 +112,58 @@
     return lax.rem(here, 2) == 0, here == 0, here == size - 1
 
 
-def prep_kernel(sizes, rows, own_ref, e_ref, o_ref, weight_ref, u_ref, v_ref, m_ref, lame_ref, level_ref, sel):
+def load_kernel(bounds, *refs):
+    u_hbm, v_hbm, m_hbm, first_hbm, second_hbm, level_hbm, *tables_hbm = refs[: 6 + 3]
+    u_out, out, *tables = refs[9 : 9 + 2 + 3]
+    first, second, level, sems = refs[14:]
+    copies = [
+        (first_hbm, first), (second_hbm, second), (level_hbm, level), (u_hbm, u_out),
+        (v_hbm, out.at[0 : bounds[0]]), (m_hbm, out.at[bounds[0] : bounds[1]]), *zip(tables_hbm, tables),
+    ]
+    copies = [pltpu.make_async_copy(a, b, sems.at[n]) for n, (a, b) in enumerate(copies)]
+    for copy in copies:
+        copy.start()
+    for p, table in enumerate((first, second)):
+        copies[p].wait()
+        for row in range(125):
+            i, j, k = row // 25, row // 5 % 5, row % 5
+            out[bounds[1 + p] + row : bounds[1 + p] + row + 1, :] = table[i, j, k]
+    copies[2].wait()
+    out[bounds[3] : bounds[3] + 1, :] = level[...].astype(F32)
+    for copy in copies[3:]:
+        copy.wait()
+
+
+def prep_kernel(sizes, bounds, own_u, e_u, o_u, own_ref, e_ref, o_ref, weight_ref, u_ref, v_ref, m_ref, lame_ref, level_ref, sel):
     ny, ey, lanes = sizes
     even, first, last = place("py", ny)
-    base_v, base_m, base_first, base_second, base_level, total = rows
     tall = 4 * ey
-
-    def left(at):
-        return jnp.where(first, 0.0, jnp.where(even, o_ref[at], e_ref[at]))
-
-    def right(at):
-        return jnp.where(last, 0.0, jnp.where(even, e_ref[at], o_ref[at]))
-
-    def spread(base, out):
+    base_first, base_second, base_level = bounds[1:4]
+
+    def left(e, o, at):
+        return jnp.where(first, 0.0, jnp.where(even, o[at], e[at]))
+
+    def right(e, o, at):
+        return jnp.where(last, 0.0, jnp.where(even, e[at], o[at]))
+
+    def spread(own, e, o, base, out):
         for j in range(4):
-            at = pl.ds(base + j, ey, stride=4)
-            out[j, 0:ey, :] = left((at, slice(None)))
-            out[j, ey : 2 * ey, :] = own_ref[at, :]
-            out[j, 2 * ey : 3 * ey, :] = right((at, slice(None)))
+            at = (pl.ds(base + j, ey, stride=4), slice(None))
+            out[j, 0:ey, :] = left(e, o, at)
+            out[j, ey : 2 * ey, :] = own[at]
+            out[j, 2 * ey : 3 * ey, :] = right(e, o, at)
             out[j, 3 * ey :, :] = jnp.zeros((ey, lanes), F32)
 
-    for c in range(3):
-        for i in range(4):
-            spread((c * 4 + i) * tall, u_ref.at[c, i])
-            spread(base_v + (c * 4 + i) * tall, v_ref.at[c, i])
     for i in range(4):
-        spread(base_m + i * tall, m_ref.at[i])
-
-    tail = slice(base_first, total)
-    sel[0] = left((tail, slice(None)))
-    sel[1] = own_ref[tail, :]
-    sel[2] = right((tail, slice(None)))
+        for c in range(3):
+            spread(own_u, e_u, o_u, (c * 4 + i) * tall, u_ref.at[c, i])
+            spread(own_ref, e_ref, o_ref, (c * 4 + i) * tall, v_ref.at[c, i])
+        spread(own_ref, e_ref, o_ref, bounds[0] + i * tall, m_ref.at[i])
+
+    tail = (slice(base_first, own_ref.shape[0]), slice(None))
+    sel[0] = left(e_ref, o_ref, tail)
+    sel[1] = own_ref[tail]
+    sel[2] = right(e_ref, o_ref, tail)
 
     shape = (2 * ey, lanes)
     sub = lax.broadcasted_iota(jnp.int32, shape, 0)
@@ -407,7 +428,7 @@
 
 
 def call(kernel, name, outs, scratch, *args):
-    shapes = [jax.ShapeDtypeStruct(s, F32) for s in outs]
+    shapes = [jax.ShapeDtypeStruct(s, F32) if name == "end" else pltpu.VMEM(s, F32) for s in outs]
     return pl.pallas_call(
         kernel,
         out_shape=shapes,
@@ -424,36 +445,45 @@
     tall, wide, short = 4 * ey, 3 * ey, 2 * ey
     move = functools.partial(swap, sizes)
 
-    def rows_of(x, pad):
-        x = x.reshape(-1, lanes).astype(F32)
-        return jnp.pad(x, ((0, pad), (0, 0))) if pad else x
-
-    pieces = [rows_of(displacement, 0), rows_of(velocity, 0), rows_of(inverse_mass, 0),
-              rows_of(lame_first, 3), rows_of(lame_second, 3), rows_of(level_map, 7)]
-    bounds = np.cumsum([0] + [p.shape[0] for p in pieces])
-    own = jnp.concatenate(pieces, axis=0)
-    from_e = move(False, False, own)
-    from_o = move(False, True, own)
+    flat_u = displacement.reshape(-1, lanes)
+    u_e, u_o = move(False, False, flat_u), move(False, True, flat_u)
+    flat_v, flat_m = velocity.reshape(-1, lanes), inverse_mass.reshape(-1, lanes)
+    bounds = [int(b) for b in np.cumsum([flat_v.shape[0], flat_m.shape[0], 128, 128, 8])]
+    gradient, divergence = depth_tables(lanes // 4)
+    tables = [jnp.asarray(t) for t in (gradient, divergence, weight_table(lanes // 4))]
+    anywhere = pl.BlockSpec(memory_space=pl.ANY)
+    own_u, own, gradient, divergence, weights = pl.pallas_call(
+        functools.partial(load_kernel, bounds),
+        out_shape=[pltpu.VMEM(flat_u.shape, F32), pltpu.VMEM((bounds[4], lanes), F32)]
+        + [pltpu.VMEM(t.shape, t.dtype) for t in tables],
+        in_specs=[anywhere] * 9,
+        scratch_shapes=[
+            pltpu.VMEM(lame_first.shape, F32),
+            pltpu.VMEM(lame_second.shape, F32),
+            pltpu.VMEM(level_map.shape, jnp.int32),
+            pltpu.SemaphoreType.DMA((9,)),
+        ],
+        name="load",
+    )(flat_u, flat_v, flat_m, lame_first, lame_second, level_map, *tables)
+    from_e, from_o = move(False, False, own), move(False, True, own)
     here = lax.axis_index("py")
     even_y = here % 2 == 0
 
     def layer(x):
-        return x[: bounds[1]].reshape(3, 4, ey4, lanes)[:, 0]
-
-    layer_left = jnp.where(here == 0, 0.0, jnp.where(even_y, layer(from_o), layer(from_e)))
-    layer_right = jnp.where(here == ny - 1, 0.0, jnp.where(even_y, layer(from_e), layer(from_o)))
-    rim = jnp.concatenate([layer_left, displacement[:, 0], layer_right], axis=1)
+        return x.reshape(3, 4, ey4, lanes)[:, 0]
+
+    layer_left = jnp.where(here == 0, 0.0, jnp.where(even_y, layer(u_o), layer(u_e)))
+    layer_right = jnp.where(here == ny - 1, 0.0, jnp.where(even_y, layer(u_e), layer(u_o)))
+    rim = jnp.concatenate([layer_left, layer(own_u), layer_right], axis=1)
     rim_a = move(True, False, rim)
     rim_b = move(True, True, rim)
 
-    weights = jnp.asarray(weight_table(lanes // 4))
-    gradient, divergence = (jnp.asarray(t) for t in depth_tables(lanes // 4))
     field = (3, 4, 4, tall, lanes)
     u, v, m, lame, level = call(
-        functools.partial(prep_kernel, (ny, ey, lanes), tuple(int(b) for b in bounds[1:])), "prep",
+        functools.partial(prep_kernel, (ny, ey, lanes), bounds), "prep",
         [field, field, field[1:], (2, 2, 25, tall, lanes), (2, tall, lanes)],
-        [(3, int(bounds[6] - bounds[3]), lanes)],
-        own, from_e, from_o, weights,
+        [(3, bounds[4] - bounds[1], lanes)],
+        own_u, u_e, u_o, own, from_e, from_o, weights,
     )
 
     def scratch(rows, with_flux):

time: 52.6 us -> 47.4 us (0.901)
  local copies, waits for them, and re-layouts: 4.12 us -> 0.01 us
  other arithmetic: 2.71 us -> 0.02 us
  starting transfers between devices: 12.7 us -> 14.3 us
  Pallas kernels: 10.2 us -> 11.6 us
  waiting for transfers between devices: 21.5 us -> 20.6 us
    unnamed x11 -> x0, local copies, waits for them, and re-layouts: 3.34 us -> none
    unnamed x2 -> x0, other arithmetic: 1.98 us -> none
    ppermute x12 -> x14, starting transfers between devices: 12.7 us -> 14.3 us  [swap(): return lax.ppermute(x, ('px', 'py'), swap_pairs(*mesh_sizes, along_x, odd))]
    pallas_call x0 -> x1, Pallas kernels: none -> 1.3 us  [shards(): pl.pallas_call(functools.partial(load_kernel, bounds), out_shape=[pltpu.V...]
    ppermute x12 -> x14, waiting for transfers between devices: 21.5 us -> 20.6 us  [swap(): return lax.ppermute(x, ('px', 'py'), swap_pairs(*mesh_sizes, along_x, odd))]
    squeeze x1, local copies, waits for them, and re-layouts: 0.74 us -> 0.01 us  [layer(): return x.reshape(3, 4, ey4, lanes)[:, 0]]
    convert_element_type x1 -> x0, other arithmetic: 0.71 us -> none  [rows_of(): x = x.reshape(-1, lanes).astype(F32)]
  transfers between devices with their start and end apart: 12 -> 14, of which waited for: 9 -> 10; matrix products, arithmetic and copies ran while one was open for 1% -> 0% of each run, Pallas kernels for 5% -> 8%
where the time goes in v1:
time: 47.4 us; the launch traced here: 47.1 us
  waiting for transfers between devices  20.6 us (43%)
  starting transfers between devices  14.3 us (30%)
  Pallas kernels  11.6 us (24%)
  between operations  0.69 us (1%)
    ppermute x14, waiting for transfers between devices, swap(): return lax.ppermute(x, ('px', 'py'), swap_pairs(*mesh_sizes, along_x, odd))  20.6 us
    ppermute x14, starting transfers between devices, swap(): return lax.ppermute(x, ('px', 'py'), swap_pairs(*mesh_sizes, along_x, odd))  14.3 us
    pallas_call x6, Pallas kernels, call(): pl.pallas_call(kernel, out_shape=shapes, scratch_shapes=[pltpu.VMEM(s, F3...  10.3 us
    pallas_call x1, Pallas kernels, shards(): pl.pallas_call(functools.partial(load_kernel, bounds), out_shape=[pltpu.V...  1.3 us
  transfers between devices with their start and end apart: 14, of which 10 were waited for; matrix products, arithmetic and copies ran while one was open for 0% of the time, Pallas kernels for 8%

profile of v1, /device:TPU:16, one launch (start us, length us, event | category | flops | bytes accessed | tf_op | source)
XLA Modules:
  0.0 47.1 jit_solution(9684053860313281472)
XLA Ops:
  0.6 1.6 %collective-permute-start.1 = (f32[192,128]{1,0:T(8,128)}, f32[192,128]{1,0:T(8,128)S(1)}, u32[]{:S(2)}, u32[]{:S(2)}) collective-permute-start(f32[192,128]{1,0:T(8,128)} %bitcast.30), channel_id=1, source_target_pairs={{0,4},{1,2},{2,1},{3,7},{4,0},{5,6},{6,5},{7,3},{8,12},{9,10},{10,... | collective-permute-start | bytes 294920 | tf_op jit(solution)/shard_map/ppermute | solution.py:107
  2.2 0.1 collective-permute-start
  2.3 1.3 %load.1 = (f32[192,128]{1,0:T(8,128)S(1)}, f32[520,128]{1,0:T(8,128)S(1)}, bf16[384,256]{1,0:T(8,128)(2,1)S(1)}, bf16[768,128]{1,0:T(8,128)(2,1)S(1)}, f32[50,128]{1,0:T(8,128)S(1)}) custom-call(f32[192,128]{1,0:T(8,128)} %bitcast.32, f32[192,128]{1,0:T(8,128)} %bitcast.29, f32[64,128]{1,0:T(8,128)} %bitcast.33, f32[5,5,5,1,128]{4,3,2,1,0:T(1,128)} %refs_3_.1, ...), custom_call_target="tpu_custom_call" | custom-call | tf_op jit(solution)/shard_map/load/pallas_call | solution.py:455
  3.6 1.6 %collective-permute-start.3 = (f32[520,128]{1,0:T(8,128)S(1)}, f32[520,128]{1,0:T(8,128)S(1)}, u32[]{:S(2)}, u32[]{:S(2)}) collective-permute-start(f32[520,128]{1,0:T(8,128)S(1)} %get-tuple-element.35.own_ref), channel_id=1, source_target_pairs={{0,4},{1,2},{2,1},{3,7},{4,0},{5,6},{6,5},{7,3},{8,12},{9,10},{10,... | collective-permute-start | bytes 798728 | tf_op jit(solution)/shard_map/ppermute | solution.py:107
  5.2 0.0 collective-permute-start.2
  5.2 0.3 collective-permute-done.1.o_u
  5.6 1.4 %collective-permute-start.5 = (f32[3,48,128]{2,1,0:T(8,128)S(1)}, f32[3,48,128]{2,1,0:T(8,128)S(1)}, u32[]{:S(2)}, u32[]{:S(2)}) collective-permute-start(f32[3,48,128]{2,1,0:T(8,128)S(1)} %pad_maximum_fusion), channel_id=1, source_target_pairs={{0,1},{1,0},{2,3},{3,2},{4,8},{5,9},{6,10},{7,11},{8,4},{9,5},{10,... | collective-permute-start | bytes 221192 | tf_op jit(solution)/shard_map/ppermute | solution.py:107
  7.0 1.7 %collective-permute-start.4 = (f32[3,48,128]{2,1,0:T(8,128)S(1)}, f32[3,48,128]{2,1,0:T(8,128)S(1)}, u32[]{:S(2)}, u32[]{:S(2)}) collective-permute-start(f32[3,48,128]{2,1,0:T(8,128)S(1)} %pad_maximum_fusion), channel_id=1, source_target_pairs={{0,4},{1,5},{2,6},{3,7},{4,0},{5,1},{6,2},{7,3},{8,12},{9,13},{10,... | collective-permute-start | bytes 221192 | tf_op jit(solution)/shard_map/ppermute | solution.py:107
  8.7 3.7 %collective-permute-done.3.o_ref = f32[520,128]{1,0:T(8,128)S(1)} collective-permute-done((f32[520,128]{1,0:T(8,128)S(1)}, f32[520,128]{1,0:T(8,128)S(1)}, u32[]{:S(2)}, u32[]{:S(2)}) %collective-permute-start.3) | collective-permute-done | bytes 266272 | tf_op jit(solution)/shard_map/ppermute | solution.py:107
  12.4 0.0 collective-permute-done.2.e_ref
  12.4 2.6 %prep.1 = (f32[3,4,4,16,128]{4,3,2,1,0:T(8,128)S(1)}, f32[3,4,4,16,128]{4,3,2,1,0:T(8,128)S(1)}, f32[4,4,16,128]{3,2,1,0:T(8,128)S(1)}, f32[2,2,25,16,128]{4,3,2,1,0:T(8,128)S(1)}, f32[2,16,128]{2,1,0:T(8,128)S(1)}) custom-call(f32[192,128]{1,0:T(8,128)S(1)} %get-tuple-element.34.own_u, f32[192,128]{1,0:T(8,128)S(1)} %collective-permute-done.e_u, ...), custom_call_target="tpu_custom_call" | custom-call | tf_op jit(solution)/shard_map/prep/pallas_call | solution.py:432
  15.0 2.1 %substep0.1 = (f32[3,4,16,128]{3,2,1,0:T(8,128)S(1)}, f32[6,2,25,16,128]{4,3,2,1,0:T(8,128)S(1)}, f32[3,5,4,16,128]{4,3,2,1,0:T(8,128)S(1)}, f32[4,40,128]{2,1,0:T(8,128)S(1)}, f32[4,40,128]{2,1,0:T(8,128)S(1)}) custom-call(f32[3,4,4,16,128]{4,3,2,1,0:T(8,128)S(1)} %get-tuple-element.37.u_ref, f32[3,4,4,16,128]{4,3,2,1,0:T(8,128)S(1)} %get-tuple-element.38.v_ref, ...), custom_call_target="tpu_custom_call" | custom-call | tf_op jit(solution)/shard_map/substep0/pallas_call | solution.py:432
  17.1 1.7 %collective-permute-start.6 = (f32[4,40,128]{2,1,0:T(8,128)S(1)}, f32[4,40,128]{2,1,0:T(8,128)S(1)}, u32[]{:S(2)}, u32[]{:S(2)}) collective-permute-start(f32[4,40,128]{2,1,0:T(8,128)S(1)} %get-tuple-element.46), channel_id=1, source_target_pairs={{0,4},{1,5},{2,6},{3,7},{4,0},{5,1},{6,2},{7,3},{8,12},{9,13},{10,... | collective-permute-start | bytes 245768 | tf_op jit(solution)/shard_map/ppermute | solution.py:107
  18.8 0.3 collective-permute-start.7
  19.1 2.5 %collective-permute-done.6.a_ref = f32[4,40,128]{2,1,0:T(8,128)S(1)} collective-permute-done((f32[4,40,128]{2,1,0:T(8,128)S(1)}, f32[4,40,128]{2,1,0:T(8,128)S(1)}, u32[]{:S(2)}, u32[]{:S(2)}) %collective-permute-start.6) | collective-permute-done | bytes 81952 | tf_op jit(solution)/shard_map/ppermute | solution.py:107
  21.6 2.5 %collective-permute-done.7.b_ref = f32[4,40,128]{2,1,0:T(8,128)S(1)} collective-permute-done((f32[4,40,128]{2,1,0:T(8,128)S(1)}, f32[4,40,128]{2,1,0:T(8,128)S(1)}, u32[]{:S(2)}, u32[]{:S(2)}) %collective-permute-start.7) | collective-permute-done | bytes 81952 | tf_op jit(solution)/shard_map/ppermute | solution.py:107
  24.1 2.3 %substep1.1 = (f32[3,5,4,8,128]{4,3,2,1,0:T(8,128)S(1)}, f32[3,5,4,8,128]{4,3,2,1,0:T(8,128)S(1)}, f32[5,4,8,128]{3,2,1,0:T(8,128)S(1)}, f32[3,5,4,8,128]{4,3,2,...) custom-call(f32[3,4,4,16,128]{4,3,2,1,0:T(8,128)S(1)} %get-tuple-element.37.u_ref, ...), custom_call_target="tpu_custom_call" | custom-call | tf_op jit(solution)/shard_map/substep1/pallas_call | solution.py:432
  26.4 0.5 collective-permute-start.8
  26.9 1.5 %collective-permute-start.9 = (f32[3,4,8,128]{3,2,1,0:T(8,128)S(1)}, f32[3,4,8,128]{3,2,1,0:T(8,128)S(1)}, u32[]{:S(2)}, u32[]{:S(2)}) collective-permute-start(f32[3,4,8,128]{3,2,1,0:T(8,128)S(1)} %get-tuple-element.54), channel_id=1, source_target_pairs={{0,1},{1,0},{2,3},{3,2},{4,8},{5,9},{6,10},{7,11},{8,4},{9,5},{10,... | collective-permute-start | bytes 147464 | tf_op jit(solution)/shard_map/ppermute | solution.py:107
  28.4 2.2 %collective-permute-done.8.a_ref = f32[3,4,8,128]{3,2,1,0:T(8,128)S(1)} collective-permute-done((f32[3,4,8,128]{3,2,1,0:T(8,128)S(1)}, f32[3,4,8,128]{3,2,1,0:T(8,128)S(1)}, u32[]{:S(2)}, u32[]{:S(2)}) %collective-permute-start.8) | collective-permute-done | bytes 49184 | tf_op jit(solution)/shard_map/ppermute | solution.py:107
  30.6 1.3 %collective-permute-done.9.b_ref = f32[3,4,8,128]{3,2,1,0:T(8,128)S(1)} collective-permute-done((f32[3,4,8,128]{3,2,1,0:T(8,128)S(1)}, f32[3,4,8,128]{3,2,1,0:T(8,128)S(1)}, u32[]{:S(2)}, u32[]{:S(2)}) %collective-permute-start.9) | collective-permute-done | bytes 49184 | tf_op jit(solution)/shard_map/ppermute | solution.py:107
  31.9 1.2 %substep2.1 = (f32[3,5,4,8,128]{4,3,2,1,0:T(8,128)S(1)}, f32[3,5,4,8,128]{4,3,2,1,0:T(8,128)S(1)}, f32[6,2,25,8,128]{4,3,2,1,0:T(8,128)S(1)}, f32[3,5,4,8,128]{4...) custom-call(f32[3,5,4,8,128]{4,3,2,1,0:T(8,128)S(1)} %get-tuple-element.49.u_ref, ...), custom_call_target="tpu_custom_call" | custom-call | tf_op jit(solution)/shard_map/substep2/pallas_call | solution.py:432
  33.1 1.8 %collective-permute-start.10 = (f32[3,4,8,128]{3,2,1,0:T(8,128)S(1)}, f32[3,4,8,128]{3,2,1,0:T(8,128)S(1)}, u32[]{:S(2)}, u32[]{:S(2)}) collective-permute-start(f32[3,4,8,128]{3,2,1,0:T(8,128)S(1)} %get-tuple-element.58), channel_id=1, source_target_pairs={{0,4},{1,5},{2,6},{3,7},{4,0},{5,1},{6,2},{7,3},{8,12},{9,13},{10,... | collective-permute-start | bytes 147464 | tf_op jit(solution)/shard_map/ppermute | solution.py:107
  35.0 0.1 collective-permute-start.11
  35.1 2.4 %collective-permute-done.10.a_ref = f32[3,4,8,128]{3,2,1,0:T(8,128)S(1)} collective-permute-done((f32[3,4,8,128]{3,2,1,0:T(8,128)S(1)}, f32[3,4,8,128]{3,2,1,0:T(8,128)S(1)}, u32[]{:S(2)}, u32[]{:S(2)}) %collective-permute-start.10) | collective-permute-done | bytes 49184 | tf_op jit(solution)/shard_map/ppermute | solution.py:107
  37.5 2.4 %collective-permute-done.11.b_ref = f32[3,4,8,128]{3,2,1,0:T(8,128)S(1)} collective-permute-done((f32[3,4,8,128]{3,2,1,0:T(8,128)S(1)}, f32[3,4,8,128]{3,2,1,0:T(8,128)S(1)}, u32[]{:S(2)}, u32[]{:S(2)}) %collective-permute-start.11) | collective-permute-done | bytes 49184 | tf_op jit(solution)/shard_map/ppermute | solution.py:107
  39.9 1.3 %substep3.1 = (f32[3,5,4,8,128]{4,3,2,1,0:T(8,128)S(1)}, f32[3,5,4,8,128]{4,3,2,1,0:T(8,128)S(1)}, f32[3,5,4,8,128]{4,3,2,1,0:T(8,128)S(1)}, f32[3,16,128]{2,1,0:T(8,128)S(1)}, f32[3,16,128]{2,1,0:T(8,128)S(1)}) custom-call(f32[3,5,4,8,128]{4,3,2,1,0:T(8,128)S(1)} %get-tuple-element.55.u_ref, f32[3,5,4,8,128]{4,3,2,1,0:T(8,128)S(1)} %get-tuple-element.56.v_ref, ...), custom_call_target="tpu_custom_call" | custom-call | tf_op jit(solution)/shard_map/substep3/pallas_call | solution.py:432
  41.2 0.4 collective-permute-start.12
  41.6 1.5 %collective-permute-start.13 = (f32[3,16,128]{2,1,0:T(8,128)S(1)}, f32[3,16,128]{2,1,0:T(8,128)S(1)}, u32[]{:S(2)}, u32[]{:S(2)}) collective-permute-start(f32[3,16,128]{2,1,0:T(8,128)S(1)} %get-tuple-element.65), channel_id=1, source_target_pairs={{0,1},{1,0},{2,3},{3,2},{4,8},{5,9},{6,10},{7,11},{8,4},{9,5},{10,... | collective-permute-start | bytes 73736 | tf_op jit(solution)/shard_map/ppermute | solution.py:107
  43.2 1.9 %collective-permute-done.12.a_ref = f32[3,16,128]{2,1,0:T(8,128)S(1)} collective-permute-done((f32[3,16,128]{2,1,0:T(8,128)S(1)}, f32[3,16,128]{2,1,0:T(8,128)S(1)}, u32[]{:S(2)}, u32[]{:S(2)}) %collective-permute-start.12) | collective-permute-done | bytes 24608 | tf_op jit(solution)/shard_map/ppermute | solution.py:107
  45.1 1.3 %collective-permute-done.13.b_ref = f32[3,16,128]{2,1,0:T(8,128)S(1)} collective-permute-done((f32[3,16,128]{2,1,0:T(8,128)S(1)}, f32[3,16,128]{2,1,0:T(8,128)S(1)}, u32[]{:S(2)}, u32[]{:S(2)}) %collective-permute-start.13) | collective-permute-done | bytes 24608 | tf_op jit(solution)/shard_map/ppermute | solution.py:107
  46.4 0.8 %end.1 = (f32[3,4,16,128]{3,2,1,0:T(8,128)}, f32[3,4,16,128]{3,2,1,0:T(8,128)}) custom-call(f32[3,5,4,8,128]{4,3,2,1,0:T(8,128)S(1)} %get-tuple-element.61.u_ref, f32[3,5,4,8,128]{4,3,2,1,0:T(8,128)S(1)} %get-tuple-element.62.v_ref, f32[5,4,8,128]{3,2,1,0:T(8,128)S(1)} %get-tuple-element.51.m_ref, f32[3,5,4,8,128]{4,3,2,1,0:T(8,128)S(1)} %get-tuple-element.63.total_ref, ...), custom_call_target="tpu_custom_call" | custom-call | tf_op jit(solution)/shard_map/end/pallas_call | solution.py:432
  (6 shorter events, 0.0 us)
Async XLA Ops:
  0.6 4.9 %collective-permute-start.1 = (f32[192,128]{1,0:T(8,128)}, f32[192,128]{1,0:T(8,128)S(1)}, u32[]{:S(2)}, u32[]{:S(2)}) collective-permute-start(f32[192,128]{1,0:T(8,128)} %bitcast.30), channel_id=1, source_target_pairs={{0,4},{1,2},{2,1},{3,7},{4,0},{5,6},{6,5},{7,3},{8,12},{9,10},{10,... | collective-permute-start | bytes 294920 | tf_op jit(solution)/shard_map/ppermute | solution.py:107
  2.2 3.3 %collective-permute-start = (f32[192,128]{1,0:T(8,128)}, f32[192,128]{1,0:T(8,128)S(1)}, u32[]{:S(2)}, u32[]{:S(2)}) collective-permute-start(f32[192,128]{1,0:T(8,128)} %bitcast.31), channel_id=1, source_target_pairs={{0,1},{1,0},{2,3},{3,2},{4,5},{5,4},{6,7},{7,6},{8,9},{9,8},{10,11... | collective-permute-start | bytes 294920 | tf_op jit(solution)/shard_map/ppermute | solution.py:107
  3.6 8.7 %collective-permute-start.3 = (f32[520,128]{1,0:T(8,128)S(1)}, f32[520,128]{1,0:T(8,128)S(1)}, u32[]{:S(2)}, u32[]{:S(2)}) collective-permute-start(f32[520,128]{1,0:T(8,128)S(1)} %get-tuple-element.35.own_ref), channel_id=1, source_target_pairs={{0,4},{1,2},{2,1},{3,7},{4,0},{5,6},{6,5},{7,3},{8,12},{9,10},{10,... | collective-permute-start | bytes 798728 | tf_op jit(solution)/shard_map/ppermute | solution.py:107
  5.2 7.2 %collective-permute-start.2 = (f32[520,128]{1,0:T(8,128)S(1)}, f32[520,128]{1,0:T(8,128)S(1)}, u32[]{:S(2)}, u32[]{:S(2)}) collective-permute-start(f32[520,128]{1,0:T(8,128)S(1)} %get-tuple-element.35.own_ref), channel_id=1, source_target_pairs={{0,1},{1,0},{2,3},{3,2},{4,5},{5,4},{6,7},{7,6},{8,9},{9,8},{10,11... | collective-permute-start | bytes 798728 | tf_op jit(solution)/shard_map/ppermute | solution.py:107
  5.6 9.4 %collective-permute-start.5 = (f32[3,48,128]{2,1,0:T(8,128)S(1)}, f32[3,48,128]{2,1,0:T(8,128)S(1)}, u32[]{:S(2)}, u32[]{:S(2)}) collective-permute-start(f32[3,48,128]{2,1,0:T(8,128)S(1)} %pad_maximum_fusion), channel_id=1, source_target_pairs={{0,1},{1,0},{2,3},{3,2},{4,8},{5,9},{6,10},{7,11},{8,4},{9,5},{10,... | collective-permute-start | bytes 221192 | tf_op jit(solution)/shard_map/ppermute | solution.py:107
  7.0 8.0 %collective-permute-start.4 = (f32[3,48,128]{2,1,0:T(8,128)S(1)}, f32[3,48,128]{2,1,0:T(8,128)S(1)}, u32[]{:S(2)}, u32[]{:S(2)}) collective-permute-start(f32[3,48,128]{2,1,0:T(8,128)S(1)} %pad_maximum_fusion), channel_id=1, source_target_pairs={{0,4},{1,5},{2,6},{3,7},{4,0},{5,1},{6,2},{7,3},{8,12},{9,13},{10,... | collective-permute-start | bytes 221192 | tf_op jit(solution)/shard_map/ppermute | solution.py:107
  17.1 4.5 %collective-permute-start.6 = (f32[4,40,128]{2,1,0:T(8,128)S(1)}, f32[4,40,128]{2,1,0:T(8,128)S(1)}, u32[]{:S(2)}, u32[]{:S(2)}) collective-permute-start(f32[4,40,128]{2,1,0:T(8,128)S(1)} %get-tuple-element.46), channel_id=1, source_target_pairs={{0,4},{1,5},{2,6},{3,7},{4,0},{5,1},{6,2},{7,3},{8,12},{9,13},{10,... | collective-permute-start | bytes 245768 | tf_op jit(solution)/shard_map/ppermute | solution.py:107
  18.8 5.3 %collective-permute-start.7 = (f32[4,40,128]{2,1,0:T(8,128)S(1)}, f32[4,40,128]{2,1,0:T(8,128)S(1)}, u32[]{:S(2)}, u32[]{:S(2)}) collective-permute-start(f32[4,40,128]{2,1,0:T(8,128)S(1)} %get-tuple-element.47), channel_id=1, source_target_pairs={{0,1},{1,0},{2,3},{3,2},{4,8},{5,9},{6,10},{7,11},{8,4},{9,5},{10,... | collective-permute-start | bytes 245768 | tf_op jit(solution)/shard_map/ppermute | solution.py:107
  26.4 4.2 %collective-permute-start.8 = (f32[3,4,8,128]{3,2,1,0:T(8,128)S(1)}, f32[3,4,8,128]{3,2,1,0:T(8,128)S(1)}, u32[]{:S(2)}, u32[]{:S(2)}) collective-permute-start(f32[3,4,8,128]{3,2,1,0:T(8,128)S(1)} %get-tuple-element.53), channel_id=1, source_target_pairs={{0,4},{1,5},{2,6},{3,7},{4,0},{5,1},{6,2},{7,3},{8,12},{9,13},{10,... | collective-permute-start | bytes 147464 | tf_op jit(solution)/shard_map/ppermute | solution.py:107
  26.9 5.0 %collective-permute-start.9 = (f32[3,4,8,128]{3,2,1,0:T(8,128)S(1)}, f32[3,4,8,128]{3,2,1,0:T(8,128)S(1)}, u32[]{:S(2)}, u32[]{:S(2)}) collective-permute-start(f32[3,4,8,128]{3,2,1,0:T(8,128)S(1)} %get-tuple-element.54), channel_id=1, source_target_pairs={{0,1},{1,0},{2,3},{3,2},{4,8},{5,9},{6,10},{7,11},{8,4},{9,5},{10,... | collective-permute-start | bytes 147464 | tf_op jit(solution)/shard_map/ppermute | solution.py:107
  33.1 4.4 %collective-permute-start.10 = (f32[3,4,8,128]{3,2,1,0:T(8,128)S(1)}, f32[3,4,8,128]{3,2,1,0:T(8,128)S(1)}, u32[]{:S(2)}, u32[]{:S(2)}) collective-permute-start(f32[3,4,8,128]{3,2,1,0:T(8,128)S(1)} %get-tuple-element.58), channel_id=1, source_target_pairs={{0,4},{1,5},{2,6},{3,7},{4,0},{5,1},{6,2},{7,3},{8,12},{9,13},{10,... | collective-permute-start | bytes 147464 | tf_op jit(solution)/shard_map/ppermute | solution.py:107
  35.0 5.0 %collective-permute-start.11 = (f32[3,4,8,128]{3,2,1,0:T(8,128)S(1)}, f32[3,4,8,128]{3,2,1,0:T(8,128)S(1)}, u32[]{:S(2)}, u32[]{:S(2)}) collective-permute-start(f32[3,4,8,128]{3,2,1,0:T(8,128)S(1)} %get-tuple-element.59), channel_id=1, source_target_pairs={{0,1},{1,0},{2,3},{3,2},{4,8},{5,9},{6,10},{7,11},{8,4},{9,5},{10,... | collective-permute-start | bytes 147464 | tf_op jit(solution)/shard_map/ppermute | solution.py:107
  41.2 3.9 %collective-permute-start.12 = (f32[3,16,128]{2,1,0:T(8,128)S(1)}, f32[3,16,128]{2,1,0:T(8,128)S(1)}, u32[]{:S(2)}, u32[]{:S(2)}) collective-permute-start(f32[3,16,128]{2,1,0:T(8,128)S(1)} %get-tuple-element.64), channel_id=1, source_target_pairs={{0,4},{1,5},{2,6},{3,7},{4,0},{5,1},{6,2},{7,3},{8,12},{9,13},{10,... | collective-permute-start | bytes 73736 | tf_op jit(solution)/shard_map/ppermute | solution.py:107
  41.6 4.7 %collective-permute-start.13 = (f32[3,16,128]{2,1,0:T(8,128)S(1)}, f32[3,16,128]{2,1,0:T(8,128)S(1)}, u32[]{:S(2)}, u32[]{:S(2)}) collective-permute-start(f32[3,16,128]{2,1,0:T(8,128)S(1)} %get-tuple-element.65), channel_id=1, source_target_pairs={{0,1},{1,0},{2,3},{3,2},{4,8},{5,9},{6,10},{7,11},{8,4},{9,5},{10,... | collective-permute-start | bytes 73736 | tf_op jit(solution)/shard_map/ppermute | solution.py:107

commit v2 on v0

v2 whole, which is shorter than its diff:
```python
import functools

import jax
import jax.numpy as jnp
import numpy as np
from jax import lax
from jax.experimental import pallas as pl
from jax.experimental.pallas import tpu as pltpu
from jax.sharding import PartitionSpec as P

time_step = 0.1
LEVELS = 3
F32 = jnp.float32
BF16 = jnp.bfloat16


def gll_tables():
    points = np.array([-1.0, -np.sqrt(3.0 / 7.0), 0.0, np.sqrt(3.0 / 7.0), 1.0])
    weights = np.array([0.1, 49.0 / 90.0, 32.0 / 45.0, 49.0 / 90.0, 0.1])
    legendre = (35.0 * points**4 - 30.0 * points**2 + 3.0) / 8.0
    derivative = np.zeros((5, 5))
    for row_index in range(5):
        for col_index in range(5):
            if row_index != col_index:
                derivative[row_index, col_index] = legendre[row_index] / (
                    legendre[col_index] * (points[row_index] - points[col_index])
                )
    derivative[0, 0] = -5.0
    derivative[4, 4] = 5.0
    return (derivative, weights)


D, W = gll_tables()


def split(table):
    high = np.asarray(table, np.float32).astype(BF16)
    low = (np.asarray(table, np.float64) - high.astype(np.float64)).astype(BF16)
    return high, low


def depth_tables(depth):
    lanes = 4 * depth
    table = np.zeros((lanes, 2 * lanes))
    for c in range(depth):
        for i in range(5):
            if 4 * c + i < lanes:
                for k in range(4):
                    table[4 * c + i, 4 * c + k] = D[k, i]
                table[4 * c + i, lanes + (4 * (c + 1)) % lanes] = D[4, i]
    high, low = split(table)
    gradient = np.concatenate([high, high, low], axis=0)
    divergence = np.concatenate([high.T, high.T, low.T], axis=0)
    return gradient, divergence


def weight_table(depth):
    lanes = 4 * depth
    pair = (W[:, None] * W[None, :]).reshape(25, 1)
    main = pair * np.tile(W[:4], depth)[None, :]
    last = pair * np.where(np.arange(lanes) % 4 == 0, W[4], 0.0)[None, :]
    return np.concatenate([main, last], axis=0).astype(np.float32)


def apply5(matrix, x):
    s0, s1 = x[0] + x[4], x[1] + x[3]
    d0, d1 = x[0] - x[4], x[1] - x[3]

    def even(a):
        p, q = (matrix[a, 0] - matrix[a, 4]) / 2, (matrix[a, 1] - matrix[a, 3]) / 2
        return d0 * float(p) + d1 * float(q)

    def odd(a):
        p, q = (matrix[a, 0] + matrix[a, 4]) / 2, (matrix[a, 1] + matrix[a, 3]) / 2
        return s0 * float(p) + s1 * float(q) + x[2] * float(matrix[a, 2])

    e0, e1, e2 = even(0), even(1), even(2)
    o0, o1 = odd(0), odd(1)
    return [e0 + o0, e1 + o1, e2, e1 - o1, e0 - o0]


def apply5_middle(matrix, x):
    s1, d1 = x[0] + x[2], x[0] - x[2]
    e = [d1 * float((matrix[a, 1] - matrix[a, 3]) / 2) for a in range(3)]
    o = [s1 * float((matrix[a, 1] + matrix[a, 3]) / 2) + x[1] * float(matrix[a, 2]) for a in range(2)]
    return [e[0] + o[0], e[1] + o[1], e[2], e[1] - o[1], e[0] - o[0]]


def apply5_ends(matrix, first, last, middle):
    s0, d0 = first + last, first - last
    e = [d0 * float((matrix[a, 0] - matrix[a, 4]) / 2) for a in range(3)]
    o = [s0 * float((matrix[a, 0] + matrix[a, 4]) / 2) for a in range(2)]
    ends = [e[0] + o[0], e[1] + o[1], e[2], e[1] - o[1], e[0] - o[0]]
    return [middle[a] + ends[a] for a in range(5)]


def halves(x):
    high = x.astype(BF16)
    return high, (x - high.astype(F32)).astype(BF16)


def rolled(x, by):
    return pltpu.roll(x, by % x.shape[0], 0)


def swap_pairs(nx, ny, along_x, odd):
    pairs = []
    for i in range(nx):
        for j in range(ny):
            here, size = (i, nx) if along_x else (j, ny)
            there = here + 1 if (here % 2 == 1) == odd else here - 1
            if 0 <= there < size:
                target = (there, j) if along_x else (i, there)
            else:
                target = (i, j ^ 1) if along_x else (i ^ 1, j)
            if target[0] < nx and target[1] < ny:
                pairs.append((i * ny + j, target[0] * ny + target[1]))
    return pairs


def swap(mesh_sizes, along_x, odd, x):
    return lax.ppermute(x, ("px", "py"), swap_pairs(*mesh_sizes, along_x, odd))


def place(axis, size):
    here = lax.axis_index(axis)
    return lax.rem(here, 2) == 0, here == 0, here == size - 1


def load_kernel(count, *refs):
    sources, targets, layer, sems = refs[:count], refs[count : 2 * count], refs[2 * count], refs[2 * count + 1]
    copies = [pltpu.make_async_copy(a, b, sems.at[n]) for n, (a, b) in enumerate(zip(sources, targets))]
    for copy in copies:
        copy.start()
    copies[0].wait()
    across = layer.shape[1]
    for c in range(3):
        layer[c] = targets[0][4 * c * across : (4 * c + 1) * across, :]
    for copy in copies[1:]:
        copy.wait()


def pack_kernel(starts, first_ref, second_ref, level_ref, out):
    for p, table in enumerate((first_ref, second_ref)):
        for row in range(125):
            i, j, k = row // 25, row // 5 % 5, row % 5
            out[starts[p] + row : starts[p] + row + 1, :] = table[i, j, k]
    out[starts[2] : starts[2] + 1, :] = level_ref[...].astype(F32)


def join_kernel(v_ref, m_ref, out):
    count = v_ref.shape[0]
    out[:count, :] = v_ref[...]
    out[count:, :] = m_ref[...]


def sides(ny):
    even, first, last = place("py", ny)

    def left(e, o, at):
        return jnp.where(first, 0.0, jnp.where(even, o[at], e[at]))

    def right(e, o, at):
        return jnp.where(last, 0.0, jnp.where(even, e[at], o[at]))

    return left, right


def rim_kernel(ny, own, e, o, out):
    left, right = sides(ny)
    across = own.shape[1]
    for c in range(3):
        at = (slice(4 * c * across, (4 * c + 1) * across), slice(None))
        out[c, :across, :] = left(e, o, at)
        out[c, across : 2 * across, :] = own[c]
        out[c, 2 * across :, :] = right(e, o, at)


def spread(sizes, own, e, o, base, out):
    ny, ey, lanes = sizes
    left, right = sides(ny)
    for j in range(4):
        at = (pl.ds(base + j, ey, stride=4), slice(None))
        out[j, 0:ey, :] = left(e, o, at)
        out[j, ey : 2 * ey, :] = own[at]
        out[j, 2 * ey : 3 * ey, :] = right(e, o, at)
        out[j, 3 * ey :, :] = jnp.zeros((ey, lanes), F32)


def spread_u_kernel(sizes, own, e, o, ends, inner):
    tall = 4 * sizes[1]
    for c in range(3):
        spread(sizes, own, e, o, 4 * c * tall, ends.at[c])
        for i in range(3):
            spread(sizes, own, e, o, (4 * c + 1 + i) * tall, inner.at[c, i])


def spread_v_kernel(sizes, own_v, own_m, e, o, v_ends, v_inner, m_ends, m_inner):
    tall = 4 * sizes[1]
    base = 12 * tall
    for c in range(3):
        spread(sizes, own_v, e, o, 4 * c * tall, v_ends.at[c])
        for i in range(3):
            spread(sizes, own_v, e, o, (4 * c + 1 + i) * tall, v_inner.at[c, i])
    spread(sizes, own_m, e.at[base:], o.at[base:], 0, m_ends)
    for i in range(3):
        spread(sizes, own_m, e.at[base:], o.at[base:], (1 + i) * tall, m_inner.at[i])


def tables_kernel(sizes, starts, own_ref, e_ref, o_ref, weight_ref, lame_ref, level_ref, sel):
    ny, ey, lanes = sizes
    left, right = sides(ny)
    sel[0] = left(e_ref, o_ref, ...)
    sel[1] = own_ref[...]
    sel[2] = right(e_ref, o_ref, ...)

    shape = (2 * ey, lanes)
    sub = lax.broadcasted_iota(jnp.int32, shape, 0)
    lane = lax.broadcasted_iota(jnp.int32, shape, 1)
    ez = lanes // 4
    column = lax.rem(sub, ey) * ez
    main_at = column + lane // 4
    last_at = column + lax.rem(lane // 4 + ez - 1, ez)
    point = lax.rem(lane, 4)
    upper = sub < ey

    def both(row):
        zero = jnp.zeros(shape, F32)
        a = jnp.broadcast_to(sel[0, pl.ds(row, 1), :], shape)
        b = jnp.broadcast_to(sel[1, pl.ds(row, 1), :], shape)
        c = jnp.broadcast_to(sel[2, pl.ds(row, 1), :], shape)
        return jnp.where(upper, a, b), jnp.where(upper, c, zero)

    def gather(x, at):
        return jnp.take_along_axis(x, at, axis=1, mode="promise_in_bounds")

    for ij in range(25):
        weight = jnp.broadcast_to(weight_ref[ij : ij + 1, :], shape)
        weight_last = jnp.broadcast_to(weight_ref[25 + ij : 26 + ij, :], shape)
        for p in range(2):
            points = [both(starts[p] + ij * 5 + k) for k in range(5)]
            for h in range(2):
                got = [gather(points[k][h], main_at) for k in range(4)]
                main = jnp.where(
                    point < 2, jnp.where(point == 0, got[0], got[1]), jnp.where(point == 2, got[2], got[3])
                )
                lame_ref[p, 0, ij, 2 * ey * h : 2 * ey * (h + 1), :] = main * weight
                lame_ref[p, 1, ij, 2 * ey * h : 2 * ey * (h + 1), :] = gather(points[4][h], last_at) * weight_last
    levels = both(starts[2])
    for h in range(2):
        level_ref[0, 2 * ey * h : 2 * ey * (h + 1), :] = gather(levels[h], main_at)
        level_ref[1, 2 * ey * h : 2 * ey * (h + 1), :] = gather(levels[h], last_at)


def five(values):
    return list(values) + [rolled(values[0], -1)]


def grad_z(points, grad_ref, out):
    count, tall, lanes = points.shape
    high, low = halves(points[...].reshape(count * tall, lanes))
    lhs = jnp.concatenate([high, low, high], axis=1)
    out[...] = jnp.dot(lhs, grad_ref[...], preferred_element_type=F32).reshape(count, tall, 2 * lanes)


def div_z(flux_z, spans, div_ref, out):
    _, _, _, tall, lanes = flux_z.shape
    parts = []
    for e in range(2):
        rows = [flux_z[c, e, at].reshape(-1, lanes) for c in range(3) for at in spans]
        parts.append(halves(jnp.concatenate(rows, axis=0)))
    lhs = jnp.concatenate([parts[0][0], parts[1][0], parts[0][1], parts[1][1], parts[0][0], parts[1][0]], axis=1)
    out[...] = jnp.dot(lhs, div_ref[...], preferred_element_type=F32).reshape(out.shape)


def before(inner, tall, grad_ref, gz, gy, px, us):
    for c in range(3):
        points = [five(inner[c][i]) for i in range(3)]
        for i in range(3):
            for j in range(5):
                us[15 * c + 5 * i + j] = points[i][j]
        for i in range(3):
            y = apply5(D, points[i])
            for j in range(5):
                gy[c, 5 * i + j] = y[j]
        for j in range(5):
            y = apply5_middle(D, [points[i][j] for i in range(3)])
            for i in range(5):
                px[c, 5 * i + j] = y[i]
    grad_z(us, grad_ref, gz)


def stresses(tall, windows, keep, ends, gz, gy, px, lame, level, old, new, flux, flux_z, grad_ref, div_ref, us, gx, gz_ends, qz, total):
    lanes = px.shape[-1]
    points = [[five(ends[c][side]) for side in range(2)] for c in range(3)]
    for c in range(3):
        for side in range(2):
            for j in range(5):
                us[10 * c + 5 * side + j] = points[c][side][j]
    grad_z(us, grad_ref, gz_ends)
    for c in range(3):
        for j in range(5):
            y = apply5_ends(D, points[c][0][j], points[c][1][j], [px[c, 5 * i + j] for i in range(5)])
            for i in range(5):
                gx[c, 5 * i + j] = y[i]
    inner = (lax.broadcasted_iota(jnp.int32, (8, lanes), 1) > 0).astype(F32)
    for h in range(tall // 8):
        at = slice(8 * h, 8 * h + 8)
        table = slice(windows[0] + 8 * h, windows[0] + 8 * h + 8)
        stored = slice(windows[1] + 8 * h, windows[1] + 8 * h + 8)
        if keep is not None:
            fresh = [keep(level[e, table, :]) for e in range(2)]
        for i in (0, 4, 1, 2, 3):
            side = {0: 0, 4: 1}.get(i)
            if side is not None:
                ends_y = [apply5(D, [us[10 * c + 5 * side + j, at, :] for j in range(5)]) for c in range(3)]
            for j in range(5):
                p = 5 * i + j
                grads_x = [gx[c, p, at, :] for c in range(3)]
                if side is None:
                    grads_y = [gy[c, p - 5, at, :] for c in range(3)]
                else:
                    grads_y = [ends_y[c][j] for c in range(3)]
                sums = []
                for e in range(2):
                    span = slice(e * lanes, (e + 1) * lanes)
                    if side is None:
                        grads_z = [gz[15 * c + p - 5, at, span] for c in range(3)]
                    else:
                        grads_z = [gz_ends[10 * c + 5 * side + j, at, span] for c in range(3)]
                    if e == 1:
                        grads_x = [g * inner for g in grads_x]
                        grads_y = [g * inner for g in grads_y]
                    first, second = lame[0, e, p, table, :], lame[1, e, p, table, :]
                    trace = first * (grads_x[0] + grads_y[1] + grads_z[2])
                    twice = second + second
                    stress = [
                        trace + twice * grads_x[0],
                        trace + twice * grads_y[1],
                        second * (grads_y[0] + grads_x[1]),
                        second * (grads_z[0] + grads_x[2]),
                        second * (grads_z[1] + grads_y[2]),
                        trace + twice * grads_z[2],
                    ]
                    if keep is not None:
                        stress = [jnp.where(fresh[e], stress[n], old[n, e, p, stored, :]) for n in range(6)]
                    if new is not None:
                        for n in range(6):
                            new[n, e, p, at, :] = stress[n]
                    else:
                        for n in range(3):
                            flux_z[n, e, p, at, :] = stress[3 + n]
                    if e == 1:
                        stress = [x * inner for x in stress[:5]]
                    sums.append(stress)
                for n in range(5):
                    flux[n, p, at, :] = sums[0][n] + sums[1][n]
    if flux_z is None:
        flux_z = new.at[3:6]
    div_z(flux_z, [slice(0, 5), slice(20, 25)], div_ref, qz)
    assemble((0, 4), flux, qz, lambda c, side, j, value: total.__setitem__((c, side, j), value))


ACROSS_X, ACROSS_Y = (0, 2, 3), (2, 1, 4)


def assemble(layers, flux, qz, put):
    for c in range(3):
        pieces = []
        for j in range(5):
            x = apply5(D.T, [flux[ACROSS_X[c], 5 * i + j] for i in range(5)])
            pieces.append([x[i] for i in layers])
        for n, i in enumerate(layers):
            y = apply5(D.T, [flux[ACROSS_Y[c], 5 * i + j] for j in range(5)])
            z = [pieces[j][n] + (y[j] + qz[c, 5 * n + j]) for j in range(5)]
            put(c, n, 0, z[0] + rolled(z[4], 1))
            for j in range(1, 4):
                put(c, n, j, z[j])


def first_kernel(u_inner, grad_ref, gz, gy, px, us):
    tall = u_inner.shape[3]
    inner = [[[u_inner[c, i, j] for j in range(4)] for i in range(3)] for c in range(3)]
    before(inner, tall, grad_ref, gz, gy, px, us)


def between_kernel(rows, last, flux, flux_z, u_ref, v_ref, m_ref, grad_ref, div_ref, *refs):
    if last:
        u_out, v_out, qz = refs
    else:
        u_out, v_out, m_out, gz, gy, px, qz, us = refs
    if flux_z.shape[0] == 6:
        flux_z = flux_z.at[3:6]
    div_z(flux_z, [slice(5, 20)], div_ref, qz)
    inner = [[[None] * 4 for _ in range(3)] for _ in range(3)]

    def put(c, n, j, force):
        mass = m_ref[n, j, rows, :]
        speed = v_ref[c, n, j, rows, :] - time_step * mass * force[rows]
        position = u_ref[c, n, j, rows, :] + time_step * speed
        if last:
            count = rows.stop - rows.start
            u_out[c, n, pl.ds(j, count, stride=4), :] = position
            v_out[c, n, pl.ds(j, count, stride=4), :] = speed
            return
        u_out[c, n, j], v_out[c, n, j] = position, speed
        if c == 0:
            m_out[n, j] = mass
        inner[c][n][j] = position

    assemble((1, 2, 3), flux, qz, put)
    if not last:
        before(inner, rows.stop - rows.start, grad_ref, gz, gy, px, us)


def start_kernel(sizes, u_ref, v_ref, m_ref, a_ref, b_ref, gz, gy, px, lame, level, grad_ref, div_ref,
                 rim_ref, new, flux, total, send_a, send_b, us, gx, gz_ends, qz):
    nx, ey, lanes = sizes
    even, _, last = place("px", nx)
    tall, wide = 4 * ey, 3 * ey
    for c in range(3):
        for j in range(4):
            at = pl.ds(j, wide, stride=4)
            rim = jnp.where(last, 0.0, jnp.where(even, a_ref[c, at, :], b_ref[c, at, :]))
            rim_ref[c, j, 0:wide, :] = rim
            rim_ref[c, j, wide:, :] = jnp.zeros((tall - wide, lanes), F32)
    ends = [[[u_ref[c, j] for j in range(4)], [rim_ref[c, j] for j in range(4)]] for c in range(3)]
    stresses(tall, (0, 0), None, ends, gz, gy, px, lame, level, None, new, flux, None, grad_ref, div_ref, us, gx, gz_ends, qz, total)
    count = wide - 2
    rows = slice(1, 1 + count)
    for j in range(4):
        at = slice(j * count, (j + 1) * count)
        mass = m_ref[j, rows, :]
        for c in range(3):
            back = v_ref[c, j, rows, :] - time_step * mass * total[c, 0, j, rows, :]
            ahead = total[c, 1, j, rows, :]
            send_a[c, at, :] = jnp.where(even, ahead, back)
            send_b[c, at, :] = jnp.where(even, back, ahead)
        send_a[3, at, :] = mass
        send_b[3, at, :] = mass


def second_kernel(sizes, u_ref, rim_ref, v_ref, m_ref, total_ref, a_ref, b_ref, gz, gy, px, old, lame, level, grad_ref, div_ref,
                  u_out, v_out, m_out, flux, flux_z, total_out, send_a, send_b, got, us, gx, gz_ends, qz, total):
    nx, ey, lanes = sizes
    even, first, last = place("px", nx)
    tall, count = 4 * ey, 3 * ey - 2
    rows = slice(1, 1 + count)
    window = slice(ey - 2, 3 * ey - 2)
    got[...] = jnp.zeros(got.shape, F32)
    for j in range(4):
        at = slice(j * count, (j + 1) * count)
        for c in range(4):
            got[0, c, j, rows, :] = jnp.where(last, 0.0, jnp.where(even, a_ref[c, at, :], b_ref[c, at, :]))
        for c in range(3):
            got[1, c, j, rows, :] = jnp.where(first, 0.0, jnp.where(even, b_ref[c, at, :], a_ref[c, at, :]))
    ends = [[[], []] for _ in range(3)]
    for c in range(3):
        for side in range(2):
            for j in range(4):
                if side == 0:
                    mass, speed, position = m_ref[j], v_ref[c, j], u_ref[c, j]
                    force = total_ref[c, 0, j] + got[1, c, j]
                else:
                    mass, speed, position = got[0, 3, j], got[0, c, j], rim_ref[c, j]
                    force = total_ref[c, 1, j]
                speed = speed - time_step * mass * force
                position = position + time_step * speed
                u_out[c, side, j], v_out[c, side, j] = position[window], speed[window]
                if c == 0:
                    m_out[side, j] = mass[window]
                ends[c][side].append(position)
    stresses(tall, (0, 0), lambda level_of: level_of > 1.5, ends, gz, gy, px, lame, level, old, None, flux, flux_z,
             grad_ref, div_ref, us, gx, gz_ends, qz, total)
    for c in range(3):
        for j in range(4):
            back, ahead = total[c, 0, j, window, :], total[c, 1, j, window, :]
            total_out[c, 0, j], total_out[c, 1, j] = back, ahead
            send_a[c, j] = jnp.where(even, ahead, back)
            send_b[c, j] = jnp.where(even, back, ahead)


def later_kernel(sizes, final, u_ref, v_ref, m_ref, total_ref, a_ref, b_ref, gz, gy, px, old, lame, level, grad_ref, div_ref, *refs):
    nx, ey, lanes = sizes
    u_out, v_out, flux, held, total, send_a, send_b, us, gx, gz_ends, qz = refs
    if final:
        new, flux_z, keep, windows = None, held, lambda level_of: level_of > 1.5, (ey - 2, 0)
    else:
        new, flux_z, keep, windows = held, None, lambda level_of: level_of > 0.5, (ey - 2, ey - 2)
    even, first, last = place("px", nx)
    ends = [[[], []] for _ in range(3)]
    for c in range(3):
        for side in range(2):
            for j in range(4):
                if side == 0:
                    got = jnp.where(first, 0.0, jnp.where(even, b_ref[c, j], a_ref[c, j]))
                else:
                    got = jnp.where(last, 0.0, jnp.where(even, a_ref[c, j], b_ref[c, j]))
                speed = v_ref[c, side, j] - time_step * m_ref[side, j] * (total_ref[c, side, j] + got)
                position = u_ref[c, side, j] + time_step * speed
                u_out[c, side, j], v_out[c, side, j] = position, speed
                ends[c][side].append(position)
    stresses(2 * ey, windows, keep, ends, gz, gy, px, lame, level, old, new, flux, flux_z,
             grad_ref, div_ref, us, gx, gz_ends, qz, total)
    for c in range(3):
        for j in range(4):
            if final:
                at = slice(j * ey, (j + 1) * ey)
                ahead = total[c, 1, j, 2 : 2 + ey, :]
                send_a[c, at, :] = ahead
                send_b[c, at, :] = ahead
            else:
                back, ahead = total[c, 0, j], total[c, 1, j]
                send_a[c, j] = jnp.where(even, ahead, back)
                send_b[c, j] = jnp.where(even, back, ahead)


def end_kernel(sizes, u_ref, v_ref, m_ref, total_ref, a_ref, b_ref, u_inner, v_inner, u_out, v_out):
    nx, ey, lanes = sizes
    even, first, _ = place("px", nx)
    mine = slice(2, 2 + ey)
    for c in range(3):
        for j in range(4):
            at = slice(j * ey, (j + 1) * ey)
            got = jnp.where(first, 0.0, jnp.where(even, b_ref[c, at, :], a_ref[c, at, :]))
            force = total_ref[c, 0, j, mine, :] + got
            speed = v_ref[c, 0, j, mine, :] - time_step * m_ref[0, j, mine, :] * force
            v_out[c, 0, pl.ds(j, ey, stride=4), :] = speed
            u_out[c, 0, pl.ds(j, ey, stride=4), :] = u_ref[c, 0, j, mine, :] + time_step * speed
        for i in range(3):
            u_out[c, 1 + i] = u_inner[c, i]
            v_out[c, 1 + i] = v_inner[c, i]


def call(kernel, name, outs, scratch, *args, cost=None):
    shapes = [jax.ShapeDtypeStruct(s, F32) if name == "end" else pltpu.VMEM(s, F32) for s in outs]
    return pl.pallas_call(
        kernel,
        out_shape=shapes,
        scratch_shapes=[pltpu.VMEM(s, F32) for s in scratch],
        compiler_params=pltpu.CompilerParams(vmem_limit_bytes=32 * 1024 * 1024),
        cost_estimate=cost,
        name=name,
    )(*args)


def shards(sizes, displacement, velocity, inverse_mass, lame_first, lame_second, level_map):
    nx, ny = sizes
    _, ex4, ey4, lanes = displacement.shape
    ey = ey4 // 4
    tall, wide, short = 4 * ey, 3 * ey, 2 * ey
    move = functools.partial(swap, sizes)

    def along_x(a, b):
        return move(True, False, a), move(True, True, b)

    def along_y(x):
        return move(False, False, x), move(False, True, x)

    flat = [x.reshape(-1, lanes) for x in (displacement, velocity, inverse_mass)]
    u_e, u_o = along_y(flat[0])
    gradient, divergence = depth_tables(lanes // 4)
    tables = [jnp.asarray(t) for t in (gradient, divergence, weight_table(lanes // 4))]
    sources = flat + [lame_first, lame_second, level_map] + tables
    own_u, own_v, own_m, first, second, level, gradient, divergence, weights, layer = pl.pallas_call(
        functools.partial(load_kernel, len(sources)),
        out_shape=[pltpu.VMEM(x.shape, x.dtype) for x in sources] + [pltpu.VMEM((3, ey4, lanes), F32)],
        in_specs=[pl.BlockSpec(memory_space=pl.ANY)] * len(sources),
        scratch_shapes=[pltpu.SemaphoreType.DMA((len(sources),))],
        name="load",
    )(*sources)
    starts = (0, 128, 256)
    (own,) = call(functools.partial(pack_kernel, starts), "pack", [(264, lanes)], [], first, second, level)
    from_e, from_o = along_y(own)
    (rim,) = call(functools.partial(rim_kernel, ny), "rim", [(3, 3 * ey4, lanes)], [], layer, u_e, u_o)
    rim_a, rim_b = along_x(rim, rim)
    (joined,) = call(join_kernel, "join", [(own_v.shape[0] + own_m.shape[0], lanes)], [], own_v, own_m)
    v_e, v_o = along_y(joined)

    sizes_y, sizes_x = (ny, ey, lanes), (nx, ey, lanes)

    def shape(*lead, rows=tall):
        return (*lead, rows, lanes)

    def gradients(rows):
        return [(45, rows, 2 * lanes), shape(3, 15, rows=rows), shape(3, 25, rows=rows)]

    def scratch(rows):
        return [shape(30, rows=rows), shape(3, 25, rows=rows), (30, rows, 2 * lanes), shape(3, 10, rows=rows)]

    def fluxes(rows, kinds):
        return [shape(5, 25, rows=rows), shape(kinds, 2, 25, rows=rows)]

    u_ends, u_inner = call(
        functools.partial(spread_u_kernel, sizes_y), "spread_u", [shape(3, 4), shape(3, 3, 4)], [], own_u, u_e, u_o
    )
    near = call(first_kernel, "before0", gradients(tall), [shape(45)], u_inner, gradient)
    lame, level = call(
        functools.partial(tables_kernel, sizes_y, starts), "tables", [shape(2, 2, 25), shape(2)], [(3, 264, lanes)],
        own, from_e, from_o, weights,
    )
    v_ends, v_inner, m_ends, m_inner = call(
        functools.partial(spread_v_kernel, sizes_y), "spread_v",
        [shape(3, 4), shape(3, 3, 4), shape(4), shape(3, 4)], [], own_v, own_m, v_e, v_o,
    )

    count = wide - 2
    rim_u, old, flux, total, send_a, send_b = call(
        functools.partial(start_kernel, sizes_x), "stress0",
        [shape(3, 4), shape(6, 2, 25), shape(5, 25), shape(3, 2, 4), (4, 4 * count, lanes), (4, 4 * count, lanes)],
        scratch(tall),
        u_ends, v_ends, m_ends, rim_a, rim_b, *near, lame, level, gradient, divergence,
    )
    got_a, got_b = along_x(send_a, send_b)
    every, window, mine = slice(0, tall), slice(ey - 2, 3 * ey - 2), slice(2, 2 + ey)
    u_inner, v_inner, m_inner, *near = call(
        functools.partial(between_kernel, every, False), "between0",
        [shape(3, 3, 4), shape(3, 3, 4), shape(3, 4)] + gradients(tall), [shape(3, 15), shape(45)],
        flux, old, u_inner, v_inner, m_inner, gradient, divergence,
    )

    ends = shape(3, 2, 4, rows=short)
    message = shape(3, 4, rows=short)
    u_ends, v_ends, m_ends, flux, flux_z, total, send_a, send_b = call(
        functools.partial(second_kernel, sizes_x), "stress1",
        [ends, ends, ends[1:], *fluxes(tall, 3), ends, message, message],
        [shape(2, 4, 4)] + scratch(tall) + [shape(3, 2, 4)],
        u_ends, rim_u, v_ends, m_ends, total, got_a, got_b, *near, old, lame, level, gradient, divergence,
    )
    got_a, got_b = along_x(send_a, send_b)
    inner = shape(3, 3, 4, rows=short)
    u_inner, v_inner, m_inner, *near = call(
        functools.partial(between_kernel, window, False), "between1",
        [inner, inner, inner[1:]] + gradients(short), [shape(3, 15), shape(45, rows=short)],
        flux, flux_z, u_inner, v_inner, m_inner, gradient, divergence,
    )

    u_ends, v_ends, flux, old, total, send_a, send_b = call(
        functools.partial(later_kernel, sizes_x, False), "stress2",
        [ends, ends, *fluxes(short, 6), ends, message, message], scratch(short),
        u_ends, v_ends, m_ends, total, got_a, got_b, *near, old, lame, level, gradient, divergence,
    )
    got_a, got_b = along_x(send_a, send_b)
    every = slice(0, short)
    u_inner, v_inner, m_inner, *near = call(
        functools.partial(between_kernel, every, False), "between2",
        [inner, inner, inner[1:]] + gradients(short), [shape(3, 15, rows=short), shape(45, rows=short)],
        flux, old, u_inner, v_inner, m_inner, gradient, divergence,
    )

    message = (3, 4 * ey, lanes)
    u_ends, v_ends, flux, flux_z, total, send_a, send_b = call(
        functools.partial(later_kernel, sizes_x, True), "stress3",
        [ends, ends, *fluxes(short, 3), ends, message, message], scratch(short),
        u_ends, v_ends, m_ends, total, got_a, got_b, *near, old, lame, level, gradient, divergence,
    )
    got_a, got_b = along_x(send_a, send_b)
    final = (3, 3, ey4, lanes)
    u_inner, v_inner = call(
        functools.partial(between_kernel, mine, True), "between3", [final, final], [shape(3, 15, rows=short)],
        flux, flux_z, u_inner, v_inner, m_inner, gradient, divergence,
    )

    return tuple(call(
        functools.partial(end_kernel, sizes_x), "end", [displacement.shape, velocity.shape], [],
        u_ends, v_ends, m_ends, total, got_a, got_b, u_inner, v_inner,
    ))


def solution(mesh):
    sizes = (mesh.shape["px"], mesh.shape["py"])
    in_specs = (
        P(None, "px", "py", None),
        P(None, "px", "py", None),
        P("px", "py", None),
        P(None, None, None, "px", "py"),
        P(None, None, None, "px", "py"),
        P("px", "py"),
    )
    out_specs = (P(None, "px", "py", None), P(None, "px", "py", None))
    return jax.shard_map(
        functools.partial(shards, sizes), mesh=mesh, in_specs=in_specs, out_specs=out_specs, check_vma=False
    )
```

time: 52.6 us -> 42.2 us (0.80)
  waiting for transfers between devices: 21.5 us -> 17.1 us
  local copies, waits for them, and re-layouts: 4.12 us -> 0 us
  other arithmetic: 2.71 us -> 0 us
  starting transfers between devices: 12.7 us -> 13.8 us
    ppermute x12 -> x16, waiting for transfers between devices: 21.5 us -> 17.1 us  [swap(): return lax.ppermute(x, ('px', 'py'), swap_pairs(*mesh_sizes, along_x, odd))]
    unnamed x11 -> x0, local copies, waits for them, and re-layouts: 3.34 us -> none
    unnamed x2 -> x0, other arithmetic: 1.98 us -> none
    pallas_call x0 -> x1, Pallas kernels: none -> 1.29 us  [shards(): pl.pallas_call(functools.partial(load_kernel, len(sources)), out_shape=[p...]
    pallas_call x6 -> x16, Pallas kernels: 10.2 us -> 9.13 us  [call(): pl.pallas_call(kernel, out_shape=shapes, scratch_shapes=[pltpu.VMEM(s, F3...]
    ppermute x12 -> x16, starting transfers between devices: 12.7 us -> 13.8 us  [swap(): return lax.ppermute(x, ('px', 'py'), swap_pairs(*mesh_sizes, along_x, odd))]
    squeeze x1 -> x0, local copies, waits for them, and re-layouts: 0.74 us -> none  [shards(): rim = jnp.concatenate([layer_left, displacement[:, 0], layer_right], axis=1)]
    convert_element_type x1 -> x0, other arithmetic: 0.71 us -> none  [rows_of(): x = x.reshape(-1, lanes).astype(F32)]
  transfers between devices with their start and end apart: 12 -> 16, of which waited for: 9 -> 11; matrix products, arithmetic and copies ran while one was open for 1% -> 0% of each run, Pallas kernels for 5% -> 14%
where the time goes in v2:
time: 42.2 us; the launch traced here: 42 us
  waiting for transfers between devices  17.1 us (41%)
  starting transfers between devices  13.8 us (33%)
  Pallas kernels  10.4 us (25%)
  between operations  0.74 us (2%)
    ppermute x16, waiting for transfers between devices, swap(): return lax.ppermute(x, ('px', 'py'), swap_pairs(*mesh_sizes, along_x, odd))  17.1 us
    ppermute x16, starting transfers between devices, swap(): return lax.ppermute(x, ('px', 'py'), swap_pairs(*mesh_sizes, along_x, odd))  13.8 us
    pallas_call x16, Pallas kernels, call(): pl.pallas_call(kernel, out_shape=shapes, scratch_shapes=[pltpu.VMEM(s, F3...  9.13 us
    pallas_call x1, Pallas kernels, shards(): pl.pallas_call(functools.partial(load_kernel, len(sources)), out_shape=[p...  1.29 us
  transfers between devices with their start and end apart: 16, of which 11 were waited for; matrix products, arithmetic and copies ran while one was open for 0% of the time, Pallas kernels for 14%

profile of v2, /device:TPU:16, one launch (start us, length us, event | category | flops | bytes accessed | tf_op | source)
XLA Modules:
  0.0 42.0 jit_solution(3659861048228972510)
XLA Ops:
  0.6 1.6 %collective-permute-start.1 = (f32[192,128]{1,0:T(8,128)}, f32[192,128]{1,0:T(8,128)S(1)}, u32[]{:S(2)}, u32[]{:S(2)}) collective-permute-start(f32[192,128]{1,0:T(8,128)} %bitcast.4), channel_id=1, source_target_pairs={{0,4},{1,2},{2,1},{3,7},{4,0},{5,6},{6,5},{7,3},{8,12},{9,10},{10,... | collective-permute-start | bytes 294920 | tf_op jit(solution)/shard_map/ppermute | solution.py:122
  2.2 1.3 %load.1 = (f32[192,128]{1,0:T(8,128)S(1)}, f32[192,128]{1,0:T(8,128)S(1)}, f32[64,128]{1,0:T(8,128)S(1)}, f32[5,5,5,1,128]{4,3,2,1,0:T(1,128)S(1)}, f32[5,5,5,1,...) custom-call(f32[192,128]{1,0:T(8,128)} %bitcast.5, ...), custom_call_target="tpu_custom_call" | custom-call | tf_op jit(solution)/shard_map/load/pallas_call | solution.py:565
  4.1 1.6 %collective-permute-start.7 = (f32[264,128]{1,0:T(8,128)S(1)}, f32[264,128]{1,0:T(8,128)S(1)}, u32[]{:S(2)}, u32[]{:S(2)}) collective-permute-start(f32[264,128]{1,0:T(8,128)S(1)} %pack.1.own_ref), channel_id=1, source_target_pairs={{0,4},{1,2},{2,1},{3,7},{4,0},{5,6},{6,5},{7,3},{8,12},{9,10},{10,... | collective-permute-start | bytes 405512 | tf_op jit(solution)/shard_map/ppermute | solution.py:122
  6.2 0.9 %collective-permute-start.5 = (f32[3,48,128]{2,1,0:T(8,128)S(1)}, f32[3,48,128]{2,1,0:T(8,128)S(1)}, u32[]{:S(2)}, u32[]{:S(2)}) collective-permute-start(f32[3,48,128]{2,1,0:T(8,128)S(1)} %rim.1), channel_id=1, source_target_pairs={{0,1},{1,0},{2,3},{3,2},{4,8},{5,9},{6,10},{7,11},{8,4},{9,5},{10,... | collective-permute-start | bytes 221192 | tf_op jit(solution)/shard_map/ppermute | solution.py:122
  7.1 1.5 %collective-permute-done.3.o = f32[256,128]{1,0:T(8,128)S(1)} collective-permute-done((f32[256,128]{1,0:T(8,128)S(1)}, f32[256,128]{1,0:T(8,128)S(1)}, u32[]{:S(2)}, u32[]{:S(2)}) %collective-permute-start.3) | collective-permute-done | bytes 131104 | tf_op jit(solution)/shard_map/ppermute | solution.py:122
  8.5 0.8 %collective-permute-start.4 = (f32[3,48,128]{2,1,0:T(8,128)S(1)}, f32[3,48,128]{2,1,0:T(8,128)S(1)}, u32[]{:S(2)}, u32[]{:S(2)}) collective-permute-start(f32[3,48,128]{2,1,0:T(8,128)S(1)} %rim.1), channel_id=1, source_target_pairs={{0,4},{1,5},{2,6},{3,7},{4,0},{5,1},{6,2},{7,3},{8,12},{9,13},{10,... | collective-permute-start | bytes 221192 | tf_op jit(solution)/shard_map/ppermute | solution.py:122
  9.9 1.1 %collective-permute-done.7.o_ref = f32[264,128]{1,0:T(8,128)S(1)} collective-permute-done((f32[264,128]{1,0:T(8,128)S(1)}, f32[264,128]{1,0:T(8,128)S(1)}, u32[]{:S(2)}, u32[]{:S(2)}) %collective-permute-start.7) | collective-permute-done | bytes 135200 | tf_op jit(solution)/shard_map/ppermute | solution.py:122
  11.0 1.0 %tables.1 = (f32[2,2,25,16,128]{4,3,2,1,0:T(8,128)S(1)}, f32[2,16,128]{2,1,0:T(8,128)S(1)}) custom-call(f32[264,128]{1,0:T(8,128)S(1)} %pack.1.own_ref, f32[264,128]{1,0:T(8,128)S(1)} %collective-permute-done.6.e_ref, f32[264,128]{1,0:T(8,128)S(1)} %collective-permute-done.7.o_ref, f32[50,128]{1,0:T(8,128)S(1)} %get-tuple-element.86.weight_ref), custom_call_target="tpu_custom_call" | custom-call | tf_op jit(solution)/shard_map/tables/pallas_call | solution.py:537
  12.0 1.1 %collective-permute-done.4.a_ref = f32[3,48,128]{2,1,0:T(8,128)S(1)} collective-permute-done((f32[3,48,128]{2,1,0:T(8,128)S(1)}, f32[3,48,128]{2,1,0:T(8,128)S(1)}, u32[]{:S(2)}, u32[]{:S(2)}) %collective-permute-start.4) | collective-permute-done | bytes 73760 | tf_op jit(solution)/shard_map/ppermute | solution.py:122
  13.1 1.1 %stress0.1 = (f32[3,4,16,128]{3,2,1,0:T(8,128)S(1)}, f32[6,2,25,16,128]{4,3,2,1,0:T(8,128)S(1)}, f32[5,25,16,128]{3,2,1,0:T(8,128)S(1)}, f32[3,2,4,16,128]{4,3,2...) custom-call(f32[3,4,16,128]{3,2,1,0:T(8,128)S(1)} %get-tuple-element.72.u_ref, ...), custom_call_target="tpu_custom_call" | custom-call | tf_op jit(solution)/shard_map/stress0/pallas_call | solution.py:537
  14.3 1.2 %collective-permute-start.8 = (f32[4,40,128]{2,1,0:T(8,128)S(1)}, f32[4,40,128]{2,1,0:T(8,128)S(1)}, u32[]{:S(2)}, u32[]{:S(2)}) collective-permute-start(f32[4,40,128]{2,1,0:T(8,128)S(1)} %get-tuple-element.92), channel_id=1, source_target_pairs={{0,4},{1,5},{2,6},{3,7},{4,0},{5,1},{6,2},{7,3},{8,12},{9,13},{10,... | collective-permute-start | bytes 245768 | tf_op jit(solution)/shard_map/ppermute | solution.py:122
  15.5 0.8 %collective-permute-start.9 = (f32[4,40,128]{2,1,0:T(8,128)S(1)}, f32[4,40,128]{2,1,0:T(8,128)S(1)}, u32[]{:S(2)}, u32[]{:S(2)}) collective-permute-start(f32[4,40,128]{2,1,0:T(8,128)S(1)} %get-tuple-element.93), channel_id=1, source_target_pairs={{0,1},{1,0},{2,3},{3,2},{4,8},{5,9},{6,10},{7,11},{8,4},{9,5},{10,... | collective-permute-start | bytes 245768 | tf_op jit(solution)/shard_map/ppermute | solution.py:122
  16.2 1.1 %between0.1 = (f32[3,3,4,16,128]{4,3,2,1,0:T(8,128)S(1)}, f32[3,3,4,16,128]{4,3,2,1,0:T(8,128)S(1)}, f32[3,4,16,128]{3,2,1,0:T(8,128)S(1)}, f32[45,16,256]{2,1,0...) custom-call(f32[5,25,16,128]{3,2,1,0:T(8,128)S(1)} %get-tuple-element.94.flux, ...), custom_call_target="tpu_custom_call" | custom-call | tf_op jit(solution)/shard_map/between0/pallas_call | solution.py:537
  17.4 2.3 %collective-permute-done.8.a_ref = f32[4,40,128]{2,1,0:T(8,128)S(1)} collective-permute-done((f32[4,40,128]{2,1,0:T(8,128)S(1)}, f32[4,40,128]{2,1,0:T(8,128)S(1)}, u32[]{:S(2)}, u32[]{:S(2)}) %collective-permute-start.8) | collective-permute-done | bytes 81952 | tf_op jit(solution)/shard_map/ppermute | solution.py:122
  19.6 1.2 %collective-permute-done.9.b_ref = f32[4,40,128]{2,1,0:T(8,128)S(1)} collective-permute-done((f32[4,40,128]{2,1,0:T(8,128)S(1)}, f32[4,40,128]{2,1,0:T(8,128)S(1)}, u32[]{:S(2)}, u32[]{:S(2)}) %collective-permute-start.9) | collective-permute-done | bytes 81952 | tf_op jit(solution)/shard_map/ppermute | solution.py:122
  20.8 1.2 %stress1.1 = (f32[3,2,4,8,128]{4,3,2,1,0:T(8,128)S(1)}, f32[3,2,4,8,128]{4,3,2,1,0:T(8,128)S(1)}, f32[2,4,8,128]{3,2,1,0:T(8,128)S(1)}, f32[5,25,16,128]{3,2,1,0...) custom-call(f32[3,4,16,128]{3,2,1,0:T(8,128)S(1)} %get-tuple-element, ...), custom_call_target="tpu_custom_call" | custom-call | tf_op jit(solution)/shard_map/stress1/pallas_call | solution.py:537
  22.0 0.9 %collective-permute-start.10 = (f32[3,4,8,128]{3,2,1,0:T(8,128)S(1)}, f32[3,4,8,128]{3,2,1,0:T(8,128)S(1)}, u32[]{:S(2)}, u32[]{:S(2)}) collective-permute-start(f32[3,4,8,128]{3,2,1,0:T(8,128)S(1)} %get-tuple-element.105), channel_id=1, source_target_pairs={{0,4},{1,5},{2,6},{3,7},{4,0},{5,1},{6,2},{7,3},{8,12},{9,13},{10,... | collective-permute-start | bytes 147464 | tf_op jit(solution)/shard_map/ppermute | solution.py:122
  23.0 1.0 %collective-permute-start.11 = (f32[3,4,8,128]{3,2,1,0:T(8,128)S(1)}, f32[3,4,8,128]{3,2,1,0:T(8,128)S(1)}, u32[]{:S(2)}, u32[]{:S(2)}) collective-permute-start(f32[3,4,8,128]{3,2,1,0:T(8,128)S(1)} %get-tuple-element.106), channel_id=1, source_target_pairs={{0,1},{1,0},{2,3},{3,2},{4,8},{5,9},{6,10},{7,11},{8,4},{9,5},{10,... | collective-permute-start | bytes 147464 | tf_op jit(solution)/shard_map/ppermute | solution.py:122
  24.0 0.8 %between1.1 = (f32[3,3,4,8,128]{4,3,2,1,0:T(8,128)S(1)}, f32[3,3,4,8,128]{4,3,2,1,0:T(8,128)S(1)}, f32[3,4,8,128]{3,2,1,0:T(8,128)S(1)}, f32[45,8,256]{2,1,0:T(8...) custom-call(f32[5,25,16,128]{3,2,1,0:T(8,128)S(1)} %get-tuple-element.107.flux, ...), custom_call_target="tpu_custom_call" | custom-call | tf_op jit(solution)/shard_map/between1/pallas_call | solution.py:537
  24.9 1.3 %collective-permute-done.10.a_ref = f32[3,4,8,128]{3,2,1,0:T(8,128)S(1)} collective-permute-done((f32[3,4,8,128]{3,2,1,0:T(8,128)S(1)}, f32[3,4,8,128]{3,2,1,0:T(8,128)S(1)}, u32[]{:S(2)}, u32[]{:S(2)}) %collective-permute-start.10) | collective-permute-done | bytes 49184 | tf_op jit(solution)/shard_map/ppermute | solution.py:122
  26.2 1.8 %collective-permute-done.11.b_ref = f32[3,4,8,128]{3,2,1,0:T(8,128)S(1)} collective-permute-done((f32[3,4,8,128]{3,2,1,0:T(8,128)S(1)}, f32[3,4,8,128]{3,2,1,0:T(8,128)S(1)}, u32[]{:S(2)}, u32[]{:S(2)}) %collective-permute-start.11) | collective-permute-done | bytes 49184 | tf_op jit(solution)/shard_map/ppermute | solution.py:122
  28.0 0.7 %stress2.1 = (f32[3,2,4,8,128]{4,3,2,1,0:T(8,128)S(1)}, f32[3,2,4,8,128]{4,3,2,1,0:T(8,128)S(1)}, f32[5,25,8,128]{3,2,1,0:T(8,128)S(1)}, f32[6,2,25,8,128]{4,3,2...) custom-call(f32[3,2,4,8,128]{4,3,2,1,0:T(8,128)S(1)} %get-tuple-elem, ...), custom_call_target="tpu_custom_call" | custom-call | tf_op jit(solution)/shard_map/stress2/pallas_call | solution.py:537
  28.7 1.2 %collective-permute-start.12 = (f32[3,4,8,128]{3,2,1,0:T(8,128)S(1)}, f32[3,4,8,128]{3,2,1,0:T(8,128)S(1)}, u32[]{:S(2)}, u32[]{:S(2)}) collective-permute-start(f32[3,4,8,128]{3,2,1,0:T(8,128)S(1)} %get-tuple-element.118), channel_id=1, source_target_pairs={{0,4},{1,5},{2,6},{3,7},{4,0},{5,1},{6,2},{7,3},{8,12},{9,13},{10,... | collective-permute-start | bytes 147464 | tf_op jit(solution)/shard_map/ppermute | solution.py:122
  29.9 0.8 %collective-permute-start.13 = (f32[3,4,8,128]{3,2,1,0:T(8,128)S(1)}, f32[3,4,8,128]{3,2,1,0:T(8,128)S(1)}, u32[]{:S(2)}, u32[]{:S(2)}) collective-permute-start(f32[3,4,8,128]{3,2,1,0:T(8,128)S(1)} %get-tuple-element.119), channel_id=1, source_target_pairs={{0,1},{1,0},{2,3},{3,2},{4,8},{5,9},{6,10},{7,11},{8,4},{9,5},{10,... | collective-permute-start | bytes 147464 | tf_op jit(solution)/shard_map/ppermute | solution.py:122
  31.4 1.5 %collective-permute-done.12.a_ref = f32[3,4,8,128]{3,2,1,0:T(8,128)S(1)} collective-permute-done((f32[3,4,8,128]{3,2,1,0:T(8,128)S(1)}, f32[3,4,8,128]{3,2,1,0:T(8,128)S(1)}, u32[]{:S(2)}, u32[]{:S(2)}) %collective-permute-start.12) | collective-permute-done | bytes 49184 | tf_op jit(solution)/shard_map/ppermute | solution.py:122
  32.9 2.0 %collective-permute-done.13.b_ref = f32[3,4,8,128]{3,2,1,0:T(8,128)S(1)} collective-permute-done((f32[3,4,8,128]{3,2,1,0:T(8,128)S(1)}, f32[3,4,8,128]{3,2,1,0:T(8,128)S(1)}, u32[]{:S(2)}, u32[]{:S(2)}) %collective-permute-start.13) | collective-permute-done | bytes 49184 | tf_op jit(solution)/shard_map/ppermute | solution.py:122
  34.9 0.7 %stress3.1 = (f32[3,2,4,8,128]{4,3,2,1,0:T(8,128)S(1)}, f32[3,2,4,8,128]{4,3,2,1,0:T(8,128)S(1)}, f32[5,25,8,128]{3,2,1,0:T(8,128)S(1)}, f32[3,2,25,8,128]{4,3,2...) custom-call(f32[3,2,4,8,128]{4,3,2,1,0:T(8,128)S(1)} %get-tuple-element.11, ...), custom_call_target="tpu_custom_call" | custom-call | tf_op jit(solution)/shard_map/stress3/pallas_call | solution.py:537
  35.6 0.9 %collective-permute-start.14 = (f32[3,16,128]{2,1,0:T(8,128)S(1)}, f32[3,16,128]{2,1,0:T(8,128)S(1)}, u32[]{:S(2)}, u32[]{:S(2)}) collective-permute-start(f32[3,16,128]{2,1,0:T(8,128)S(1)} %get-tuple-element.131), channel_id=1, source_target_pairs={{0,4},{1,5},{2,6},{3,7},{4,0},{5,1},{6,2},{7,3},{8,12},{9,13},{10,... | collective-permute-start | bytes 73736 | tf_op jit(solution)/shard_map/ppermute | solution.py:122
  36.6 1.0 %collective-permute-start.15 = (f32[3,16,128]{2,1,0:T(8,128)S(1)}, f32[3,16,128]{2,1,0:T(8,128)S(1)}, u32[]{:S(2)}, u32[]{:S(2)}) collective-permute-start(f32[3,16,128]{2,1,0:T(8,128)S(1)} %get-tuple-element.132), channel_id=1, source_target_pairs={{0,1},{1,0},{2,3},{3,2},{4,8},{5,9},{6,10},{7,11},{8,4},{9,5},{10,... | collective-permute-start | bytes 73736 | tf_op jit(solution)/shard_map/ppermute | solution.py:122
  38.0 1.6 %collective-permute-done.14.a_ref = f32[3,16,128]{2,1,0:T(8,128)S(1)} collective-permute-done((f32[3,16,128]{2,1,0:T(8,128)S(1)}, f32[3,16,128]{2,1,0:T(8,128)S(1)}, u32[]{:S(2)}, u32[]{:S(2)}) %collective-permute-start.14) | collective-permute-done | bytes 24608 | tf_op jit(solution)/shard_map/ppermute | solution.py:122
  39.5 1.8 %collective-permute-done.15.b_ref = f32[3,16,128]{2,1,0:T(8,128)S(1)} collective-permute-done((f32[3,16,128]{2,1,0:T(8,128)S(1)}, f32[3,16,128]{2,1,0:T(8,128)S(1)}, u32[]{:S(2)}, u32[]{:S(2)}) %collective-permute-start.15) | collective-permute-done | bytes 24608 | tf_op jit(solution)/shard_map/ppermute | solution.py:122
  41.3 0.7 %end.1 = (f32[3,4,16,128]{3,2,1,0:T(8,128)}, f32[3,4,16,128]{3,2,1,0:T(8,128)}) custom-call(f32[3,2,4,8,128]{4,3,2,1,0:T(8,128)S(1)} %get-tuple-element.128.u_ref, f32[3,2,4,8,128]{4,3,2,1,0:T(8,128)S(1)} %get-tuple-element.129.v_ref, f32[2,4,8,128]{3,2,1,0:T(8,128)S(1)} %get-tuple-element.103.m_ref, f32[3,2,4,8,128]{4,3,2,1,0:T(8,128)S(1)} %get-tuple-element.130.total_ref, ...), custom_call_target="tpu_custom_call" | custom-call | tf_op jit(solution)/shard_map/end/pallas_call | solution.py:537
  (17 shorter events, 2.8 us)
Async XLA Ops:
  0.6 5.1 %collective-permute-start.1 = (f32[192,128]{1,0:T(8,128)}, f32[192,128]{1,0:T(8,128)S(1)}, u32[]{:S(2)}, u32[]{:S(2)}) collective-permute-start(f32[192,128]{1,0:T(8,128)} %bitcast.4), channel_id=1, source_target_pairs={{0,4},{1,2},{2,1},{3,7},{4,0},{5,6},{6,5},{7,3},{8,12},{9,10},{10,... | collective-permute-start | bytes 294920 | tf_op jit(solution)/shard_map/ppermute | solution.py:122
  3.5 5.0 %collective-permute-start.3 = (f32[256,128]{1,0:T(8,128)S(1)}, f32[256,128]{1,0:T(8,128)S(1)}, u32[]{:S(2)}, u32[]{:S(2)}) collective-permute-start(f32[256,128]{1,0:T(8,128)S(1)} %join.1), channel_id=1, source_target_pairs={{0,4},{1,2},{2,1},{3,7},{4,0},{5,6},{6,5},{7,3},{8,12},{9,10},{10,... | collective-permute-start | bytes 393224 | tf_op jit(solution)/shard_map/ppermute | solution.py:122
  4.1 2.1 %collective-permute-start = (f32[192,128]{1,0:T(8,128)}, f32[192,128]{1,0:T(8,128)S(1)}, u32[]{:S(2)}, u32[]{:S(2)}) collective-permute-start(f32[192,128]{1,0:T(8,128)} %bitcast.6), channel_id=1, source_target_pairs={{0,1},{1,0},{2,3},{3,2},{4,5},{5,4},{6,7},{7,6},{8,9},{9,8},{10,11... | collective-permute-start | bytes 294920 | tf_op jit(solution)/shard_map/ppermute | solution.py:122
  4.1 6.9 %collective-permute-start.7 = (f32[264,128]{1,0:T(8,128)S(1)}, f32[264,128]{1,0:T(8,128)S(1)}, u32[]{:S(2)}, u32[]{:S(2)}) collective-permute-start(f32[264,128]{1,0:T(8,128)S(1)} %pack.1.own_ref), channel_id=1, source_target_pairs={{0,4},{1,2},{2,1},{3,7},{4,0},{5,6},{6,5},{7,3},{8,12},{9,10},{10,... | collective-permute-start | bytes 405512 | tf_op jit(solution)/shard_map/ppermute | solution.py:122
  5.7 5.3 %collective-permute-start.6 = (f32[264,128]{1,0:T(8,128)S(1)}, f32[264,128]{1,0:T(8,128)S(1)}, u32[]{:S(2)}, u32[]{:S(2)}) collective-permute-start(f32[264,128]{1,0:T(8,128)S(1)} %pack.1.own_ref), channel_id=1, source_target_pairs={{0,1},{1,0},{2,3},{3,2},{4,5},{5,4},{6,7},{7,6},{8,9},{9,8},{10,11... | collective-permute-start | bytes 405512 | tf_op jit(solution)/shard_map/ppermute | solution.py:122
  5.7 4.1 %collective-permute-start.2 = (f32[256,128]{1,0:T(8,128)S(1)}, f32[256,128]{1,0:T(8,128)S(1)}, u32[]{:S(2)}, u32[]{:S(2)}) collective-permute-start(f32[256,128]{1,0:T(8,128)S(1)} %join.1), channel_id=1, source_target_pairs={{0,1},{1,0},{2,3},{3,2},{4,5},{5,4},{6,7},{7,6},{8,9},{9,8},{10,11... | collective-permute-start | bytes 393224 | tf_op jit(solution)/shard_map/ppermute | solution.py:122
  6.2 5.8 %collective-permute-start.5 = (f32[3,48,128]{2,1,0:T(8,128)S(1)}, f32[3,48,128]{2,1,0:T(8,128)S(1)}, u32[]{:S(2)}, u32[]{:S(2)}) collective-permute-start(f32[3,48,128]{2,1,0:T(8,128)S(1)} %rim.1), channel_id=1, source_target_pairs={{0,1},{1,0},{2,3},{3,2},{4,8},{5,9},{6,10},{7,11},{8,4},{9,5},{10,... | collective-permute-start | bytes 221192 | tf_op jit(solution)/shard_map/ppermute | solution.py:122
  8.5 4.6 %collective-permute-start.4 = (f32[3,48,128]{2,1,0:T(8,128)S(1)}, f32[3,48,128]{2,1,0:T(8,128)S(1)}, u32[]{:S(2)}, u32[]{:S(2)}) collective-permute-start(f32[3,48,128]{2,1,0:T(8,128)S(1)} %rim.1), channel_id=1, source_target_pairs={{0,4},{1,5},{2,6},{3,7},{4,0},{5,1},{6,2},{7,3},{8,12},{9,13},{10,... | collective-permute-start | bytes 221192 | tf_op jit(solution)/shard_map/ppermute | solution.py:122
  14.3 5.4 %collective-permute-start.8 = (f32[4,40,128]{2,1,0:T(8,128)S(1)}, f32[4,40,128]{2,1,0:T(8,128)S(1)}, u32[]{:S(2)}, u32[]{:S(2)}) collective-permute-start(f32[4,40,128]{2,1,0:T(8,128)S(1)} %get-tuple-element.92), channel_id=1, source_target_pairs={{0,4},{1,5},{2,6},{3,7},{4,0},{5,1},{6,2},{7,3},{8,12},{9,13},{10,... | collective-permute-start | bytes 245768 | tf_op jit(solution)/shard_map/ppermute | solution.py:122
  15.5 5.3 %collective-permute-start.9 = (f32[4,40,128]{2,1,0:T(8,128)S(1)}, f32[4,40,128]{2,1,0:T(8,128)S(1)}, u32[]{:S(2)}, u32[]{:S(2)}) collective-permute-start(f32[4,40,128]{2,1,0:T(8,128)S(1)} %get-tuple-element.93), channel_id=1, source_target_pairs={{0,1},{1,0},{2,3},{3,2},{4,8},{5,9},{6,10},{7,11},{8,4},{9,5},{10,... | collective-permute-start | bytes 245768 | tf_op jit(solution)/shard_map/ppermute | solution.py:122
  22.0 4.2 %collective-permute-start.10 = (f32[3,4,8,128]{3,2,1,0:T(8,128)S(1)}, f32[3,4,8,128]{3,2,1,0:T(8,128)S(1)}, u32[]{:S(2)}, u32[]{:S(2)}) collective-permute-start(f32[3,4,8,128]{3,2,1,0:T(8,128)S(1)} %get-tuple-element.105), channel_id=1, source_target_pairs={{0,4},{1,5},{2,6},{3,7},{4,0},{5,1},{6,2},{7,3},{8,12},{9,13},{10,... | collective-permute-start | bytes 147464 | tf_op jit(solution)/shard_map/ppermute | solution.py:122
  23.0 5.0 %collective-permute-start.11 = (f32[3,4,8,128]{3,2,1,0:T(8,128)S(1)}, f32[3,4,8,128]{3,2,1,0:T(8,128)S(1)}, u32[]{:S(2)}, u32[]{:S(2)}) collective-permute-start(f32[3,4,8,128]{3,2,1,0:T(8,128)S(1)} %get-tuple-element.106), channel_id=1, source_target_pairs={{0,1},{1,0},{2,3},{3,2},{4,8},{5,9},{6,10},{7,11},{8,4},{9,5},{10,... | collective-permute-start | bytes 147464 | tf_op jit(solution)/shard_map/ppermute | solution.py:122
  28.7 4.2 %collective-permute-start.12 = (f32[3,4,8,128]{3,2,1,0:T(8,128)S(1)}, f32[3,4,8,128]{3,2,1,0:T(8,128)S(1)}, u32[]{:S(2)}, u32[]{:S(2)}) collective-permute-start(f32[3,4,8,128]{3,2,1,0:T(8,128)S(1)} %get-tuple-element.118), channel_id=1, source_target_pairs={{0,4},{1,5},{2,6},{3,7},{4,0},{5,1},{6,2},{7,3},{8,12},{9,13},{10,... | collective-permute-start | bytes 147464 | tf_op jit(solution)/shard_map/ppermute | solution.py:122
  29.9 5.0 %collective-permute-start.13 = (f32[3,4,8,128]{3,2,1,0:T(8,128)S(1)}, f32[3,4,8,128]{3,2,1,0:T(8,128)S(1)}, u32[]{:S(2)}, u32[]{:S(2)}) collective-permute-start(f32[3,4,8,128]{3,2,1,0:T(8,128)S(1)} %get-tuple-element.119), channel_id=1, source_target_pairs={{0,1},{1,0},{2,3},{3,2},{4,8},{5,9},{6,10},{7,11},{8,4},{9,5},{10,... | collective-permute-start | bytes 147464 | tf_op jit(solution)/shard_map/ppermute | solution.py:122
  35.6 3.9 %collective-permute-start.14 = (f32[3,16,128]{2,1,0:T(8,128)S(1)}, f32[3,16,128]{2,1,0:T(8,128)S(1)}, u32[]{:S(2)}, u32[]{:S(2)}) collective-permute-start(f32[3,16,128]{2,1,0:T(8,128)S(1)} %get-tuple-element.131), channel_id=1, source_target_pairs={{0,4},{1,5},{2,6},{3,7},{4,0},{5,1},{6,2},{7,3},{8,12},{9,13},{10,... | collective-permute-start | bytes 73736 | tf_op jit(solution)/shard_map/ppermute | solution.py:122
  36.6 4.7 %collective-permute-start.15 = (f32[3,16,128]{2,1,0:T(8,128)S(1)}, f32[3,16,128]{2,1,0:T(8,128)S(1)}, u32[]{:S(2)}, u32[]{:S(2)}) collective-permute-start(f32[3,16,128]{2,1,0:T(8,128)S(1)} %get-tuple-element.132), channel_id=1, source_target_pairs={{0,1},{1,0},{2,3},{3,2},{4,8},{5,9},{6,10},{7,11},{8,4},{9,5},{10,... | collective-permute-start | bytes 73736 | tf_op jit(solution)/shard_map/ppermute | solution.py:122

commit v3 on v2

v3 whole, which is shorter than its diff:
```python
import functools

import jax
import jax.numpy as jnp
import numpy as np
from jax import lax
from jax.experimental import pallas as pl
from jax.experimental.pallas import tpu as pltpu
from jax.sharding import PartitionSpec as P

time_step = 0.1
LEVELS = 3
F32 = jnp.float32
BF16 = jnp.bfloat16


def gll_tables():
    points = np.array([-1.0, -np.sqrt(3.0 / 7.0), 0.0, np.sqrt(3.0 / 7.0), 1.0])
    weights = np.array([0.1, 49.0 / 90.0, 32.0 / 45.0, 49.0 / 90.0, 0.1])
    legendre = (35.0 * points**4 - 30.0 * points**2 + 3.0) / 8.0
    derivative = np.zeros((5, 5))
    for row_index in range(5):
        for col_index in range(5):
            if row_index != col_index:
                derivative[row_index, col_index] = legendre[row_index] / (
                    legendre[col_index] * (points[row_index] - points[col_index])
                )
    derivative[0, 0] = -5.0
    derivative[4, 4] = 5.0
    return (derivative, weights)


D, W = gll_tables()


def split(table):
    high = np.asarray(table, np.float32).astype(BF16)
    low = (np.asarray(table, np.float64) - high.astype(np.float64)).astype(BF16)
    return high, low


def depth_tables(depth):
    lanes = 4 * depth
    table = np.zeros((lanes, 2 * lanes))
    for c in range(depth):
        for i in range(5):
            if 4 * c + i < lanes:
                for k in range(4):
                    table[4 * c + i, 4 * c + k] = D[k, i]
                table[4 * c + i, lanes + (4 * (c + 1)) % lanes] = D[4, i]
    high, low = split(table)
    gradient = np.concatenate([high, high, low], axis=0)
    divergence = np.concatenate([high.T, high.T, low.T], axis=0)
    return gradient, divergence


def weight_table(depth):
    lanes = 4 * depth
    pair = (W[:, None] * W[None, :]).reshape(25, 1)
    main = pair * np.tile(W[:4], depth)[None, :]
    last = pair * np.where(np.arange(lanes) % 4 == 0, W[4], 0.0)[None, :]
    return np.concatenate([main, last], axis=0).astype(np.float32)


def apply5(matrix, x):
    s0, s1 = x[0] + x[4], x[1] + x[3]
    d0, d1 = x[0] - x[4], x[1] - x[3]

    def even(a):
        p, q = (matrix[a, 0] - matrix[a, 4]) / 2, (matrix[a, 1] - matrix[a, 3]) / 2
        return d0 * float(p) + d1 * float(q)

    def odd(a):
        p, q = (matrix[a, 0] + matrix[a, 4]) / 2, (matrix[a, 1] + matrix[a, 3]) / 2
        return s0 * float(p) + s1 * float(q) + x[2] * float(matrix[a, 2])

    e0, e1, e2 = even(0), even(1), even(2)
    o0, o1 = odd(0), odd(1)
    return [e0 + o0, e1 + o1, e2, e1 - o1, e0 - o0]


def apply5_middle(matrix, x):
    s1, d1 = x[0] + x[2], x[0] - x[2]
    e = [d1 * float((matrix[a, 1] - matrix[a, 3]) / 2) for a in range(3)]
    o = [s1 * float((matrix[a, 1] + matrix[a, 3]) / 2) + x[1] * float(matrix[a, 2]) for a in range(2)]
    return [e[0] + o[0], e[1] + o[1], e[2], e[1] - o[1], e[0] - o[0]]


def apply5_ends(matrix, first, last, middle):
    s0, d0 = first + last, first - last
    e = [d0 * float((matrix[a, 0] - matrix[a, 4]) / 2) for a in range(3)]
    o = [s0 * float((matrix[a, 0] + matrix[a, 4]) / 2) for a in range(2)]
    ends = [e[0] + o[0], e[1] + o[1], e[2], e[1] - o[1], e[0] - o[0]]
    return [middle[a] + ends[a] for a in range(5)]


def halves(x):
    high = x.astype(BF16)
    return high, (x - high.astype(F32)).astype(BF16)


def rolled(x, by):
    return pltpu.roll(x, by % x.shape[0], 0)


def pairs_of(kind, nx, ny):
    pairs = []
    for i in range(nx):
        for j in range(ny):
            if kind == "core":
                target = (i, j ^ 1)
            elif kind == "near":
                target = (i ^ 1, j ^ 1)
            elif kind == "home":
                target = (i ^ 1, j)
            elif kind == "far":
                there = i + 1 if i % 2 else i - 1
                target = (there if 0 <= there < nx else i, j ^ 1)
            elif i % 2:
                there = j + 2 if j % 2 else j - 2
                target = (i, there if 0 <= there < ny else j ^ 1)
            else:
                there = j + 1 if j % 2 else j - 1
                target = (i, there) if 0 <= there < ny else (i ^ 2, j) if nx % 4 == 0 else (i, ny - 1 - j)
            pairs.append((i * ny + j, target[0] * ny + target[1]))
    return pairs


def place(axis, size):
    here = lax.axis_index(axis)
    return lax.rem(here, 2) == 0, here == 0, here == size - 1


def load_kernel(count, *refs):
    sources, targets, sems = refs[:count], refs[count : 2 * count], refs[2 * count]
    copies = [pltpu.make_async_copy(a, b, sems.at[n]) for n, (a, b) in enumerate(zip(sources, targets))]
    for copy in copies:
        copy.start()
    for copy in copies:
        copy.wait()


def pack_kernel(starts, v_ref, m_ref, first_ref, second_ref, level_ref, out):
    out[0 : v_ref.shape[0], :] = v_ref[...]
    out[starts[0] : starts[0] + m_ref.shape[0], :] = m_ref[...]
    for p, table in enumerate((first_ref, second_ref)):
        for row in range(125):
            i, j, k = row // 25, row // 5 % 5, row % 5
            out[starts[1 + p] + row : starts[1 + p] + row + 1, :] = table[i, j, k]
    out[starts[3] : starts[3] + 1, :] = level_ref[...].astype(F32)


def sides(ny):
    here = lax.axis_index("py")
    changed = lax.rem(lax.axis_index("px"), 2) == 1
    even = (lax.rem(here, 2) == 0) != changed
    first = jnp.logical_and(here < 2, even)
    last = jnp.logical_and(here >= ny - 2, jnp.logical_not(even))

    def centre(own, core, chip, at):
        return jnp.where(changed, core[at], own[at])

    def other(own, core, at):
        return jnp.where(changed, own[at], core[at])

    def left(own, core, chip, at):
        return jnp.where(first, 0.0, jnp.where(even, chip[at], other(own, core, at)))

    def right(own, core, chip, at):
        return jnp.where(last, 0.0, jnp.where(even, other(own, core, at), chip[at]))

    return left, centre, right


def rim_kernel(ny, across, own, core, chip, out):
    ahead = across - 3
    for c in range(3):
        base = c * (2 * across + ahead)
        for n, (side, count) in enumerate(zip(sides(ny), (across, across, ahead))):
            at = (slice(4 * c * across, 4 * c * across + count), slice(None))
            out[base + n * across : base + n * across + count, :] = side(own, core, chip, at)


def spread(sizes, own, core, chip, base, out):
    ny, ey, lanes = sizes
    for j in range(4):
        at = (pl.ds(base + j, ey, stride=4), slice(None))
        for n, side in enumerate(sides(ny)):
            out[j, n * ey : (n + 1) * ey, :] = side(own, core, chip, at)
        out[j, 3 * ey :, :] = jnp.zeros((ey, lanes), F32)


def segments(low, high):
    found, offset = [], 0
    for j in range(4):
        stop = high + (j == 0)
        found.append((offset, slice(low, stop)))
        offset += stop - low
    return found, offset


def message_rows(low, high, fields):
    return -(-segments(low, high)[1] * fields // 8) * 8


def write_message(ref, low, high, field, rows_of):
    found, total = segments(low, high)
    for j, (offset, rows) in enumerate(found):
        start = field * total + offset
        ref[start : start + rows.stop - rows.start, :] = rows_of(j, rows)


def read_message(out, low, high, field, one_ref, other_ref, even, none):
    found, total = segments(low, high)
    for j, (offset, rows) in enumerate(found):
        at = (slice(field * total + offset, field * total + offset + rows.stop - rows.start), slice(None))
        out[j, rows, :] = jnp.where(none, 0.0, jnp.where(even, one_ref[at], other_ref[at]))


def spread_u_kernel(sizes, own, e, o, ends, inner):
    tall = 4 * sizes[1]
    for c in range(3):
        spread(sizes, own, e, o, 4 * c * tall, ends.at[c])
        for i in range(3):
            spread(sizes, own, e, o, (4 * c + 1 + i) * tall, inner.at[c, i])


def spread_v_kernel(sizes, start, own, e, o, v_ends, v_inner, m_ends, m_inner):
    tall = 4 * sizes[1]
    for c in range(3):
        spread(sizes, own, e, o, 4 * c * tall, v_ends.at[c])
        for i in range(3):
            spread(sizes, own, e, o, (4 * c + 1 + i) * tall, v_inner.at[c, i])
    spread(sizes, own, e, o, start, m_ends)
    for i in range(3):
        spread(sizes, own, e, o, start + (1 + i) * tall, m_inner.at[i])


def tables_kernel(sizes, starts, own_ref, e_ref, o_ref, weight_ref, lame_ref, level_ref, sel):
    ny, ey, lanes = sizes
    for n, side in enumerate(sides(ny)):
        sel[n] = side(own_ref, e_ref, o_ref, (slice(starts[1], own_ref.shape[0]), slice(None)))

    shape = (2 * ey, lanes)
    sub = lax.broadcasted_iota(jnp.int32, shape, 0)
    lane = lax.broadcasted_iota(jnp.int32, shape, 1)
    ez = lanes // 4
    column = lax.rem(sub, ey) * ez
    main_at = column + lane // 4
    last_at = column + lax.rem(lane // 4 + ez - 1, ez)
    point = lax.rem(lane, 4)
    upper = sub < ey

    def both(row):
        zero = jnp.zeros(shape, F32)
        a = jnp.broadcast_to(sel[0, pl.ds(row, 1), :], shape)
        b = jnp.broadcast_to(sel[1, pl.ds(row, 1), :], shape)
        c = jnp.broadcast_to(sel[2, pl.ds(row, 1), :], shape)
        return jnp.where(upper, a, b), jnp.where(upper, c, zero)

    def gather(x, at):
        return jnp.take_along_axis(x, at, axis=1, mode="promise_in_bounds")

    for ij in range(25):
        weight = jnp.broadcast_to(weight_ref[ij : ij + 1, :], shape)
        weight_last = jnp.broadcast_to(weight_ref[25 + ij : 26 + ij, :], shape)
        for p in range(2):
            points = [both(starts[1 + p] - starts[1] + ij * 5 + k) for k in range(5)]
            for h in range(2):
                got = [gather(points[k][h], main_at) for k in range(4)]
                main = jnp.where(
                    point < 2, jnp.where(point == 0, got[0], got[1]), jnp.where(point == 2, got[2], got[3])
                )
                lame_ref[p, 0, ij, 2 * ey * h : 2 * ey * (h + 1), :] = main * weight
                lame_ref[p, 1, ij, 2 * ey * h : 2 * ey * (h + 1), :] = gather(points[4][h], last_at) * weight_last
    levels = both(starts[3] - starts[1])
    for h in range(2):
        level_ref[0, 2 * ey * h : 2 * ey * (h + 1), :] = gather(levels[h], main_at)
        level_ref[1, 2 * ey * h : 2 * ey * (h + 1), :] = gather(levels[h], last_at)


def five(values):
    return list(values) + [rolled(values[0], -1)]


def grad_z(points, grad_ref, out):
    count, tall, lanes = points.shape
    high, low = halves(points[...].reshape(count * tall, lanes))
    lhs = jnp.concatenate([high, low, high], axis=1)
    out[...] = jnp.dot(lhs, grad_ref[...], preferred_element_type=F32).reshape(count, tall, 2 * lanes)


def div_z(flux_z, div_ref, out):
    _, _, count, tall, lanes = flux_z.shape
    parts = [halves(flux_z[:, e].reshape(3 * count * tall, lanes)) for e in range(2)]
    lhs = jnp.concatenate([parts[0][0], parts[1][0], parts[0][1], parts[1][1], parts[0][0], parts[1][0]], axis=1)
    out[...] = jnp.dot(lhs, div_ref[...], preferred_element_type=F32).reshape(out.shape)


def inside(lanes):
    return (lax.broadcasted_iota(jnp.int32, (8, lanes), 1) > 0).astype(F32)


def stress_of(first, second, x, y, z):
    trace = first * (x[0] + y[1] + z[2])
    twice = second + second
    return [
        trace + twice * x[0],
        trace + twice * y[1],
        second * (y[0] + x[1]),
        second * (z[0] + x[2]),
        second * (z[1] + y[2]),
        trace + twice * z[2],
    ]


def before(inner, tall, window, keep, lame, level, old, old_window, grad_ref, gz, gy, px, part, scale, us):
    lanes = gy.shape[-1]
    for c in range(3):
        points = [five(inner[c][i]) for i in range(3)]
        for i in range(3):
            for j in range(5):
                us[15 * c + 5 * i + j] = points[i][j]
        for i in range(3):
            y = apply5(D, points[i])
            for j in range(5):
                gy[c, 5 * i + j] = y[j]
        for j in range(5):
            y = apply5_middle(D, [points[i][j] for i in range(3)])
            for i in range(5):
                px[c, 5 * i + j] = y[i]
    grad_z(us, grad_ref, gz)
    mask = inside(lanes)
    for h in range(tall // 8):
        at = slice(8 * h, 8 * h + 8)
        table = slice(window + 8 * h, window + 8 * h + 8)
        stored = slice(old_window + 8 * h, old_window + 8 * h + 8)
        if keep is not None:
            fresh = [keep(level[e, table, :]) for e in range(2)]
        for p in range(15):
            y = [gy[c, p, at, :] for c in range(3)]
            sums = []
            for e in range(2):
                span = slice(e * lanes, (e + 1) * lanes)
                z0, z2 = gz[p, at, span], gz[30 + p, at, span]
                first, second = lame[0, e, 5 + p, table, :], lame[1, e, 5 + p, table, :]
                parts = [first * (y[1] + z2), second * y[0], second * z0]
                scales = [first + (second + second), second]
                if keep is not None:
                    parts = [jnp.where(fresh[e], parts[n], old[(0, 2, 3)[n], e, p, stored, :]) for n in range(3)]
                    scales = [jnp.where(fresh[e], x, 0.0) for x in scales]
                both = parts + scales
                sums.append([x * mask for x in both] if e == 1 else both)
            for n in range(3):
                part[n, p, at, :] = sums[0][n] + sums[1][n]
            for n in range(2):
                scale[n, p, at, :] = sums[0][3 + n] + sums[1][3 + n]


def stresses(tall, windows, keep, ends, px, part, scale, lame, level, old, new, flux_x, gx, flux_z, flux_y, us, gz_ends, qz, grad_ref, div_ref, total):
    lanes = px.shape[-1]
    points = [[five(ends[c][side]) for side in range(2)] for c in range(3)]
    for c in range(3):
        for side in range(2):
            for j in range(5):
                us[10 * c + 5 * side + j] = points[c][side][j]
    grad_z(us, grad_ref, gz_ends)
    for c in range(3):
        for j in range(5):
            y = apply5_ends(D, points[c][0][j], points[c][1][j], [px[c, 5 * i + j] for i in range(5)])
            for i in range(5):
                gx[c, 5 * i + j] = y[i]
                if 0 < i < 4:
                    flux_x[c, 5 * i + j] = scale[min(c, 1), 5 * i + j - 5] * y[i] + part[c, 5 * i + j - 5]
    mask = inside(lanes)
    for h in range(tall // 8):
        at = slice(8 * h, 8 * h + 8)
        table = slice(windows[0] + 8 * h, windows[0] + 8 * h + 8)
        stored = slice(windows[1] + 8 * h, windows[1] + 8 * h + 8)
        if keep is not None:
            fresh = [keep(level[e, table, :]) for e in range(2)]
        for side in range(2):
            ends_y = [apply5(D, [us[10 * c + 5 * side + j, at, :] for j in range(5)]) for c in range(3)]
            for j in range(5):
                p, q = 20 * side + j, 5 * side + j
                x = [gx[c, p, at, :] for c in range(3)]
                y = [ends_y[c][j] for c in range(3)]
                sums = []
                for e in range(2):
                    span = slice(e * lanes, (e + 1) * lanes)
                    z = [gz_ends[10 * c + q, at, span] for c in range(3)]
                    if e == 1:
                        x, y = [g * mask for g in x], [g * mask for g in y]
                    stress = stress_of(lame[0, e, p, table, :], lame[1, e, p, table, :], x, y, z)
                    if keep is not None:
                        stress = [jnp.where(fresh[e], stress[n], old[n, e, q, stored, :]) for n in range(6)]
                    if new is not None:
                        for n in range(6):
                            new[n, e, q, at, :] = stress[n]
                    else:
                        for n in range(3):
                            flux_z[n, e, q, at, :] = stress[3 + n]
                    sums.append([v * mask for v in stress[:5]] if e == 1 else stress[:5])
                xx, yy, xy, xz, yz = [sums[0][n] + sums[1][n] for n in range(5)]
                for c in range(3):
                    flux_x[c, p, at, :] = (xx, xy, xz)[c]
                    flux_y[c, q, at, :] = (xy, yy, yz)[c]
    if new is not None:
        flux_z = new.at[3:6]
    div_z(flux_z, div_ref, qz)
    assemble((0, 4), flux_x, flux_y, qz, lambda c, side, j, value: total.__setitem__((c, side, j), value))


def assemble(layers, flux_x, flux_y, qz, put):
    for c in range(3):
        pieces = []
        for j in range(5):
            x = apply5(D.T, [flux_x[c, 5 * i + j] for i in range(5)])
            pieces.append([x[i] for i in layers])
        for n in range(len(layers)):
            y = apply5(D.T, [flux_y[c, 5 * n + j] for j in range(5)])
            z = [pieces[j][n] + (y[j] + qz[c, 5 * n + j]) for j in range(5)]
            put(c, n, 0, z[0] + rolled(z[4], 1))
            for j in range(1, 4):
                put(c, n, j, z[j])


def first_kernel(u_inner, lame, grad_ref, gz, gy, px, part, scale, us):
    tall = u_inner.shape[3]
    inner = [[[u_inner[c, i, j] for j in range(4)] for i in range(3)] for c in range(3)]
    before(inner, tall, 0, None, lame, None, None, 0, grad_ref, gz, gy, px, part, scale, us)


def between_kernel(rows, last, keep, windows, stores, keep_next, windows_next, flux_x, gx, gz, gy, u_ref, v_ref, m_ref, old,
                   lame, level, grad_ref, div_ref, *refs):
    refs = list(refs)
    new = None
    if last:
        u_ends, v_ends, m_ends, total, send = refs[:5]
        count = rows.stop - rows.start
        for j in range(4):
            mass = m_ends[0, j, rows, :]
            send[pl.ds(final_rows(count, 4, 0) + j, count, stride=4), :] = mass
            for c in range(3):
                speed = v_ends[c, 0, j, rows, :] - time_step * mass * total[c, 0, j, rows, :]
                send[pl.ds(final_rows(count, 2, c) + j, count, stride=4), :] = u_ends[c, 0, j, rows, :]
                send[pl.ds(final_rows(count, 3, c) + j, count, stride=4), :] = speed
    else:
        u_out, v_out = refs[:2]
        m_out, gz_out, gy_out, px_out, part, scale = refs[2:8]
    if stores:
        new = refs[8]
    flux_y, flux_z, qz = refs[-4:-1] if not last else refs[-3:]
    us = None if last else refs[-1]
    _, _, tall, lanes = gx.shape
    mask = inside(lanes)
    for h in range(tall // 8):
        at = slice(8 * h, 8 * h + 8)
        table = slice(windows[0] + 8 * h, windows[0] + 8 * h + 8)
        stored = slice(windows[1] + 8 * h, windows[1] + 8 * h + 8)
        if keep is not None:
            fresh = [keep(level[e, table, :]) for e in range(2)]
        for p in range(15):
            x = [gx[c, 5 + p, at, :] for c in range(3)]
            y = [gy[c, p, at, :] for c in range(3)]
            sums = []
            for e in range(2):
                z = [gz[15 * c + p, at, e * lanes : (e + 1) * lanes] for c in range(3)]
                if e == 1:
                    x, y = [g * mask for g in x], [g * mask for g in y]
                stress = stress_of(lame[0, e, 5 + p, table, :], lame[1, e, 5 + p, table, :], x, y, z)
                if keep is not None:
                    stress = [jnp.where(fresh[e], stress[n], old[n, e, p, stored, :]) for n in range(6)]
                if stores:
                    for n in range(6):
                        new[n, e, p, at, :] = stress[n]
                else:
                    for n in range(3):
                        flux_z[n, e, p, at, :] = stress[3 + n]
                sums.append([v * mask for v in stress[:5]] if e == 1 else stress[:5])
            for c, n in enumerate((2, 1, 4)):
                flux_y[c, p, at, :] = sums[0][n] + sums[1][n]
    div_z(new.at[3:6] if stores else flux_z, div_ref, qz)
    inner = [[[None] * 4 for _ in range(3)] for _ in range(3)]

    def put(c, n, j, force):
        mass = m_ref[n, j, rows, :]
        speed = v_ref[c, n, j, rows, :] - time_step * mass * force[rows]
        position = u_ref[c, n, j, rows, :] + time_step * speed
        if last:
            send[pl.ds(final_rows(count, 0, c, n) + j, count, stride=4), :] = position
            send[pl.ds(final_rows(count, 1, c, n) + j, count, stride=4), :] = speed
            return
        u_out[c, n, j], v_out[c, n, j] = position, speed
        if c == 0:
            m_out[n, j] = mass
        inner[c][n][j] = position

    assemble((1, 2, 3), flux_x, flux_y, qz, put)
    if not last:
        before(inner, rows.stop - rows.start, windows_next[0], keep_next, lame, level, new if stores else old, windows_next[1],
               grad_ref, gz_out, gy_out, px_out, part, scale, us)


def newest(level_of):
    return level_of > LEVELS - 1.5


def newer(level_of):
    return level_of > LEVELS - 2.5


def start_kernel(sizes, u_ref, v_ref, m_ref, a_ref, b_ref, px, part, scale, lame, level, grad_ref, div_ref,
                 rim_ref, new, flux_x, gx, total, send_a, send_b, flux_y, us, gz_ends, qz):
    nx, ey, lanes = sizes
    even, _, last = place("px", nx)
    tall = 4 * ey
    rim_ref[...] = jnp.zeros(rim_ref.shape, F32)
    for c in range(3):
        for j in range(4):
            count = 3 * ey - (j > 0)
            at = (pl.ds(c * (12 * ey - 3) + j, count, stride=4), slice(None))
            rim_ref[c, j, 0:count, :] = jnp.where(last, 0.0, jnp.where(even, a_ref[at], b_ref[at]))
    ends = [[[u_ref[c, j] for j in range(4)], [rim_ref[c, j] for j in range(4)]] for c in range(3)]
    stresses(tall, (0, 0), None, ends, px, part, scale, lame, level, None, new, flux_x, gx, None, flux_y, us, gz_ends, qz,
             grad_ref, div_ref, total)
    low, high = 1, 3 * ey - 2
    for c in range(3):

        def back(j, rows):
            return v_ref[c, j, rows, :] - time_step * m_ref[j, rows, :] * total[c, 0, j, rows, :]

        def ahead(j, rows):
            return total[c, 1, j, rows, :]

        write_message(send_a, low, high, c, lambda j, rows: jnp.where(even, ahead(j, rows), back(j, rows)))
        write_message(send_b, low, high, c, lambda j, rows: jnp.where(even, back(j, rows), ahead(j, rows)))
    for send in (send_a, send_b):
        write_message(send, low, high, 3, lambda j, rows: m_ref[j, rows, :])


def second_kernel(sizes, u_ref, rim_ref, v_ref, m_ref, total_ref, a_ref, b_ref, px, part, scale, old, lame, level, grad_ref, div_ref,
                  u_out, v_out, m_out, flux_x, gx, total_out, send_a, send_b, got, flux_z, total, flux_y, us, gz_ends, qz):
    nx, ey, lanes = sizes
    even, first, last = place("px", nx)
    tall = 4 * ey
    window = slice(ey - 2, 3 * ey - 2)
    got[...] = jnp.zeros(got.shape, F32)
    for c in range(4):
        read_message(got.at[0, c], 1, 3 * ey - 2, c, a_ref, b_ref, even, last)
    for c in range(3):
        read_message(got.at[1, c], 1, 3 * ey - 2, c, b_ref, a_ref, even, first)
    ends = [[[], []] for _ in range(3)]
    for c in range(3):
        for side in range(2):
            for j in range(4):
                if side == 0:
                    mass, speed, position = m_ref[j], v_ref[c, j], u_ref[c, j]
                    force = total_ref[c, 0, j] + got[1, c, j]
                else:
                    mass, speed, position = got[0, 3, j], got[0, c, j], rim_ref[c, j]
                    force = total_ref[c, 1, j]
                speed = speed - time_step * mass * force
                position = position + time_step * speed
                u_out[c, side, j], v_out[c, side, j] = position[window], speed[window]
                if c == 0:
                    m_out[side, j] = mass[window]
                ends[c][side].append(position)
    stresses(tall, (0, 0), newest, ends, px, part, scale, lame, level, old, None, flux_x, gx, flux_z, flux_y, us, gz_ends, qz,
             grad_ref, div_ref, total)
    for c in range(3):
        for side in range(2):
            for j in range(4):
                total_out[c, side, j] = total[c, side, j, window, :]
    send_faces(even, total_out, 0, 2 * ey - 1, send_a, send_b)


def send_faces(even, total, low, high, send_a, send_b):
    for c in range(3):

        def back(j, rows):
            return total[c, 0, j, rows, :]

        def ahead(j, rows):
            return total[c, 1, j, rows, :]

        write_message(send_a, low, high, c, lambda j, rows: jnp.where(even, ahead(j, rows), back(j, rows)))
        write_message(send_b, low, high, c, lambda j, rows: jnp.where(even, back(j, rows), ahead(j, rows)))


def later_kernel(sizes, final, u_ref, v_ref, m_ref, total_ref, a_ref, b_ref, px, part, scale, old, lame, level, grad_ref, div_ref, *refs):
    nx, ey, lanes = sizes
    if final:
        u_out, v_out, flux_x, gx, total, send_a, send_b, got, flux_z, flux_y, us, gz_ends, qz = refs
        new, keep, windows, low, high = None, newest, (ey - 2, 0), 1, 2 + ey
    else:
        u_out, v_out, new, flux_x, gx, total, send_a, send_b, got, flux_y, us, gz_ends, qz = refs
        flux_z, keep, windows, low, high = None, newer, (ey - 2, ey - 2), 0, 2 * ey - 1
    even, first, last = place("px", nx)
    got[...] = jnp.zeros(got.shape, F32)
    for c in range(3):
        read_message(got.at[1, c], low, high, c, a_ref, b_ref, even, last)
        read_message(got.at[0, c], low, high, c, b_ref, a_ref, even, first)
    ends = [[[], []] for _ in range(3)]
    for c in range(3):
        for side in range(2):
            for j in range(4):
                speed = v_ref[c, side, j] - time_step * m_ref[side, j] * (total_ref[c, side, j] + got[side, c, j])
                position = u_ref[c, side, j] + time_step * speed
                u_out[c, side, j], v_out[c, side, j] = position, speed
                ends[c][side].append(position)
    stresses(2 * ey, windows, keep, ends, px, part, scale, lame, level, old, new, flux_x, gx, flux_z, flux_y, us, gz_ends, qz,
             grad_ref, div_ref, total)
    if not final:
        send_faces(even, total, 1, 2 + ey, send_a, send_b)
        return
    for c in range(3):
        for j in range(4):
            at = slice((4 * c + j) * ey, (4 * c + j + 1) * ey)
            ahead = total[c, 1, j, 2 : 2 + ey, :]
            send_a[at, :] = ahead
            send_b[at, :] = ahead


def final_rows(ey, field, c, i=0):
    across = 4 * ey
    if field < 2:
        return (9 * field + 3 * c + i) * across
    return (18 + 3 * (field - 2) + c) * across


def pick_kernel(nx, a_ref, b_ref, out):
    even, first, _ = place("px", nx)
    out[...] = jnp.where(first, 0.0, jnp.where(even, b_ref[...], a_ref[...]))


def end_kernel(sizes, mine, core, force_ref, u_out, v_out):
    nx, ey, lanes = sizes
    even, _, _ = place("px", nx)

    def at(start, j=None):
        rows = (slice(start, start + 4 * ey) if j is None else pl.ds(start + j, ey, stride=4), slice(None))
        return jnp.where(even, mine[rows], core[rows])

    for c in range(3):
        for j in range(4):
            rows = (slice((4 * c + j) * ey, (4 * c + j + 1) * ey), slice(None))
            mass = at(final_rows(ey, 4, 0), j)
            speed = at(final_rows(ey, 3, c), j) - time_step * mass * force_ref[rows]
            v_out[c, 0, pl.ds(j, ey, stride=4), :] = speed
            u_out[c, 0, pl.ds(j, ey, stride=4), :] = at(final_rows(ey, 2, c), j) + time_step * speed
        for i in range(3):
            u_out[c, 1 + i] = at(final_rows(ey, 0, c, i))
            v_out[c, 1 + i] = at(final_rows(ey, 1, c, i))


def call(kernel, name, outs, scratch, *args, cost=None):
    shapes = [jax.ShapeDtypeStruct(s, F32) if name == "end" else pltpu.VMEM(s, F32) for s in outs]
    return pl.pallas_call(
        kernel,
        out_shape=shapes,
        scratch_shapes=[pltpu.VMEM(s, F32) for s in scratch],
        compiler_params=pltpu.CompilerParams(vmem_limit_bytes=32 * 1024 * 1024),
        cost_estimate=cost,
        name=name,
    )(*args)


def shards(sizes, displacement, velocity, inverse_mass, lame_first, lame_second, level_map):
    nx, ny = sizes
    _, ex4, ey4, lanes = displacement.shape
    ey = ey4 // 4
    tall, wide, short = 4 * ey, 3 * ey, 2 * ey

    def move(kind, x):
        return lax.ppermute(x, ("px", "py"), pairs_of(kind, nx, ny))

    def along_x(a, b):
        return move("near", a), move("far", b)

    def along_y(x):
        return move("core", x), move("across", x)

    flat = [x.reshape(-1, lanes) for x in (displacement, velocity, inverse_mass)]
    u_e, u_o = along_y(flat[0])
    gradient, divergence = depth_tables(lanes // 4)
    tables = [jnp.asarray(t) for t in (gradient, divergence, weight_table(lanes // 4))]
    sources = flat + [lame_first, lame_second, level_map] + tables
    own_u, own_v, own_m, first, second, level, gradient, divergence, weights = pl.pallas_call(
        functools.partial(load_kernel, len(sources)),
        out_shape=[pltpu.VMEM(x.shape, x.dtype) for x in sources],
        in_specs=[pl.BlockSpec(memory_space=pl.ANY)] * len(sources),
        scratch_shapes=[pltpu.SemaphoreType.DMA((len(sources),))],
        name="load",
    )(*sources)
    long = pl.CostEstimate(flops=20_000_000_000, bytes_accessed=0, transcendentals=0)
    starts = [int(n) for n in np.cumsum([own_v.shape[0], own_m.shape[0], 128, 128])]
    (own,) = call(functools.partial(pack_kernel, starts), "pack", [(starts[3] + 8, lanes)], [], own_v, own_m, first, second, level)
    from_e, from_o = along_y(own)
    (rim,) = call(functools.partial(rim_kernel, ny, ey4), "rim", [(-(-3 * (3 * ey4 - 3) // 8) * 8, lanes)], [], own_u, u_e, u_o, cost=long)
    rim_a, rim_b = along_x(rim, rim)
    sizes_y, sizes_x = (ny, ey, lanes), (nx, ey, lanes)

    def shape(*lead, rows=tall):
        return (*lead, rows, lanes)

    def near_shapes(rows):
        points = functools.partial(shape, rows=rows)
        return [(45, rows, 2 * lanes), points(3, 15), points(3, 25), points(3, 15), points(2, 15)]

    def ends_scratch(rows):
        points = functools.partial(shape, rows=rows)
        return [points(3, 10), points(30), (30, rows, 2 * lanes), points(3, 10)]

    def between_scratch(rows, rows_next):
        points = functools.partial(shape, rows=rows)
        return [points(3, 15), points(3, 2, 15), points(3, 15)] + ([shape(45, rows=rows_next)] if rows_next else [])

    u_ends, u_inner = call(
        functools.partial(spread_u_kernel, sizes_y), "spread_u", [shape(3, 4), shape(3, 3, 4)], [], own_u, u_e, u_o
    )
    lame, level = call(
        functools.partial(tables_kernel, sizes_y, starts), "tables", [shape(2, 2, 25), shape(2)], [(3, 264, lanes)],
        own, from_e, from_o, weights,
    )
    gz, gy, *near = call(first_kernel, "before0", near_shapes(tall), [shape(45)], u_inner, lame, gradient)
    v_ends, v_inner, m_ends, m_inner = call(
        functools.partial(spread_v_kernel, sizes_y, starts[0]), "spread_v",
        [shape(3, 4), shape(3, 3, 4), shape(4), shape(3, 4)], [], own, from_e, from_o,
    )

    tables = (lame, level, gradient, divergence)
    message = (message_rows(1, 3 * ey - 2, 4), lanes)
    rim_u, old_ends, flux_x, gx, total, send_a, send_b = call(
        functools.partial(start_kernel, sizes_x), "stress0",
        [shape(3, 4), shape(6, 2, 10), shape(3, 25), shape(3, 25), shape(3, 2, 4), message, message],
        ends_scratch(tall),
        u_ends, v_ends, m_ends, rim_a, rim_b, *near, *tables,
    )
    got_a, got_b = along_x(send_a, send_b)
    every, window, mine = slice(0, tall), slice(ey - 2, 3 * ey - 2), slice(2, 2 + ey)
    *state, old_inner = call(
        functools.partial(between_kernel, every, False, None, (0, 0), True, newest, (0, 0)), "between0",
        [shape(3, 3, 4), shape(3, 3, 4), shape(3, 4)] + near_shapes(tall) + [shape(6, 2, 15)], between_scratch(tall, tall),
        flux_x, gx, gz, gy, u_inner, v_inner, m_inner, level, *tables,
    )
    u_inner, v_inner, m_inner, gz, gy, *near = state

    ends = shape(3, 2, 4, rows=short)
    message = (message_rows(0, 2 * ey - 1, 3), lanes)
    u_ends, v_ends, m_ends, flux_x, gx, total, send_a, send_b = call(
        functools.partial(second_kernel, sizes_x), "stress1",
        [ends, ends, ends[1:], shape(3, 25), shape(3, 25), ends, message, message],
        [shape(2, 4, 4), shape(3, 2, 10), shape(3, 2, 4)] + ends_scratch(tall),
        u_ends, rim_u, v_ends, m_ends, total, got_a, got_b, *near, old_ends, *tables,
    )
    got_a, got_b = along_x(send_a, send_b)
    inner = shape(3, 3, 4, rows=short)
    u_inner, v_inner, m_inner, gz, gy, *near = call(
        functools.partial(between_kernel, window, False, newest, (0, 0), False, newer, (ey - 2, ey - 2)), "between1",
        [inner, inner, inner[1:]] + near_shapes(short), between_scratch(tall, short),
        flux_x, gx, gz, gy, u_inner, v_inner, m_inner, old_inner, *tables,
    )

    points, got = shape(3, 25, rows=short), shape(2, 3, 4, rows=short)
    message = (message_rows(1, 2 + ey, 3), lanes)
    u_ends, v_ends, old_ends, flux_x, gx, total, send_a, send_b = call(
        functools.partial(later_kernel, sizes_x, False), "stress2",
        [ends, ends, shape(6, 2, 10, rows=short), points, points, ends, message, message], [got] + ends_scratch(short),
        u_ends, v_ends, m_ends, total, got_a, got_b, *near, old_ends, *tables,
    )
    got_a, got_b = along_x(send_a, send_b)
    every = slice(0, short)
    *state, old_inner = call(
        functools.partial(between_kernel, every, False, newer, (ey - 2, ey - 2), True, newest, (ey - 2, 0)), "between2",
        [inner, inner, inner[1:]] + near_shapes(short) + [shape(6, 2, 15, rows=short)], between_scratch(short, short),
        flux_x, gx, gz, gy, u_inner, v_inner, m_inner, old_inner, *tables,
    )
    u_inner, v_inner, m_inner, gz, gy, *near = state

    message = (12 * ey, lanes)
    u_ends, v_ends, flux_x, gx, total, send_a, send_b = call(
        functools.partial(later_kernel, sizes_x, True), "stress3",
        [ends, ends, points, points, ends, message, message], [got, shape(3, 2, 10, rows=short)] + ends_scratch(short),
        u_ends, v_ends, m_ends, total, got_a, got_b, *near, old_ends, *tables,
    )
    got_a, got_b = move("home", send_a), move("far", send_b)
    (results,) = call(
        functools.partial(between_kernel, mine, True, newest, (ey - 2, 0), False, None, None), "between3",
        [(25 * ey4, lanes)], between_scratch(short, 0),
        flux_x, gx, gz, gy, u_inner, v_inner, m_inner, old_inner, *tables, u_ends, v_ends, m_ends, total,
    )
    (force,) = call(functools.partial(pick_kernel, nx), "pick", [message], [], got_a, got_b, cost=long)
    return tuple(call(
        functools.partial(end_kernel, sizes_x), "end", [displacement.shape, velocity.shape], [],
        results, move("core", results), force,
    ))


def solution(mesh):
    sizes = (mesh.shape["px"], mesh.shape["py"])
    in_specs = (
        P(None, "px", "py", None),
        P(None, "px", "py", None),
        P("px", "py", None),
        P(None, None, None, "px", "py"),
        P(None, None, None, "px", "py"),
        P("px", "py"),
    )
    out_specs = (P(None, "px", "py", None), P(None, "px", "py", None))
    return jax.shard_map(
        functools.partial(shards, sizes), mesh=mesh, in_specs=in_specs, out_specs=out_specs, check_vma=False
    )
```

time: 42.2 us -> 38.3 us (0.908)
  waiting for transfers between devices: 17.1 us -> 15.2 us
  starting transfers between devices: 13.8 us -> 11.9 us
    ppermute x16 -> x15, waiting for transfers between devices: 17.1 us -> 15.2 us  [move(): return lax.ppermute(x, ('px', 'py'), pairs_of(kind, nx, ny))]
    ppermute x16 -> x15, starting transfers between devices: 13.8 us -> 11.9 us  [move(): return lax.ppermute(x, ('px', 'py'), pairs_of(kind, nx, ny))]
    pallas_call x16, Pallas kernels: 9.13 us -> 8.71 us  [call(): pl.pallas_call(kernel, out_shape=shapes, scratch_shapes=[pltpu.VMEM(s, F3...]
  transfers between devices with their start and end apart: 16 -> 15, of which waited for: 11 -> 11; matrix products, arithmetic and copies ran while one was open for 0% -> 0% of each run, Pallas kernels for 14% -> 17%
where the time goes in v3:
time: 38.3 us; the launch traced here: 37.8 us
  waiting for transfers between devices  15.2 us (40%)
  starting transfers between devices  11.9 us (31%)
  Pallas kernels  10 us (26%)
  between operations  0.75 us (2%)
    ppermute x15, waiting for transfers between devices, move(): return lax.ppermute(x, ('px', 'py'), pairs_of(kind, nx, ny))  15.2 us
    ppermute x15, starting transfers between devices, move(): return lax.ppermute(x, ('px', 'py'), pairs_of(kind, nx, ny))  11.9 us
    pallas_call x16, Pallas kernels, call(): pl.pallas_call(kernel, out_shape=shapes, scratch_shapes=[pltpu.VMEM(s, F3...  8.71 us
    pallas_call x1, Pallas kernels, shards(): pl.pallas_call(functools.partial(load_kernel, len(sources)), out_shape=[p...  1.29 us
  transfers between devices with their start and end apart: 15, of which 11 were waited for; matrix products, arithmetic and copies ran while one was open for 0% of the time, Pallas kernels for 17%

profile of v3, /device:TPU:16, one launch (start us, length us, event | category | flops | bytes accessed | tf_op | source)
XLA Modules:
  0.0 37.8 jit_solution(8803494876872956995)
XLA Ops:
  0.6 1.6 %collective-permute-start.1 = (f32[192,128]{1,0:T(8,128)}, f32[192,128]{1,0:T(8,128)S(1)}, u32[]{:S(2)}, u32[]{:S(2)}) collective-permute-start(f32[192,128]{1,0:T(8,128)} %bitcast.4), channel_id=1, source_target_pairs={{0,8},{1,2},{2,1},{3,11},{4,5},{5,7},{6,4},{7,6},{8,0},{9,10},{10,... | collective-permute-start | bytes 294920 | tf_op jit(solution)/shard_map/ppermute | solution.py:676
  2.3 1.3 %load.1 = (f32[192,128]{1,0:T(8,128)S(1)}, f32[192,128]{1,0:T(8,128)S(1)}, f32[64,128]{1,0:T(8,128)S(1)}, f32[5,5,5,1,128]{4,3,2,1,0:T(1,128)S(1)}, f32[5,5,5,1,...) custom-call(f32[192,128]{1,0:T(8,128)} %bitcast.6, ...), custom_call_target="tpu_custom_call" | custom-call | tf_op jit(solution)/shard_map/load/pallas_call | solution.py:689
  3.7 1.6 %collective-permute-start.3 = (f32[520,128]{1,0:T(8,128)S(1)}, f32[520,128]{1,0:T(8,128)S(1)}, u32[]{:S(2)}, u32[]{:S(2)}) collective-permute-start(f32[520,128]{1,0:T(8,128)S(1)} %pack.1.own.own_ref), channel_id=1, source_target_pairs={{0,8},{1,2},{2,1},{3,11},{4,5},{5,7},{6,4},{7,6},{8,0},{9,10},{10,... | collective-permute-start | bytes 798728 | tf_op jit(solution)/shard_map/ppermute | solution.py:676
  5.6 2.7 %collective-permute-start.4 = (f32[136,128]{1,0:T(8,128)S(1)}, f32[136,128]{1,0:T(8,128)S(1)}, u32[]{:S(2)}, u32[]{:S(2)}) collective-permute-start(f32[136,128]{1,0:T(8,128)S(1)} %rim.1), channel_id=1, source_target_pairs={{0,5},{1,4},{2,7},{3,6},{4,1},{5,0},{6,3},{7,2},{8,13},{9,12},{10,... | collective-permute-start | bytes 208904 | tf_op jit(solution)/shard_map/ppermute | solution.py:676
  8.5 2.2 %collective-permute-done.3.o.o_ref = f32[520,128]{1,0:T(8,128)S(1)} collective-permute-done((f32[520,128]{1,0:T(8,128)S(1)}, f32[520,128]{1,0:T(8,128)S(1)}, u32[]{:S(2)}, u32[]{:S(2)}) %collective-permute-start.3) | collective-permute-done | bytes 266272 | tf_op jit(solution)/shard_map/ppermute | solution.py:676
  10.7 1.0 %tables.1 = (f32[2,2,25,16,128]{4,3,2,1,0:T(8,128)S(1)}, f32[2,16,128]{2,1,0:T(8,128)S(1)}) custom-call(f32[520,128]{1,0:T(8,128)S(1)} %pack.1.own.own_ref, f32[520,128]{1,0:T(8,128)S(1)} %collective-permute-done.2.e.e_ref, f32[520,128]{1,0:T(8,128)S(1)} %collective-permute-done.3.o.o_ref, f32[50,128]{1,0:T(8,128)S(1)} %get-tuple-element.90.weight_ref), custom_call_target="tpu_custom_call" | custom-call | tf_op jit(solution)/shard_map/tables/pallas_call | solution.py:659
  11.6 0.4 %before0.1 = (f32[45,16,256]{2,1,0:T(8,128)S(1)}, f32[3,15,16,128]{3,2,1,0:T(8,128)S(1)}, f32[3,25,16,128]{3,2,1,0:T(8,128)S(1)}, f32[3,15,16,128]{3,2,1,0:T(8,128)S(1)}, f32[2,15,16,128]{3,2,1,0:T(8,128)S(1)}) custom-call(f32[3,3,4,16,128]{4,3,2,1,0:T(8,128)S(1)} %get-tuple-element.89.u_inner.u_ref, f32[2,2,25,16,128]{4,3,2,1,0:T(8,128)S(1)} %get-tuple-element.91.lame, ...), custom_call_target="tpu_custom_call" | custom-call | tf_op jit(solution)/shard_map/before0/pallas_call | solution.py:659
  12.4 0.8 %stress0.1 = (f32[3,4,16,128]{3,2,1,0:T(8,128)S(1)}, f32[6,2,10,16,128]{4,3,2,1,0:T(8,128)S(1)}, f32[3,25,16,128]{3,2,1,0:T(8,128)S(1)}, f32[3,25,16,128]{3,2,1,...) custom-call(f32[3,4,16,128]{3,2,1,0:T(8,128)S(1)} %get-tuple-element.81.u_ref, ...), custom_call_target="tpu_custom_call" | custom-call | tf_op jit(solution)/shard_map/stress0/pallas_call | solution.py:659
  13.2 0.9 %collective-permute-start.6 = (f32[152,128]{1,0:T(8,128)S(1)}, f32[152,128]{1,0:T(8,128)S(1)}, u32[]{:S(2)}, u32[]{:S(2)}) collective-permute-start(f32[152,128]{1,0:T(8,128)S(1)} %get-tuple-element.100), channel_id=1, source_target_pairs={{0,5},{1,4},{2,7},{3,6},{4,1},{5,0},{6,3},{7,2},{8,13},{9,12},{10,... | collective-permute-start | bytes 233480 | tf_op jit(solution)/shard_map/ppermute | solution.py:676
  14.2 0.6 %collective-permute-start.7 = (f32[152,128]{1,0:T(8,128)S(1)}, f32[152,128]{1,0:T(8,128)S(1)}, u32[]{:S(2)}, u32[]{:S(2)}) collective-permute-start(f32[152,128]{1,0:T(8,128)S(1)} %get-tuple-element.101), channel_id=1, source_target_pairs={{0,1},{1,0},{2,3},{3,2},{4,9},{5,8},{6,11},{7,10},{8,5},{9,4},{10,... | collective-permute-start | bytes 233480 | tf_op jit(solution)/shard_map/ppermute | solution.py:676
  14.8 1.2 %between0.1 = (f32[3,3,4,16,128]{4,3,2,1,0:T(8,128)S(1)}, f32[3,3,4,16,128]{4,3,2,1,0:T(8,128)S(1)}, f32[3,4,16,128]{3,2,1,0:T(8,128)S(1)}, f32[45,16,256]{2,1,0...) custom-call(f32[3,25,16,128]{3,2,1,0:T(8,128)S(1)} %get-tuple-elemen, ...), custom_call_target="tpu_custom_call" | custom-call | tf_op jit(solution)/shard_map/between0/pallas_call | solution.py:659
  16.0 1.7 %collective-permute-done.6.a_ref = f32[152,128]{1,0:T(8,128)S(1)} collective-permute-done((f32[152,128]{1,0:T(8,128)S(1)}, f32[152,128]{1,0:T(8,128)S(1)}, u32[]{:S(2)}, u32[]{:S(2)}) %collective-permute-start.6) | collective-permute-done | bytes 77856 | tf_op jit(solution)/shard_map/ppermute | solution.py:676
  17.7 1.8 %collective-permute-done.7.b_ref = f32[152,128]{1,0:T(8,128)S(1)} collective-permute-done((f32[152,128]{1,0:T(8,128)S(1)}, f32[152,128]{1,0:T(8,128)S(1)}, u32[]{:S(2)}, u32[]{:S(2)}) %collective-permute-start.7) | collective-permute-done | bytes 77856 | tf_op jit(solution)/shard_map/ppermute | solution.py:676
  19.5 0.9 %stress1.1 = (f32[3,2,4,8,128]{4,3,2,1,0:T(8,128)S(1)}, f32[3,2,4,8,128]{4,3,2,1,0:T(8,128)S(1)}, f32[2,4,8,128]{3,2,1,0:T(8,128)S(1)}, f32[3,25,16,128]{3,2,1,0...) custom-call(f32[3,4,16,128]{3,2,1,0:T(8,128)S(1)} %get-tuple-element, ...), custom_call_target="tpu_custom_call" | custom-call | tf_op jit(solution)/shard_map/stress1/pallas_call | solution.py:659
  20.4 0.6 %collective-permute-start.8 = (f32[88,128]{1,0:T(8,128)S(1)}, f32[88,128]{1,0:T(8,128)S(1)}, u32[]{:S(2)}, u32[]{:S(2)}) collective-permute-start(f32[88,128]{1,0:T(8,128)S(1)} %get-tuple-element.116), channel_id=1, source_target_pairs={{0,5},{1,4},{2,7},{3,6},{4,1},{5,0},{6,3},{7,2},{8,13},{9,12},{10,... | collective-permute-start | bytes 135176 | tf_op jit(solution)/shard_map/ppermute | solution.py:676
  21.0 0.4 %collective-permute-start.9 = (f32[88,128]{1,0:T(8,128)S(1)}, f32[88,128]{1,0:T(8,128)S(1)}, u32[]{:S(2)}, u32[]{:S(2)}) collective-permute-start(f32[88,128]{1,0:T(8,128)S(1)} %get-tuple-element.117), channel_id=1, source_target_pairs={{0,1},{1,0},{2,3},{3,2},{4,9},{5,8},{6,11},{7,10},{8,5},{9,4},{10,... | collective-permute-start | bytes 135176 | tf_op jit(solution)/shard_map/ppermute | solution.py:676
  21.5 1.0 %between1.1 = (f32[3,3,4,8,128]{4,3,2,1,0:T(8,128)S(1)}, f32[3,3,4,8,128]{4,3,2,1,0:T(8,128)S(1)}, f32[3,4,8,128]{3,2,1,0:T(8,128)S(1)}, f32[45,8,256]{2,1,0:T(8...) custom-call(f32[3,25,16,128]{3,2,1,0:T(8,128)S(1)} %get-tuple-elemen, ...), custom_call_target="tpu_custom_call" | custom-call | tf_op jit(solution)/shard_map/between1/pallas_call | solution.py:659
  22.4 1.7 %collective-permute-done.8.a_ref = f32[88,128]{1,0:T(8,128)S(1)} collective-permute-done((f32[88,128]{1,0:T(8,128)S(1)}, f32[88,128]{1,0:T(8,128)S(1)}, u32[]{:S(2)}, u32[]{:S(2)}) %collective-permute-start.8) | collective-permute-done | bytes 45088 | tf_op jit(solution)/shard_map/ppermute | solution.py:676
  24.2 1.4 %collective-permute-done.9.b_ref = f32[88,128]{1,0:T(8,128)S(1)} collective-permute-done((f32[88,128]{1,0:T(8,128)S(1)}, f32[88,128]{1,0:T(8,128)S(1)}, u32[]{:S(2)}, u32[]{:S(2)}) %collective-permute-start.9) | collective-permute-done | bytes 45088 | tf_op jit(solution)/shard_map/ppermute | solution.py:676
  25.5 0.6 %stress2.1 = (f32[3,2,4,8,128]{4,3,2,1,0:T(8,128)S(1)}, f32[3,2,4,8,128]{4,3,2,1,0:T(8,128)S(1)}, f32[6,2,10,8,128]{4,3,2,1,0:T(8,128)S(1)}, f32[3,25,8,128]{3,2...) custom-call(f32[3,2,4,8,128]{4,3,2,1,0:T(8,128)S(1)} %get-tuple-elem, ...), custom_call_target="tpu_custom_call" | custom-call | tf_op jit(solution)/shard_map/stress2/pallas_call | solution.py:659
  26.2 1.1 %collective-permute-start.10 = (f32[64,128]{1,0:T(8,128)S(1)}, f32[64,128]{1,0:T(8,128)S(1)}, u32[]{:S(2)}, u32[]{:S(2)}) collective-permute-start(f32[64,128]{1,0:T(8,128)S(1)} %get-tuple-element.132), channel_id=1, source_target_pairs={{0,5},{1,4},{2,7},{3,6},{4,1},{5,0},{6,3},{7,2},{8,13},{9,12},{10,... | collective-permute-start | bytes 98312 | tf_op jit(solution)/shard_map/ppermute | solution.py:676
  27.6 0.8 %between2.1 = (f32[3,3,4,8,128]{4,3,2,1,0:T(8,128)S(1)}, f32[3,3,4,8,128]{4,3,2,1,0:T(8,128)S(1)}, f32[3,4,8,128]{3,2,1,0:T(8,128)S(1)}, f32[45,8,256]{2,1,0:T(8...) custom-call(f32[3,25,8,128]{3,2,1,0:T(8,128)S(1)} %get-tuple-element, ...), custom_call_target="tpu_custom_call" | custom-call | tf_op jit(solution)/shard_map/between2/pallas_call | solution.py:659
  28.4 1.2 %collective-permute-done.10.a_ref = f32[64,128]{1,0:T(8,128)S(1)} collective-permute-done((f32[64,128]{1,0:T(8,128)S(1)}, f32[64,128]{1,0:T(8,128)S(1)}, u32[]{:S(2)}, u32[]{:S(2)}) %collective-permute-start.10) | collective-permute-done | bytes 32800 | tf_op jit(solution)/shard_map/ppermute | solution.py:676
  29.6 1.9 %collective-permute-done.11.b_ref = f32[64,128]{1,0:T(8,128)S(1)} collective-permute-done((f32[64,128]{1,0:T(8,128)S(1)}, f32[64,128]{1,0:T(8,128)S(1)}, u32[]{:S(2)}, u32[]{:S(2)}) %collective-permute-start.11) | collective-permute-done | bytes 32800 | tf_op jit(solution)/shard_map/ppermute | solution.py:676
  31.5 0.6 %stress3.1 = (f32[3,2,4,8,128]{4,3,2,1,0:T(8,128)S(1)}, f32[3,2,4,8,128]{4,3,2,1,0:T(8,128)S(1)}, f32[3,25,8,128]{3,2,1,0:T(8,128)S(1)}, f32[3,25,8,128]{3,2,1,0...) custom-call(f32[3,2,4,8,128]{4,3,2,1,0:T(8,128)S(1)} %get-tuple-element.129.u_ref, ...), custom_call_target="tpu_custom_call" | custom-call | tf_op jit(solution)/shard_map/stress3/pallas_call | solution.py:659
  32.1 0.8 %collective-permute-start.13 = (f32[48,128]{1,0:T(8,128)S(1)}, f32[48,128]{1,0:T(8,128)S(1)}, u32[]{:S(2)}, u32[]{:S(2)}) collective-permute-start(f32[48,128]{1,0:T(8,128)S(1)} %get-tuple-element.156), channel_id=1, source_target_pairs={{0,4},{1,5},{2,6},{3,7},{4,0},{5,1},{6,2},{7,3},{8,12},{9,13},{10,... | collective-permute-start | bytes 73736 | tf_op jit(solution)/shard_map/ppermute | solution.py:676
  32.9 0.5 %collective-permute-start.14 = (f32[48,128]{1,0:T(8,128)S(1)}, f32[48,128]{1,0:T(8,128)S(1)}, u32[]{:S(2)}, u32[]{:S(2)}) collective-permute-start(f32[48,128]{1,0:T(8,128)S(1)} %get-tuple-element.157), channel_id=1, source_target_pairs={{0,1},{1,0},{2,3},{3,2},{4,9},{5,8},{6,11},{7,10},{8,5},{9,4},{10,... | collective-permute-start | bytes 73736 | tf_op jit(solution)/shard_map/ppermute | solution.py:676
  33.5 0.4 %between3.1.mine = f32[400,128]{1,0:T(8,128)S(1)} custom-call(f32[3,25,8,128]{3,2,1,0:T(8,128)S(1)} %get-tuple-element.145.flux_x, f32[3,25,8,128]{3,2,1,0:T(8,128)S(1)} %get-tuple-element.146.gx, f32[45,8,256]{2,1,0:T(8,128)S(1)} %get-tuple-element.147.gz, f32[3,15,8,128]{3,2,1,0:T(8,128)S(1)} %get-tuple-element.148.gy, ...), custom_call_target="tpu_custom_call" | custom-call | tf_op jit(solution)/shard_map/between3/pallas_call | solution.py:659
  33.9 0.4 %collective-permute-start.12 = (f32[400,128]{1,0:T(8,128)S(1)}, f32[400,128]{1,0:T(8,128)S(1)}, u32[]{:S(2)}, u32[]{:S(2)}) collective-permute-start(f32[400,128]{1,0:T(8,128)S(1)} %between3.1.mine), channel_id=1, source_target_pairs={{0,1},{1,0},{2,3},{3,2},{4,5},{5,4},{6,7},{7,6},{8,9},{9,8},{10,11... | collective-permute-start | bytes 614408 | tf_op jit(solution)/shard_map/ppermute | solution.py:676
  34.3 1.7 %collective-permute-done.13.a_ref = f32[48,128]{1,0:T(8,128)S(1)} collective-permute-done((f32[48,128]{1,0:T(8,128)S(1)}, f32[48,128]{1,0:T(8,128)S(1)}, u32[]{:S(2)}, u32[]{:S(2)}) %collective-permute-start.13) | collective-permute-done | bytes 24608 | tf_op jit(solution)/shard_map/ppermute | solution.py:676
  36.0 1.1 %collective-permute-done.14.b_ref = f32[48,128]{1,0:T(8,128)S(1)} collective-permute-done((f32[48,128]{1,0:T(8,128)S(1)}, f32[48,128]{1,0:T(8,128)S(1)}, u32[]{:S(2)}, u32[]{:S(2)}) %collective-permute-start.14) | collective-permute-done | bytes 24608 | tf_op jit(solution)/shard_map/ppermute | solution.py:676
  37.1 0.7 %end.1 = (f32[3,4,16,128]{3,2,1,0:T(8,128)}, f32[3,4,16,128]{3,2,1,0:T(8,128)}) custom-call(f32[400,128]{1,0:T(8,128)S(1)} %between3.1.mine, f32[400,128]{1,0:T(8,128)S(1)} %collective-permute-done.12.core, f32[48,128]{1,0:T(8,128)S(1)} %pick.1.force_ref), custom_call_target="tpu_custom_call" | custom-call | tf_op jit(solution)/shard_map/end/pallas_call | solution.py:659
  (15 shorter events, 1.2 us)
Async XLA Ops:
  0.6 4.9 %collective-permute-start.1 = (f32[192,128]{1,0:T(8,128)}, f32[192,128]{1,0:T(8,128)S(1)}, u32[]{:S(2)}, u32[]{:S(2)}) collective-permute-start(f32[192,128]{1,0:T(8,128)} %bitcast.4), channel_id=1, source_target_pairs={{0,8},{1,2},{2,1},{3,11},{4,5},{5,7},{6,4},{7,6},{8,0},{9,10},{10,... | collective-permute-start | bytes 294920 | tf_op jit(solution)/shard_map/ppermute | solution.py:676
  2.3 3.3 %collective-permute-start = (f32[192,128]{1,0:T(8,128)}, f32[192,128]{1,0:T(8,128)S(1)}, u32[]{:S(2)}, u32[]{:S(2)}) collective-permute-start(f32[192,128]{1,0:T(8,128)} %bitcast.5), channel_id=1, source_target_pairs={{0,1},{1,0},{2,3},{3,2},{4,5},{5,4},{6,7},{7,6},{8,9},{9,8},{10,11... | collective-permute-start | bytes 294920 | tf_op jit(solution)/shard_map/ppermute | solution.py:676
  3.7 7.0 %collective-permute-start.3 = (f32[520,128]{1,0:T(8,128)S(1)}, f32[520,128]{1,0:T(8,128)S(1)}, u32[]{:S(2)}, u32[]{:S(2)}) collective-permute-start(f32[520,128]{1,0:T(8,128)S(1)} %pack.1.own.own_ref), channel_id=1, source_target_pairs={{0,8},{1,2},{2,1},{3,11},{4,5},{5,7},{6,4},{7,6},{8,0},{9,10},{10,... | collective-permute-start | bytes 798728 | tf_op jit(solution)/shard_map/ppermute | solution.py:676
  5.3 5.4 %collective-permute-start.2 = (f32[520,128]{1,0:T(8,128)S(1)}, f32[520,128]{1,0:T(8,128)S(1)}, u32[]{:S(2)}, u32[]{:S(2)}) collective-permute-start(f32[520,128]{1,0:T(8,128)S(1)} %pack.1.own.own_ref), channel_id=1, source_target_pairs={{0,1},{1,0},{2,3},{3,2},{4,5},{5,4},{6,7},{7,6},{8,9},{9,8},{10,11... | collective-permute-start | bytes 798728 | tf_op jit(solution)/shard_map/ppermute | solution.py:676
  5.5 6.6 %collective-permute-start.5 = (f32[136,128]{1,0:T(8,128)S(1)}, f32[136,128]{1,0:T(8,128)S(1)}, u32[]{:S(2)}, u32[]{:S(2)}) collective-permute-start(f32[136,128]{1,0:T(8,128)S(1)} %rim.1), channel_id=1, source_target_pairs={{0,1},{1,0},{2,3},{3,2},{4,9},{5,8},{6,11},{7,10},{8,5},{9,4},{10,... | collective-permute-start | bytes 208904 | tf_op jit(solution)/shard_map/ppermute | solution.py:676
  5.6 6.8 %collective-permute-start.4 = (f32[136,128]{1,0:T(8,128)S(1)}, f32[136,128]{1,0:T(8,128)S(1)}, u32[]{:S(2)}, u32[]{:S(2)}) collective-permute-start(f32[136,128]{1,0:T(8,128)S(1)} %rim.1), channel_id=1, source_target_pairs={{0,5},{1,4},{2,7},{3,6},{4,1},{5,0},{6,3},{7,2},{8,13},{9,12},{10,... | collective-permute-start | bytes 208904 | tf_op jit(solution)/shard_map/ppermute | solution.py:676
  13.2 4.4 %collective-permute-start.6 = (f32[152,128]{1,0:T(8,128)S(1)}, f32[152,128]{1,0:T(8,128)S(1)}, u32[]{:S(2)}, u32[]{:S(2)}) collective-permute-start(f32[152,128]{1,0:T(8,128)S(1)} %get-tuple-element.100), channel_id=1, source_target_pairs={{0,5},{1,4},{2,7},{3,6},{4,1},{5,0},{6,3},{7,2},{8,13},{9,12},{10,... | collective-permute-start | bytes 233480 | tf_op jit(solution)/shard_map/ppermute | solution.py:676
  14.2 5.3 %collective-permute-start.7 = (f32[152,128]{1,0:T(8,128)S(1)}, f32[152,128]{1,0:T(8,128)S(1)}, u32[]{:S(2)}, u32[]{:S(2)}) collective-permute-start(f32[152,128]{1,0:T(8,128)S(1)} %get-tuple-element.101), channel_id=1, source_target_pairs={{0,1},{1,0},{2,3},{3,2},{4,9},{5,8},{6,11},{7,10},{8,5},{9,4},{10,... | collective-permute-start | bytes 233480 | tf_op jit(solution)/shard_map/ppermute | solution.py:676
  20.4 3.7 %collective-permute-start.8 = (f32[88,128]{1,0:T(8,128)S(1)}, f32[88,128]{1,0:T(8,128)S(1)}, u32[]{:S(2)}, u32[]{:S(2)}) collective-permute-start(f32[88,128]{1,0:T(8,128)S(1)} %get-tuple-element.116), channel_id=1, source_target_pairs={{0,5},{1,4},{2,7},{3,6},{4,1},{5,0},{6,3},{7,2},{8,13},{9,12},{10,... | collective-permute-start | bytes 135176 | tf_op jit(solution)/shard_map/ppermute | solution.py:676
  21.0 4.5 %collective-permute-start.9 = (f32[88,128]{1,0:T(8,128)S(1)}, f32[88,128]{1,0:T(8,128)S(1)}, u32[]{:S(2)}, u32[]{:S(2)}) collective-permute-start(f32[88,128]{1,0:T(8,128)S(1)} %get-tuple-element.117), channel_id=1, source_target_pairs={{0,1},{1,0},{2,3},{3,2},{4,9},{5,8},{6,11},{7,10},{8,5},{9,4},{10,... | collective-permute-start | bytes 135176 | tf_op jit(solution)/shard_map/ppermute | solution.py:676
  26.2 3.4 %collective-permute-start.10 = (f32[64,128]{1,0:T(8,128)S(1)}, f32[64,128]{1,0:T(8,128)S(1)}, u32[]{:S(2)}, u32[]{:S(2)}) collective-permute-start(f32[64,128]{1,0:T(8,128)S(1)} %get-tuple-element.132), channel_id=1, source_target_pairs={{0,5},{1,4},{2,7},{3,6},{4,1},{5,0},{6,3},{7,2},{8,13},{9,12},{10,... | collective-permute-start | bytes 98312 | tf_op jit(solution)/shard_map/ppermute | solution.py:676
  27.3 4.2 %collective-permute-start.11 = (f32[64,128]{1,0:T(8,128)S(1)}, f32[64,128]{1,0:T(8,128)S(1)}, u32[]{:S(2)}, u32[]{:S(2)}) collective-permute-start(f32[64,128]{1,0:T(8,128)S(1)} %get-tuple-element.133), channel_id=1, source_target_pairs={{0,1},{1,0},{2,3},{3,2},{4,9},{5,8},{6,11},{7,10},{8,5},{9,4},{10,... | collective-permute-start | bytes 98312 | tf_op jit(solution)/shard_map/ppermute | solution.py:676
  32.1 3.9 %collective-permute-start.13 = (f32[48,128]{1,0:T(8,128)S(1)}, f32[48,128]{1,0:T(8,128)S(1)}, u32[]{:S(2)}, u32[]{:S(2)}) collective-permute-start(f32[48,128]{1,0:T(8,128)S(1)} %get-tuple-element.156), channel_id=1, source_target_pairs={{0,4},{1,5},{2,6},{3,7},{4,0},{5,1},{6,2},{7,3},{8,12},{9,13},{10,... | collective-permute-start | bytes 73736 | tf_op jit(solution)/shard_map/ppermute | solution.py:676
  32.9 4.2 %collective-permute-start.14 = (f32[48,128]{1,0:T(8,128)S(1)}, f32[48,128]{1,0:T(8,128)S(1)}, u32[]{:S(2)}, u32[]{:S(2)}) collective-permute-start(f32[48,128]{1,0:T(8,128)S(1)} %get-tuple-element.157), channel_id=1, source_target_pairs={{0,1},{1,0},{2,3},{3,2},{4,9},{5,8},{6,11},{7,10},{8,5},{9,4},{10,... | collective-permute-start | bytes 73736 | tf_op jit(solution)/shard_map/ppermute | solution.py:676
  33.9 3.2 %collective-permute-start.12 = (f32[400,128]{1,0:T(8,128)S(1)}, f32[400,128]{1,0:T(8,128)S(1)}, u32[]{:S(2)}, u32[]{:S(2)}) collective-permute-start(f32[400,128]{1,0:T(8,128)S(1)} %between3.1.mine), channel_id=1, source_target_pairs={{0,1},{1,0},{2,3},{3,2},{4,5},{5,4},{6,7},{7,6},{8,9},{9,8},{10,11... | collective-permute-start | bytes 614408 | tf_op jit(solution)/shard_map/ppermute | solution.py:676

commit v4 on v3

--- a/solution.py
+++ b/solution.py
@@ -50,7 +50,7 @@
                 table[4 * c + i, lanes + (4 * (c + 1)) % lanes] = D[4, i]
     high, low = split(table)
     gradient = np.concatenate([high, high, low], axis=0)
-    divergence = np.concatenate([high.T, high.T, low.T], axis=0)
+    divergence = np.concatenate([high.T, low.T], axis=1)
     return gradient, divergence
 
 
@@ -140,6 +140,10 @@
         copy.wait()
 
 
+def copy_kernel(x_ref, out):
+    out[...] = x_ref[...]
+
+
 def pack_kernel(starts, v_ref, m_ref, first_ref, second_ref, level_ref, out):
     out[0 : v_ref.shape[0], :] = v_ref[...]
     out[starts[0] : starts[0] + m_ref.shape[0], :] = m_ref[...]
@@ -290,11 +294,12 @@
     out[...] = jnp.dot(lhs, grad_ref[...], preferred_element_type=F32).reshape(count, tall, 2 * lanes)
 
 
-def div_z(flux_z, div_ref, out):
-    _, _, count, tall, lanes = flux_z.shape
-    parts = [halves(flux_z[:, e].reshape(3 * count * tall, lanes)) for e in range(2)]
-    lhs = jnp.concatenate([parts[0][0], parts[1][0], parts[0][1], parts[1][1], parts[0][0], parts[1][0]], axis=1)
-    out[...] = jnp.dot(lhs, div_ref[...], preferred_element_type=F32).reshape(out.shape)
+def div_z(main, point, div_ref):
+    lanes = main.shape[-1]
+    (main_high, main_low), (point_high, point_low) = halves(main), halves(point)
+    high = jnp.dot(jnp.concatenate([main_high, point_high], axis=1), div_ref[...], preferred_element_type=F32)
+    low = jnp.concatenate([main_low, point_low], axis=1)
+    return high[:, :lanes] + (high[:, lanes:] + jnp.dot(low, div_ref[:, :lanes], preferred_element_type=F32))
 
 
 def inside(lanes):
@@ -357,14 +362,16 @@
                 scale[n, p, at, :] = sums[0][3 + n] + sums[1][3 + n]
 
 
-def stresses(tall, windows, keep, ends, px, part, scale, lame, level, old, new, flux_x, gx, flux_z, flux_y, us, gz_ends, qz, grad_ref, div_ref, total):
+def stresses(tall, windows, keep, ends, px, part, scale, lame, level, old, new, flux_x, gx, flux_z, flux_y, us, gz_ends, last_z, qz, grad_ref, div_ref, total):
     lanes = px.shape[-1]
     points = [[five(ends[c][side]) for side in range(2)] for c in range(3)]
     for c in range(3):
         for side in range(2):
-            for j in range(5):
-                us[10 * c + 5 * side + j] = points[c][side][j]
+            for j in range(4):
+                us[8 * c + 4 * side + j] = points[c][side][j]
     grad_z(us, grad_ref, gz_ends)
+    for n in range(6):
+        last_z[n] = rolled(gz_ends[4 * n], -1)
     for c in range(3):
         for j in range(5):
             y = apply5_ends(D, points[c][0][j], points[c][1][j], [px[c, 5 * i + j] for i in range(5)])
@@ -380,7 +387,7 @@
         if keep is not None:
             fresh = [keep(level[e, table, :]) for e in range(2)]
         for side in range(2):
-            ends_y = [apply5(D, [us[10 * c + 5 * side + j, at, :] for j in range(5)]) for c in range(3)]
+            ends_y = [apply5(D, [points[c][side][j][at] for j in range(5)]) for c in range(3)]
             for j in range(5):
                 p, q = 20 * side + j, 5 * side + j
                 x = [gx[c, p, at, :] for c in range(3)]
@@ -388,7 +395,10 @@
                 sums = []
                 for e in range(2):
                     span = slice(e * lanes, (e + 1) * lanes)
-                    z = [gz_ends[10 * c + q, at, span] for c in range(3)]
+                    if j < 4:
+                        z = [gz_ends[8 * c + 4 * side + j, at, span] for c in range(3)]
+                    else:
+                        z = [last_z[2 * c + side, at, span] for c in range(3)]
                     if e == 1:
                         x, y = [g * mask for g in x], [g * mask for g in y]
                     stress = stress_of(lame[0, e, p, table, :], lame[1, e, p, table, :], x, y, z)
@@ -397,21 +407,28 @@
                     if new is not None:
                         for n in range(6):
                             new[n, e, q, at, :] = stress[n]
-                    else:
-                        for n in range(3):
-                            flux_z[n, e, q, at, :] = stress[3 + n]
+                    for n in range(3):
+                        flux_z[n, e, q, at, :] = stress[3 + n]
                     sums.append([v * mask for v in stress[:5]] if e == 1 else stress[:5])
                 xx, yy, xy, xz, yz = [sums[0][n] + sums[1][n] for n in range(5)]
                 for c in range(3):
                     flux_x[c, p, at, :] = (xx, xy, xz)[c]
                     flux_y[c, q, at, :] = (xy, yy, yz)[c]
-    if new is not None:
-        flux_z = new.at[3:6]
-    div_z(flux_z, div_ref, qz)
+    parts = []
+    for e in range(2):
+        rows = []
+        for c in range(3):
+            for side in range(2):
+                first = 5 * side
+                rows.append(flux_z[c, e, first] + rolled(flux_z[c, e, first + 4], 1))
+                rows.append(flux_z[c, e, first + 1 : first + 4].reshape(3 * tall, lanes))
+        parts.append(jnp.concatenate(rows, axis=0))
+    qz[...] = div_z(*parts, div_ref).reshape(qz.shape)
     assemble((0, 4), flux_x, flux_y, qz, lambda c, side, j, value: total.__setitem__((c, side, j), value))
 
 
 def assemble(layers, flux_x, flux_y, qz, put):
+    count = qz.shape[1] // len(layers)
     for c in range(3):
         pieces = []
         for j in range(5):
@@ -419,7 +436,7 @@
             pieces.append([x[i] for i in layers])
         for n in range(len(layers)):
             y = apply5(D.T, [flux_y[c, 5 * n + j] for j in range(5)])
-            z = [pieces[j][n] + (y[j] + qz[c, 5 * n + j]) for j in range(5)]
+            z = [pieces[j][n] + (y[j] + qz[c, count * n + j] if j < count else y[j]) for j in range(5)]
             put(c, n, 0, z[0] + rolled(z[4], 1))
             for j in range(1, 4):
                 put(c, n, j, z[j])
@@ -480,7 +497,9 @@
                 sums.append([v * mask for v in stress[:5]] if e == 1 else stress[:5])
             for c, n in enumerate((2, 1, 4)):
                 flux_y[c, p, at, :] = sums[0][n] + sums[1][n]
-    div_z(new.at[3:6] if stores else flux_z, div_ref, qz)
+    if stores:
+        flux_z = new.at[3:6]
+    qz[...] = div_z(*(flux_z[:, e].reshape(45 * tall, lanes) for e in range(2)), div_ref).reshape(qz.shape)
     inner = [[[None] * 4 for _ in range(3)] for _ in range(3)]
 
     def put(c, n, j, force):
@@ -511,7 +530,7 @@
 
 
 def start_kernel(sizes, u_ref, v_ref, m_ref, a_ref, b_ref, px, part, scale, lame, level, grad_ref, div_ref,
-                 rim_ref, new, flux_x, gx, total, send_a, send_b, flux_y, us, gz_ends, qz):
+                 rim_ref, new, flux_x, gx, total, send_a, send_b, flux_z, flux_y, us, gz_ends, last_z, qz):
     nx, ey, lanes = sizes
     even, _, last = place("px", nx)
     tall = 4 * ey
@@ -522,7 +541,7 @@
             at = (pl.ds(c * (12 * ey - 3) + j, count, stride=4), slice(None))
             rim_ref[c, j, 0:count, :] = jnp.where(last, 0.0, jnp.where(even, a_ref[at], b_ref[at]))
     ends = [[[u_ref[c, j] for j in range(4)], [rim_ref[c, j] for j in range(4)]] for c in range(3)]
-    stresses(tall, (0, 0), None, ends, px, part, scale, lame, level, None, new, flux_x, gx, None, flux_y, us, gz_ends, qz,
+    stresses(tall, (0, 0), None, ends, px, part, scale, lame, level, None, new, flux_x, gx, flux_z, flux_y, us, gz_ends, last_z, qz,
              grad_ref, div_ref, total)
     low, high = 1, 3 * ey - 2
     for c in range(3):
@@ -540,7 +559,7 @@
 
 
 def second_kernel(sizes, u_ref, rim_ref, v_ref, m_ref, total_ref, a_ref, b_ref, px, part, scale, old, lame, level, grad_ref, div_ref,
-                  u_out, v_out, m_out, flux_x, gx, total_out, send_a, send_b, got, flux_z, total, flux_y, us, gz_ends, qz):
+                  u_out, v_out, m_out, flux_x, gx, total_out, send_a, send_b, got, total, flux_z, flux_y, us, gz_ends, last_z, qz):
     nx, ey, lanes = sizes
     even, first, last = place("px", nx)
     tall = 4 * ey
@@ -566,7 +585,7 @@
                 if c == 0:
                     m_out[side, j] = mass[window]
                 ends[c][side].append(position)
-    stresses(tall, (0, 0), newest, ends, px, part, scale, lame, level, old, None, flux_x, gx, flux_z, flux_y, us, gz_ends, qz,
+    stresses(tall, (0, 0), newest, ends, px, part, scale, lame, level, old, None, flux_x, gx, flux_z, flux_y, us, gz_ends, last_z, qz,
              grad_ref, div_ref, total)
     for c in range(3):
         for side in range(2):
@@ -591,11 +610,11 @@
 def later_kernel(sizes, final, u_ref, v_ref, m_ref, total_ref, a_ref, b_ref, px, part, scale, old, lame, level, grad_ref, div_ref, *refs):
     nx, ey, lanes = sizes
     if final:
-        u_out, v_out, flux_x, gx, total, send_a, send_b, got, flux_z, flux_y, us, gz_ends, qz = refs
+        u_out, v_out, flux_x, gx, total, send_a, send_b, got, flux_z, flux_y, us, gz_ends, last_z, qz = refs
         new, keep, windows, low, high = None, newest, (ey - 2, 0), 1, 2 + ey
     else:
-        u_out, v_out, new, flux_x, gx, total, send_a, send_b, got, flux_y, us, gz_ends, qz = refs
-        flux_z, keep, windows, low, high = None, newer, (ey - 2, ey - 2), 0, 2 * ey - 1
+        u_out, v_out, new, flux_x, gx, total, send_a, send_b, got, flux_z, flux_y, us, gz_ends, last_z, qz = refs
+        keep, windows, low, high = newer, (ey - 2, ey - 2), 0, 2 * ey - 1
     even, first, last = place("px", nx)
     got[...] = jnp.zeros(got.shape, F32)
     for c in range(3):
@@ -609,7 +628,7 @@
                 position = u_ref[c, side, j] + time_step * speed
                 u_out[c, side, j], v_out[c, side, j] = position, speed
                 ends[c][side].append(position)
-    stresses(2 * ey, windows, keep, ends, px, part, scale, lame, level, old, new, flux_x, gx, flux_z, flux_y, us, gz_ends, qz,
+    stresses(2 * ey, windows, keep, ends, px, part, scale, lame, level, old, new, flux_x, gx, flux_z, flux_y, us, gz_ends, last_z, qz,
              grad_ref, div_ref, total)
     if not final:
         send_faces(even, total, 1, 2 + ey, send_a, send_b)
@@ -698,7 +717,8 @@
     (own,) = call(functools.partial(pack_kernel, starts), "pack", [(starts[3] + 8, lanes)], [], own_v, own_m, first, second, level)
     from_e, from_o = along_y(own)
     (rim,) = call(functools.partial(rim_kernel, ny, ey4), "rim", [(-(-3 * (3 * ey4 - 3) // 8) * 8, lanes)], [], own_u, u_e, u_o, cost=long)
-    rim_a, rim_b = along_x(rim, rim)
+    (rim_1,) = call(copy_kernel, "face", [rim.shape], [], rim, cost=long)
+    rim_a, rim_b = along_x(rim_1, rim)
     sizes_y, sizes_x = (ny, ey, lanes), (nx, ey, lanes)
 
     def shape(*lead, rows=tall):
@@ -710,7 +730,7 @@
 
     def ends_scratch(rows):
         points = functools.partial(shape, rows=rows)
-        return [points(3, 10), points(30), (30, rows, 2 * lanes), points(3, 10)]
+        return [points(3, 2, 10), points(3, 10), points(24), (24, rows, 2 * lanes), (6, rows, 2 * lanes), points(3, 8)]
 
     def between_scratch(rows, rows_next):
         points = functools.partial(shape, rows=rows)
@@ -751,7 +771,7 @@
     u_ends, v_ends, m_ends, flux_x, gx, total, send_a, send_b = call(
         functools.partial(second_kernel, sizes_x), "stress1",
         [ends, ends, ends[1:], shape(3, 25), shape(3, 25), ends, message, message],
-        [shape(2, 4, 4), shape(3, 2, 10), shape(3, 2, 4)] + ends_scratch(tall),
+        [shape(2, 4, 4), shape(3, 2, 4)] + ends_scratch(tall),
         u_ends, rim_u, v_ends, m_ends, total, got_a, got_b, *near, old_ends, *tables,
     )
     got_a, got_b = along_x(send_a, send_b)
@@ -781,7 +801,7 @@
     message = (12 * ey, lanes)
     u_ends, v_ends, flux_x, gx, total, send_a, send_b = call(
         functools.partial(later_kernel, sizes_x, True), "stress3",
-        [ends, ends, points, points, ends, message, message], [got, shape(3, 2, 10, rows=short)] + ends_scratch(short),
+        [ends, ends, points, points, ends, message, message], [got] + ends_scratch(short),
         u_ends, v_ends, m_ends, total, got_a, got_b, *near, old_ends, *tables,
     )
     got_a, got_b = move("home", send_a), move("far", send_b)

time: 38.3 us -> 37.3 us (0.974)
  starting transfers between devices: 11.9 us -> 11.2 us
  Pallas kernels: 10 us -> 9.41 us
    ppermute x15, starting transfers between devices: 11.9 us -> 11.2 us  [move(): return lax.ppermute(x, ('px', 'py'), pairs_of(kind, nx, ny))]
    pallas_call x16 -> x17, Pallas kernels: 8.71 us -> 8.14 us  [call(): pl.pallas_call(kernel, out_shape=shapes, scratch_shapes=[pltpu.VMEM(s, F3...]
  transfers between devices with their start and end apart: 15 -> 15, of which waited for: 11 -> 10; matrix products, arithmetic and copies ran while one was open for 0% -> 0% of each run, Pallas kernels for 17% -> 17%
where the time goes in v4:
time: 37.3 us; the launch traced here: 36.9 us
  waiting for transfers between devices  15.4 us (41%)
  starting transfers between devices  11.2 us (30%)
  Pallas kernels  9.41 us (25%)
  between operations  0.76 us (2%)
    ppermute x15, waiting for transfers between devices, move(): return lax.ppermute(x, ('px', 'py'), pairs_of(kind, nx, ny))  15.4 us
    ppermute x15, starting transfers between devices, move(): return lax.ppermute(x, ('px', 'py'), pairs_of(kind, nx, ny))  11.2 us
    pallas_call x17, Pallas kernels, call(): pl.pallas_call(kernel, out_shape=shapes, scratch_shapes=[pltpu.VMEM(s, F3...  8.14 us
    pallas_call x1, Pallas kernels, shards(): pl.pallas_call(functools.partial(load_kernel, len(sources)), out_shape=[p...  1.27 us
  transfers between devices with their start and end apart: 15, of which 10 were waited for; matrix products, arithmetic and copies ran while one was open for 0% of the time, Pallas kernels for 17%

profile of v4, /device:TPU:16, one launch (start us, length us, event | category | flops | bytes accessed | tf_op | source)
XLA Modules:
  0.0 36.9 jit_solution(10649474859182598158)
XLA Ops:
  0.6 1.6 %collective-permute-start.1 = (f32[192,128]{1,0:T(8,128)}, f32[192,128]{1,0:T(8,128)S(1)}, u32[]{:S(2)}, u32[]{:S(2)}) collective-permute-start(f32[192,128]{1,0:T(8,128)} %bitcast.4), channel_id=1, source_target_pairs={{0,8},{1,2},{2,1},{3,11},{4,5},{5,7},{6,4},{7,6},{8,0},{9,10},{10,... | collective-permute-start | bytes 294920 | tf_op jit(solution)/shard_map/ppermute | solution.py:695
  2.3 1.3 %load.1 = (f32[192,128]{1,0:T(8,128)S(1)}, f32[192,128]{1,0:T(8,128)S(1)}, f32[64,128]{1,0:T(8,128)S(1)}, f32[5,5,5,1,128]{4,3,2,1,0:T(1,128)S(1)}, f32[5,5,5,1,...) custom-call(f32[192,128]{1,0:T(8,128)} %bitcast.6, ...), custom_call_target="tpu_custom_call" | custom-call | tf_op jit(solution)/shard_map/load/pallas_call | solution.py:708
  3.6 1.6 %collective-permute-start.3 = (f32[520,128]{1,0:T(8,128)S(1)}, f32[520,128]{1,0:T(8,128)S(1)}, u32[]{:S(2)}, u32[]{:S(2)}) collective-permute-start(f32[520,128]{1,0:T(8,128)S(1)} %pack.1.own.own_ref), channel_id=1, source_target_pairs={{0,8},{1,2},{2,1},{3,11},{4,5},{5,7},{6,4},{7,6},{8,0},{9,10},{10,... | collective-permute-start | bytes 798728 | tf_op jit(solution)/shard_map/ppermute | solution.py:695
  5.6 1.6 %collective-permute-start.5 = (f32[136,128]{1,0:T(8,128)S(1)}, f32[136,128]{1,0:T(8,128)S(1)}, u32[]{:S(2)}, u32[]{:S(2)}) collective-permute-start(f32[136,128]{1,0:T(8,128)S(1)} %rim.1.x_ref), channel_id=1, source_target_pairs={{0,1},{1,0},{2,3},{3,2},{4,9},{5,8},{6,11},{7,10},{8,5},{9,4},{10,... | collective-permute-start | bytes 208904 | tf_op jit(solution)/shard_map/ppermute | solution.py:695
  7.4 2.8 %collective-permute-done.3.o.o_ref = f32[520,128]{1,0:T(8,128)S(1)} collective-permute-done((f32[520,128]{1,0:T(8,128)S(1)}, f32[520,128]{1,0:T(8,128)S(1)}, u32[]{:S(2)}, u32[]{:S(2)}) %collective-permute-start.3) | collective-permute-done | bytes 266272 | tf_op jit(solution)/shard_map/ppermute | solution.py:695
  10.2 1.0 %tables.1 = (f32[2,2,25,16,128]{4,3,2,1,0:T(8,128)S(1)}, f32[2,16,128]{2,1,0:T(8,128)S(1)}) custom-call(f32[520,128]{1,0:T(8,128)S(1)} %pack.1.own.own_ref, f32[520,128]{1,0:T(8,128)S(1)} %collective-permute-done.2.e.e_ref, f32[520,128]{1,0:T(8,128)S(1)} %collective-permute-done.3.o.o_ref, f32[50,128]{1,0:T(8,128)S(1)} %get-tuple-element.90.weight_ref), custom_call_target="tpu_custom_call" | custom-call | tf_op jit(solution)/shard_map/tables/pallas_call | solution.py:678
  11.2 0.4 %before0.1 = (f32[45,16,256]{2,1,0:T(8,128)S(1)}, f32[3,15,16,128]{3,2,1,0:T(8,128)S(1)}, f32[3,25,16,128]{3,2,1,0:T(8,128)S(1)}, f32[3,15,16,128]{3,2,1,0:T(8,128)S(1)}, f32[2,15,16,128]{3,2,1,0:T(8,128)S(1)}) custom-call(f32[3,3,4,16,128]{4,3,2,1,0:T(8,128)S(1)} %get-tuple-element.89.u_inner.u_ref, f32[2,2,25,16,128]{4,3,2,1,0:T(8,128)S(1)} %get-tuple-element.91.lame, ...), custom_call_target="tpu_custom_call" | custom-call | tf_op jit(solution)/shard_map/before0/pallas_call | solution.py:678
  11.7 0.7 %stress0.1 = (f32[3,4,16,128]{3,2,1,0:T(8,128)S(1)}, f32[6,2,10,16,128]{4,3,2,1,0:T(8,128)S(1)}, f32[3,25,16,128]{3,2,1,0:T(8,128)S(1)}, f32[3,25,16,128]{3,2,1,...) custom-call(f32[3,4,16,128]{3,2,1,0:T(8,128)S(1)} %get-tuple-element.81.u_ref, ...), custom_call_target="tpu_custom_call" | custom-call | tf_op jit(solution)/shard_map/stress0/pallas_call | solution.py:678
  12.5 0.8 %collective-permute-start.6 = (f32[152,128]{1,0:T(8,128)S(1)}, f32[152,128]{1,0:T(8,128)S(1)}, u32[]{:S(2)}, u32[]{:S(2)}) collective-permute-start(f32[152,128]{1,0:T(8,128)S(1)} %get-tuple-element.100), channel_id=1, source_target_pairs={{0,5},{1,4},{2,7},{3,6},{4,1},{5,0},{6,3},{7,2},{8,13},{9,12},{10,... | collective-permute-start | bytes 233480 | tf_op jit(solution)/shard_map/ppermute | solution.py:695
  13.3 0.8 %collective-permute-start.7 = (f32[152,128]{1,0:T(8,128)S(1)}, f32[152,128]{1,0:T(8,128)S(1)}, u32[]{:S(2)}, u32[]{:S(2)}) collective-permute-start(f32[152,128]{1,0:T(8,128)S(1)} %get-tuple-element.101), channel_id=1, source_target_pairs={{0,1},{1,0},{2,3},{3,2},{4,9},{5,8},{6,11},{7,10},{8,5},{9,4},{10,... | collective-permute-start | bytes 233480 | tf_op jit(solution)/shard_map/ppermute | solution.py:695
  14.1 1.2 %between0.1 = (f32[3,3,4,16,128]{4,3,2,1,0:T(8,128)S(1)}, f32[3,3,4,16,128]{4,3,2,1,0:T(8,128)S(1)}, f32[3,4,16,128]{3,2,1,0:T(8,128)S(1)}, f32[45,16,256]{2,1,0...) custom-call(f32[3,25,16,128]{3,2,1,0:T(8,128)S(1)} %get-tuple-elemen, ...), custom_call_target="tpu_custom_call" | custom-call | tf_op jit(solution)/shard_map/between0/pallas_call | solution.py:678
  15.3 1.6 %collective-permute-done.6.a_ref = f32[152,128]{1,0:T(8,128)S(1)} collective-permute-done((f32[152,128]{1,0:T(8,128)S(1)}, f32[152,128]{1,0:T(8,128)S(1)}, u32[]{:S(2)}, u32[]{:S(2)}) %collective-permute-start.6) | collective-permute-done | bytes 77856 | tf_op jit(solution)/shard_map/ppermute | solution.py:695
  16.9 1.4 %collective-permute-done.7.b_ref = f32[152,128]{1,0:T(8,128)S(1)} collective-permute-done((f32[152,128]{1,0:T(8,128)S(1)}, f32[152,128]{1,0:T(8,128)S(1)}, u32[]{:S(2)}, u32[]{:S(2)}) %collective-permute-start.7) | collective-permute-done | bytes 77856 | tf_op jit(solution)/shard_map/ppermute | solution.py:695
  18.3 0.8 %stress1.1 = (f32[3,2,4,8,128]{4,3,2,1,0:T(8,128)S(1)}, f32[3,2,4,8,128]{4,3,2,1,0:T(8,128)S(1)}, f32[2,4,8,128]{3,2,1,0:T(8,128)S(1)}, f32[3,25,16,128]{3,2,1,0...) custom-call(f32[3,4,16,128]{3,2,1,0:T(8,128)S(1)} %get-tuple-element, ...), custom_call_target="tpu_custom_call" | custom-call | tf_op jit(solution)/shard_map/stress1/pallas_call | solution.py:678
  19.1 1.1 %collective-permute-start.8 = (f32[88,128]{1,0:T(8,128)S(1)}, f32[88,128]{1,0:T(8,128)S(1)}, u32[]{:S(2)}, u32[]{:S(2)}) collective-permute-start(f32[88,128]{1,0:T(8,128)S(1)} %get-tuple-element.116), channel_id=1, source_target_pairs={{0,5},{1,4},{2,7},{3,6},{4,1},{5,0},{6,3},{7,2},{8,13},{9,12},{10,... | collective-permute-start | bytes 135176 | tf_op jit(solution)/shard_map/ppermute | solution.py:695
  20.2 0.9 %between1.1 = (f32[3,3,4,8,128]{4,3,2,1,0:T(8,128)S(1)}, f32[3,3,4,8,128]{4,3,2,1,0:T(8,128)S(1)}, f32[3,4,8,128]{3,2,1,0:T(8,128)S(1)}, f32[45,8,256]{2,1,0:T(8...) custom-call(f32[3,25,16,128]{3,2,1,0:T(8,128)S(1)} %get-tuple-elemen, ...), custom_call_target="tpu_custom_call" | custom-call | tf_op jit(solution)/shard_map/between1/pallas_call | solution.py:678
  21.1 1.5 %collective-permute-done.8.a_ref = f32[88,128]{1,0:T(8,128)S(1)} collective-permute-done((f32[88,128]{1,0:T(8,128)S(1)}, f32[88,128]{1,0:T(8,128)S(1)}, u32[]{:S(2)}, u32[]{:S(2)}) %collective-permute-start.8) | collective-permute-done | bytes 45088 | tf_op jit(solution)/shard_map/ppermute | solution.py:695
  22.7 2.1 %collective-permute-done.9.b_ref = f32[88,128]{1,0:T(8,128)S(1)} collective-permute-done((f32[88,128]{1,0:T(8,128)S(1)}, f32[88,128]{1,0:T(8,128)S(1)}, u32[]{:S(2)}, u32[]{:S(2)}) %collective-permute-start.9) | collective-permute-done | bytes 45088 | tf_op jit(solution)/shard_map/ppermute | solution.py:695
  24.8 0.5 %stress2.1 = (f32[3,2,4,8,128]{4,3,2,1,0:T(8,128)S(1)}, f32[3,2,4,8,128]{4,3,2,1,0:T(8,128)S(1)}, f32[6,2,10,8,128]{4,3,2,1,0:T(8,128)S(1)}, f32[3,25,8,128]{3,2...) custom-call(f32[3,2,4,8,128]{4,3,2,1,0:T(8,128)S(1)} %get-tuple-elem, ...), custom_call_target="tpu_custom_call" | custom-call | tf_op jit(solution)/shard_map/stress2/pallas_call | solution.py:678
  25.3 0.8 %collective-permute-start.10 = (f32[64,128]{1,0:T(8,128)S(1)}, f32[64,128]{1,0:T(8,128)S(1)}, u32[]{:S(2)}, u32[]{:S(2)}) collective-permute-start(f32[64,128]{1,0:T(8,128)S(1)} %get-tuple-element.132), channel_id=1, source_target_pairs={{0,5},{1,4},{2,7},{3,6},{4,1},{5,0},{6,3},{7,2},{8,13},{9,12},{10,... | collective-permute-start | bytes 98312 | tf_op jit(solution)/shard_map/ppermute | solution.py:695
  26.1 0.8 %collective-permute-start.11 = (f32[64,128]{1,0:T(8,128)S(1)}, f32[64,128]{1,0:T(8,128)S(1)}, u32[]{:S(2)}, u32[]{:S(2)}) collective-permute-start(f32[64,128]{1,0:T(8,128)S(1)} %get-tuple-element.133), channel_id=1, source_target_pairs={{0,1},{1,0},{2,3},{3,2},{4,9},{5,8},{6,11},{7,10},{8,5},{9,4},{10,... | collective-permute-start | bytes 98312 | tf_op jit(solution)/shard_map/ppermute | solution.py:695
  26.8 0.8 %between2.1 = (f32[3,3,4,8,128]{4,3,2,1,0:T(8,128)S(1)}, f32[3,3,4,8,128]{4,3,2,1,0:T(8,128)S(1)}, f32[3,4,8,128]{3,2,1,0:T(8,128)S(1)}, f32[45,8,256]{2,1,0:T(8...) custom-call(f32[3,25,8,128]{3,2,1,0:T(8,128)S(1)} %get-tuple-element, ...), custom_call_target="tpu_custom_call" | custom-call | tf_op jit(solution)/shard_map/between2/pallas_call | solution.py:678
  27.6 1.1 %collective-permute-done.10.a_ref = f32[64,128]{1,0:T(8,128)S(1)} collective-permute-done((f32[64,128]{1,0:T(8,128)S(1)}, f32[64,128]{1,0:T(8,128)S(1)}, u32[]{:S(2)}, u32[]{:S(2)}) %collective-permute-start.10) | collective-permute-done | bytes 32800 | tf_op jit(solution)/shard_map/ppermute | solution.py:695
  28.7 1.6 %collective-permute-done.11.b_ref = f32[64,128]{1,0:T(8,128)S(1)} collective-permute-done((f32[64,128]{1,0:T(8,128)S(1)}, f32[64,128]{1,0:T(8,128)S(1)}, u32[]{:S(2)}, u32[]{:S(2)}) %collective-permute-start.11) | collective-permute-done | bytes 32800 | tf_op jit(solution)/shard_map/ppermute | solution.py:695
  30.3 0.5 %stress3.1 = (f32[3,2,4,8,128]{4,3,2,1,0:T(8,128)S(1)}, f32[3,2,4,8,128]{4,3,2,1,0:T(8,128)S(1)}, f32[3,25,8,128]{3,2,1,0:T(8,128)S(1)}, f32[3,25,8,128]{3,2,1,0...) custom-call(f32[3,2,4,8,128]{4,3,2,1,0:T(8,128)S(1)} %get-tuple-element.129.u_ref, ...), custom_call_target="tpu_custom_call" | custom-call | tf_op jit(solution)/shard_map/stress3/pallas_call | solution.py:678
  30.8 1.1 %collective-permute-start.13 = (f32[48,128]{1,0:T(8,128)S(1)}, f32[48,128]{1,0:T(8,128)S(1)}, u32[]{:S(2)}, u32[]{:S(2)}) collective-permute-start(f32[48,128]{1,0:T(8,128)S(1)} %get-tuple-element.156), channel_id=1, source_target_pairs={{0,4},{1,5},{2,6},{3,7},{4,0},{5,1},{6,2},{7,3},{8,12},{9,13},{10,... | collective-permute-start | bytes 73736 | tf_op jit(solution)/shard_map/ppermute | solution.py:695
  31.9 0.6 %collective-permute-start.14 = (f32[48,128]{1,0:T(8,128)S(1)}, f32[48,128]{1,0:T(8,128)S(1)}, u32[]{:S(2)}, u32[]{:S(2)}) collective-permute-start(f32[48,128]{1,0:T(8,128)S(1)} %get-tuple-element.157), channel_id=1, source_target_pairs={{0,1},{1,0},{2,3},{3,2},{4,9},{5,8},{6,11},{7,10},{8,5},{9,4},{10,... | collective-permute-start | bytes 73736 | tf_op jit(solution)/shard_map/ppermute | solution.py:695
  32.5 0.4 %between3.1.mine = f32[400,128]{1,0:T(8,128)S(1)} custom-call(f32[3,25,8,128]{3,2,1,0:T(8,128)S(1)} %get-tuple-element.145.flux_x, f32[3,25,8,128]{3,2,1,0:T(8,128)S(1)} %get-tuple-element.146.gx, f32[45,8,256]{2,1,0:T(8,128)S(1)} %get-tuple-element.147.gz, f32[3,15,8,128]{3,2,1,0:T(8,128)S(1)} %get-tuple-element.148.gy, ...), custom_call_target="tpu_custom_call" | custom-call | tf_op jit(solution)/shard_map/between3/pallas_call | solution.py:678
  32.9 0.3 collective-permute-start.12
  33.1 1.6 %collective-permute-done.13.a_ref = f32[48,128]{1,0:T(8,128)S(1)} collective-permute-done((f32[48,128]{1,0:T(8,128)S(1)}, f32[48,128]{1,0:T(8,128)S(1)}, u32[]{:S(2)}, u32[]{:S(2)}) %collective-permute-start.13) | collective-permute-done | bytes 24608 | tf_op jit(solution)/shard_map/ppermute | solution.py:695
  34.7 1.4 %collective-permute-done.14.b_ref = f32[48,128]{1,0:T(8,128)S(1)} collective-permute-done((f32[48,128]{1,0:T(8,128)S(1)}, f32[48,128]{1,0:T(8,128)S(1)}, u32[]{:S(2)}, u32[]{:S(2)}) %collective-permute-start.14) | collective-permute-done | bytes 24608 | tf_op jit(solution)/shard_map/ppermute | solution.py:695
  36.1 0.7 %end.1 = (f32[3,4,16,128]{3,2,1,0:T(8,128)}, f32[3,4,16,128]{3,2,1,0:T(8,128)}) custom-call(f32[400,128]{1,0:T(8,128)S(1)} %between3.1.mine, f32[400,128]{1,0:T(8,128)S(1)} %collective-permute-done.12.core, f32[48,128]{1,0:T(8,128)S(1)} %pick.1.force_ref), custom_call_target="tpu_custom_call" | custom-call | tf_op jit(solution)/shard_map/end/pallas_call | solution.py:678
  (16 shorter events, 0.7 us)
Async XLA Ops:
  0.6 4.9 %collective-permute-start.1 = (f32[192,128]{1,0:T(8,128)}, f32[192,128]{1,0:T(8,128)S(1)}, u32[]{:S(2)}, u32[]{:S(2)}) collective-permute-start(f32[192,128]{1,0:T(8,128)} %bitcast.4), channel_id=1, source_target_pairs={{0,8},{1,2},{2,1},{3,11},{4,5},{5,7},{6,4},{7,6},{8,0},{9,10},{10,... | collective-permute-start | bytes 294920 | tf_op jit(solution)/shard_map/ppermute | solution.py:695
  2.3 3.3 %collective-permute-start = (f32[192,128]{1,0:T(8,128)}, f32[192,128]{1,0:T(8,128)S(1)}, u32[]{:S(2)}, u32[]{:S(2)}) collective-permute-start(f32[192,128]{1,0:T(8,128)} %bitcast.5), channel_id=1, source_target_pairs={{0,1},{1,0},{2,3},{3,2},{4,5},{5,4},{6,7},{7,6},{8,9},{9,8},{10,11... | collective-permute-start | bytes 294920 | tf_op jit(solution)/shard_map/ppermute | solution.py:695
  3.6 6.6 %collective-permute-start.3 = (f32[520,128]{1,0:T(8,128)S(1)}, f32[520,128]{1,0:T(8,128)S(1)}, u32[]{:S(2)}, u32[]{:S(2)}) collective-permute-start(f32[520,128]{1,0:T(8,128)S(1)} %pack.1.own.own_ref), channel_id=1, source_target_pairs={{0,8},{1,2},{2,1},{3,11},{4,5},{5,7},{6,4},{7,6},{8,0},{9,10},{10,... | collective-permute-start | bytes 798728 | tf_op jit(solution)/shard_map/ppermute | solution.py:695
  5.3 4.9 %collective-permute-start.2 = (f32[520,128]{1,0:T(8,128)S(1)}, f32[520,128]{1,0:T(8,128)S(1)}, u32[]{:S(2)}, u32[]{:S(2)}) collective-permute-start(f32[520,128]{1,0:T(8,128)S(1)} %pack.1.own.own_ref), channel_id=1, source_target_pairs={{0,1},{1,0},{2,3},{3,2},{4,5},{5,4},{6,7},{7,6},{8,9},{9,8},{10,11... | collective-permute-start | bytes 798728 | tf_op jit(solution)/shard_map/ppermute | solution.py:695
  5.6 6.2 %collective-permute-start.4 = (f32[136,128]{1,0:T(8,128)S(1)}, f32[136,128]{1,0:T(8,128)S(1)}, u32[]{:S(2)}, u32[]{:S(2)}) collective-permute-start(f32[136,128]{1,0:T(8,128)S(1)} %face.1), channel_id=1, source_target_pairs={{0,5},{1,4},{2,7},{3,6},{4,1},{5,0},{6,3},{7,2},{8,13},{9,12},{10,... | collective-permute-start | bytes 208904 | tf_op jit(solution)/shard_map/ppermute | solution.py:695
  5.6 6.1 %collective-permute-start.5 = (f32[136,128]{1,0:T(8,128)S(1)}, f32[136,128]{1,0:T(8,128)S(1)}, u32[]{:S(2)}, u32[]{:S(2)}) collective-permute-start(f32[136,128]{1,0:T(8,128)S(1)} %rim.1.x_ref), channel_id=1, source_target_pairs={{0,1},{1,0},{2,3},{3,2},{4,9},{5,8},{6,11},{7,10},{8,5},{9,4},{10,... | collective-permute-start | bytes 208904 | tf_op jit(solution)/shard_map/ppermute | solution.py:695
  12.5 4.4 %collective-permute-start.6 = (f32[152,128]{1,0:T(8,128)S(1)}, f32[152,128]{1,0:T(8,128)S(1)}, u32[]{:S(2)}, u32[]{:S(2)}) collective-permute-start(f32[152,128]{1,0:T(8,128)S(1)} %get-tuple-element.100), channel_id=1, source_target_pairs={{0,5},{1,4},{2,7},{3,6},{4,1},{5,0},{6,3},{7,2},{8,13},{9,12},{10,... | collective-permute-start | bytes 233480 | tf_op jit(solution)/shard_map/ppermute | solution.py:695
  13.3 5.0 %collective-permute-start.7 = (f32[152,128]{1,0:T(8,128)S(1)}, f32[152,128]{1,0:T(8,128)S(1)}, u32[]{:S(2)}, u32[]{:S(2)}) collective-permute-start(f32[152,128]{1,0:T(8,128)S(1)} %get-tuple-element.101), channel_id=1, source_target_pairs={{0,1},{1,0},{2,3},{3,2},{4,9},{5,8},{6,11},{7,10},{8,5},{9,4},{10,... | collective-permute-start | bytes 233480 | tf_op jit(solution)/shard_map/ppermute | solution.py:695
  19.1 3.6 %collective-permute-start.8 = (f32[88,128]{1,0:T(8,128)S(1)}, f32[88,128]{1,0:T(8,128)S(1)}, u32[]{:S(2)}, u32[]{:S(2)}) collective-permute-start(f32[88,128]{1,0:T(8,128)S(1)} %get-tuple-element.116), channel_id=1, source_target_pairs={{0,5},{1,4},{2,7},{3,6},{4,1},{5,0},{6,3},{7,2},{8,13},{9,12},{10,... | collective-permute-start | bytes 135176 | tf_op jit(solution)/shard_map/ppermute | solution.py:695
  20.2 4.5 %collective-permute-start.9 = (f32[88,128]{1,0:T(8,128)S(1)}, f32[88,128]{1,0:T(8,128)S(1)}, u32[]{:S(2)}, u32[]{:S(2)}) collective-permute-start(f32[88,128]{1,0:T(8,128)S(1)} %get-tuple-element.117), channel_id=1, source_target_pairs={{0,1},{1,0},{2,3},{3,2},{4,9},{5,8},{6,11},{7,10},{8,5},{9,4},{10,... | collective-permute-start | bytes 135176 | tf_op jit(solution)/shard_map/ppermute | solution.py:695
  25.3 3.4 %collective-permute-start.10 = (f32[64,128]{1,0:T(8,128)S(1)}, f32[64,128]{1,0:T(8,128)S(1)}, u32[]{:S(2)}, u32[]{:S(2)}) collective-permute-start(f32[64,128]{1,0:T(8,128)S(1)} %get-tuple-element.132), channel_id=1, source_target_pairs={{0,5},{1,4},{2,7},{3,6},{4,1},{5,0},{6,3},{7,2},{8,13},{9,12},{10,... | collective-permute-start | bytes 98312 | tf_op jit(solution)/shard_map/ppermute | solution.py:695
  26.1 4.2 %collective-permute-start.11 = (f32[64,128]{1,0:T(8,128)S(1)}, f32[64,128]{1,0:T(8,128)S(1)}, u32[]{:S(2)}, u32[]{:S(2)}) collective-permute-start(f32[64,128]{1,0:T(8,128)S(1)} %get-tuple-element.133), channel_id=1, source_target_pairs={{0,1},{1,0},{2,3},{3,2},{4,9},{5,8},{6,11},{7,10},{8,5},{9,4},{10,... | collective-permute-start | bytes 98312 | tf_op jit(solution)/shard_map/ppermute | solution.py:695
  30.8 3.9 %collective-permute-start.13 = (f32[48,128]{1,0:T(8,128)S(1)}, f32[48,128]{1,0:T(8,128)S(1)}, u32[]{:S(2)}, u32[]{:S(2)}) collective-permute-start(f32[48,128]{1,0:T(8,128)S(1)} %get-tuple-element.156), channel_id=1, source_target_pairs={{0,4},{1,5},{2,6},{3,7},{4,0},{5,1},{6,2},{7,3},{8,12},{9,13},{10,... | collective-permute-start | bytes 73736 | tf_op jit(solution)/shard_map/ppermute | solution.py:695
  31.9 4.2 %collective-permute-start.14 = (f32[48,128]{1,0:T(8,128)S(1)}, f32[48,128]{1,0:T(8,128)S(1)}, u32[]{:S(2)}, u32[]{:S(2)}) collective-permute-start(f32[48,128]{1,0:T(8,128)S(1)} %get-tuple-element.157), channel_id=1, source_target_pairs={{0,1},{1,0},{2,3},{3,2},{4,9},{5,8},{6,11},{7,10},{8,5},{9,4},{10,... | collective-permute-start | bytes 73736 | tf_op jit(solution)/shard_map/ppermute | solution.py:695
  32.9 3.2 %collective-permute-start.12 = (f32[400,128]{1,0:T(8,128)S(1)}, f32[400,128]{1,0:T(8,128)S(1)}, u32[]{:S(2)}, u32[]{:S(2)}) collective-permute-start(f32[400,128]{1,0:T(8,128)S(1)} %between3.1.mine), channel_id=1, source_target_pairs={{0,1},{1,0},{2,3},{3,2},{4,5},{5,4},{6,7},{7,6},{8,9},{9,8},{10,11... | collective-permute-start | bytes 614408 | tf_op jit(solution)/shard_map/ppermute | solution.py:695

commit v5 on v4

--- a/solution.py
+++ b/solution.py
@@ -185,13 +185,22 @@
             out[base + n * across : base + n * across + count, :] = side(own, core, chip, at)
 
 
-def spread(sizes, own, core, chip, base, out):
+def spread(sizes, own, core, chip, base, outs):
     ny, ey, lanes = sizes
     for j in range(4):
-        at = (pl.ds(base + j, ey, stride=4), slice(None))
+        at = (pl.ds(base + j, 2 * ey, stride=4), slice(None))
         for n, side in enumerate(sides(ny)):
-            out[j, n * ey : (n + 1) * ey, :] = side(own, core, chip, at)
-        out[j, 3 * ey :, :] = jnp.zeros((ey, lanes), F32)
+            both = side(own, core, chip, at)
+            for half, out in enumerate(outs):
+                out[j, n * ey : (n + 1) * ey, :] = both[half * ey : (half + 1) * ey]
+        for out in outs:
+            out[j, 3 * ey :, :] = jnp.zeros((ey, lanes), F32)
+
+
+def spread_layers(sizes, own, core, chip, base, ends, inner):
+    tall = 4 * sizes[1]
+    spread(sizes, own, core, chip, base, (ends, inner.at[0]))
+    spread(sizes, own, core, chip, base + 2 * tall, (inner.at[1], inner.at[2]))
 
 
 def segments(low, high):
@@ -222,22 +231,14 @@
 
 
 def spread_u_kernel(sizes, own, e, o, ends, inner):
-    tall = 4 * sizes[1]
-    for c in range(3):
-        spread(sizes, own, e, o, 4 * c * tall, ends.at[c])
-        for i in range(3):
-            spread(sizes, own, e, o, (4 * c + 1 + i) * tall, inner.at[c, i])
+    for c in range(3):
+        spread_layers(sizes, own, e, o, 16 * c * sizes[1], ends.at[c], inner.at[c])
 
 
 def spread_v_kernel(sizes, start, own, e, o, v_ends, v_inner, m_ends, m_inner):
-    tall = 4 * sizes[1]
-    for c in range(3):
-        spread(sizes, own, e, o, 4 * c * tall, v_ends.at[c])
-        for i in range(3):
-            spread(sizes, own, e, o, (4 * c + 1 + i) * tall, v_inner.at[c, i])
-    spread(sizes, own, e, o, start, m_ends)
-    for i in range(3):
-        spread(sizes, own, e, o, start + (1 + i) * tall, m_inner.at[i])
+    for c in range(3):
+        spread_layers(sizes, own, e, o, 16 * c * sizes[1], v_ends.at[c], v_inner.at[c])
+    spread_layers(sizes, own, e, o, start, m_ends, m_inner)
 
 
 def tables_kernel(sizes, starts, own_ref, e_ref, o_ref, weight_ref, lame_ref, level_ref, sel):
@@ -530,16 +531,17 @@
 
 
 def start_kernel(sizes, u_ref, v_ref, m_ref, a_ref, b_ref, px, part, scale, lame, level, grad_ref, div_ref,
-                 rim_ref, new, flux_x, gx, total, send_a, send_b, flux_z, flux_y, us, gz_ends, last_z, qz):
+                 rim_ref, new, flux_x, gx, total, send_a, send_b, layer, flux_z, flux_y, us, gz_ends, last_z, qz):
     nx, ey, lanes = sizes
     even, _, last = place("px", nx)
     tall = 4 * ey
-    rim_ref[...] = jnp.zeros(rim_ref.shape, F32)
-    for c in range(3):
+    count = 12 * ey - 3
+    layer[...] = jnp.zeros(layer.shape, F32)
+    for c in range(3):
+        at = (slice(c * count, (c + 1) * count), slice(None))
+        layer[c, 0:count, :] = jnp.where(last, 0.0, jnp.where(even, a_ref[at], b_ref[at]))
         for j in range(4):
-            count = 3 * ey - (j > 0)
-            at = (pl.ds(c * (12 * ey - 3) + j, count, stride=4), slice(None))
-            rim_ref[c, j, 0:count, :] = jnp.where(last, 0.0, jnp.where(even, a_ref[at], b_ref[at]))
+            rim_ref[c, j] = layer[c, pl.ds(j, tall, stride=4), :]
     ends = [[[u_ref[c, j] for j in range(4)], [rim_ref[c, j] for j in range(4)]] for c in range(3)]
     stresses(tall, (0, 0), None, ends, px, part, scale, lame, level, None, new, flux_x, gx, flux_z, flux_y, us, gz_ends, last_z, qz,
              grad_ref, div_ref, total)
@@ -653,7 +655,7 @@
     out[...] = jnp.where(first, 0.0, jnp.where(even, b_ref[...], a_ref[...]))
 
 
-def end_kernel(sizes, mine, core, force_ref, u_out, v_out):
+def end_kernel(sizes, mine, core, force_ref, u_out, v_out, layer):
     nx, ey, lanes = sizes
     even, _, _ = place("px", nx)
 
@@ -666,8 +668,10 @@
             rows = (slice((4 * c + j) * ey, (4 * c + j + 1) * ey), slice(None))
             mass = at(final_rows(ey, 4, 0), j)
             speed = at(final_rows(ey, 3, c), j) - time_step * mass * force_ref[rows]
-            v_out[c, 0, pl.ds(j, ey, stride=4), :] = speed
-            u_out[c, 0, pl.ds(j, ey, stride=4), :] = at(final_rows(ey, 2, c), j) + time_step * speed
+            layer[3 + c, pl.ds(j, ey, stride=4), :] = speed
+            layer[c, pl.ds(j, ey, stride=4), :] = at(final_rows(ey, 2, c), j) + time_step * speed
+        u_out[c, 0] = layer[c, : 4 * ey, :]
+        v_out[c, 0] = layer[3 + c, : 4 * ey, :]
         for i in range(3):
             u_out[c, 1 + i] = at(final_rows(ey, 0, c, i))
             v_out[c, 1 + i] = at(final_rows(ey, 1, c, i))
@@ -754,7 +758,7 @@
     rim_u, old_ends, flux_x, gx, total, send_a, send_b = call(
         functools.partial(start_kernel, sizes_x), "stress0",
         [shape(3, 4), shape(6, 2, 10), shape(3, 25), shape(3, 25), shape(3, 2, 4), message, message],
-        ends_scratch(tall),
+        [(3, 4 * tall, lanes)] + ends_scratch(tall),
         u_ends, v_ends, m_ends, rim_a, rim_b, *near, *tables,
     )
     got_a, got_b = along_x(send_a, send_b)
@@ -807,12 +811,12 @@
     got_a, got_b = move("home", send_a), move("far", send_b)
     (results,) = call(
         functools.partial(between_kernel, mine, True, newest, (ey - 2, 0), False, None, None), "between3",
-        [(25 * ey4, lanes)], between_scratch(short, 0),
+        [(26 * ey4, lanes)], between_scratch(short, 0),
         flux_x, gx, gz, gy, u_inner, v_inner, m_inner, old_inner, *tables, u_ends, v_ends, m_ends, total,
     )
     (force,) = call(functools.partial(pick_kernel, nx), "pick", [message], [], got_a, got_b, cost=long)
     return tuple(call(
-        functools.partial(end_kernel, sizes_x), "end", [displacement.shape, velocity.shape], [],
+        functools.partial(end_kernel, sizes_x), "end", [displacement.shape, velocity.shape], [(6, 2 * ey4, lanes)],
         results, move("core", results), force,
     ))
 

time: 37.3 us -> 37.4 us (level)
  transfers between devices with their start and end apart: 15 -> 15, of which waited for: 10 -> 10; matrix products, arithmetic and copies ran while one was open for 0% -> 0% of each run, Pallas kernels for 17% -> 16%
where the time goes in v5:
time: 37.4 us; the launch traced here: 36.8 us
  waiting for transfers between devices  15.4 us (41%)
  starting transfers between devices  11.4 us (30%)
  Pallas kernels  9.35 us (25%)
  between operations  0.76 us (2%)
    ppermute x15, waiting for transfers between devices, move(): return lax.ppermute(x, ('px', 'py'), pairs_of(kind, nx, ny))  15.4 us
    ppermute x15, starting transfers between devices, move(): return lax.ppermute(x, ('px', 'py'), pairs_of(kind, nx, ny))  11.4 us
    pallas_call x17, Pallas kernels, call(): pl.pallas_call(kernel, out_shape=shapes, scratch_shapes=[pltpu.VMEM(s, F3...  8.07 us
    pallas_call x1, Pallas kernels, shards(): pl.pallas_call(functools.partial(load_kernel, len(sources)), out_shape=[p...  1.27 us
  transfers between devices with their start and end apart: 15, of which 10 were waited for; matrix products, arithmetic and copies ran while one was open for 0% of the time, Pallas kernels for 16%

profile of v5, /device:TPU:16, one launch (start us, length us, event | category | flops | bytes accessed | tf_op | source)
XLA Modules:
  0.0 36.8 jit_solution(7159456127894483691)
XLA Ops:
  0.6 1.6 %collective-permute-start.1 = (f32[192,128]{1,0:T(8,128)}, f32[192,128]{1,0:T(8,128)S(1)}, u32[]{:S(2)}, u32[]{:S(2)}) collective-permute-start(f32[192,128]{1,0:T(8,128)} %bitcast.4), channel_id=1, source_target_pairs={{0,8},{1,2},{2,1},{3,11},{4,5},{5,7},{6,4},{7,6},{8,0},{9,10},{10,... | collective-permute-start | bytes 294920 | tf_op jit(solution)/shard_map/ppermute | solution.py:699
  2.3 1.3 %load.1 = (f32[192,128]{1,0:T(8,128)S(1)}, f32[192,128]{1,0:T(8,128)S(1)}, f32[64,128]{1,0:T(8,128)S(1)}, f32[5,5,5,1,128]{4,3,2,1,0:T(1,128)S(1)}, f32[5,5,5,1,...) custom-call(f32[192,128]{1,0:T(8,128)} %bitcast.6, ...), custom_call_target="tpu_custom_call" | custom-call | tf_op jit(solution)/shard_map/load/pallas_call | solution.py:712
  3.6 1.6 %collective-permute-start.3 = (f32[520,128]{1,0:T(8,128)S(1)}, f32[520,128]{1,0:T(8,128)S(1)}, u32[]{:S(2)}, u32[]{:S(2)}) collective-permute-start(f32[520,128]{1,0:T(8,128)S(1)} %pack.1.own.own_ref), channel_id=1, source_target_pairs={{0,8},{1,2},{2,1},{3,11},{4,5},{5,7},{6,4},{7,6},{8,0},{9,10},{10,... | collective-permute-start | bytes 798728 | tf_op jit(solution)/shard_map/ppermute | solution.py:699
  5.6 1.6 %collective-permute-start.5 = (f32[136,128]{1,0:T(8,128)S(1)}, f32[136,128]{1,0:T(8,128)S(1)}, u32[]{:S(2)}, u32[]{:S(2)}) collective-permute-start(f32[136,128]{1,0:T(8,128)S(1)} %rim.1.x_ref), channel_id=1, source_target_pairs={{0,1},{1,0},{2,3},{3,2},{4,9},{5,8},{6,11},{7,10},{8,5},{9,4},{10,... | collective-permute-start | bytes 208904 | tf_op jit(solution)/shard_map/ppermute | solution.py:699
  7.3 2.9 %collective-permute-done.3.o.o_ref = f32[520,128]{1,0:T(8,128)S(1)} collective-permute-done((f32[520,128]{1,0:T(8,128)S(1)}, f32[520,128]{1,0:T(8,128)S(1)}, u32[]{:S(2)}, u32[]{:S(2)}) %collective-permute-start.3) | collective-permute-done | bytes 266272 | tf_op jit(solution)/shard_map/ppermute | solution.py:699
  10.2 1.0 %tables.1 = (f32[2,2,25,16,128]{4,3,2,1,0:T(8,128)S(1)}, f32[2,16,128]{2,1,0:T(8,128)S(1)}) custom-call(f32[520,128]{1,0:T(8,128)S(1)} %pack.1.own.own_ref, f32[520,128]{1,0:T(8,128)S(1)} %collective-permute-done.2.e.e_ref, f32[520,128]{1,0:T(8,128)S(1)} %collective-permute-done.3.o.o_ref, f32[50,128]{1,0:T(8,128)S(1)} %get-tuple-element.90.weight_ref), custom_call_target="tpu_custom_call" | custom-call | tf_op jit(solution)/shard_map/tables/pallas_call | solution.py:682
  11.2 0.4 %before0.1 = (f32[45,16,256]{2,1,0:T(8,128)S(1)}, f32[3,15,16,128]{3,2,1,0:T(8,128)S(1)}, f32[3,25,16,128]{3,2,1,0:T(8,128)S(1)}, f32[3,15,16,128]{3,2,1,0:T(8,128)S(1)}, f32[2,15,16,128]{3,2,1,0:T(8,128)S(1)}) custom-call(f32[3,3,4,16,128]{4,3,2,1,0:T(8,128)S(1)} %get-tuple-element.89.u_inner.u_ref, f32[2,2,25,16,128]{4,3,2,1,0:T(8,128)S(1)} %get-tuple-element.91.lame, ...), custom_call_target="tpu_custom_call" | custom-call | tf_op jit(solution)/shard_map/before0/pallas_call | solution.py:682
  11.7 0.7 %stress0.1 = (f32[3,4,16,128]{3,2,1,0:T(8,128)S(1)}, f32[6,2,10,16,128]{4,3,2,1,0:T(8,128)S(1)}, f32[3,25,16,128]{3,2,1,0:T(8,128)S(1)}, f32[3,25,16,128]{3,2,1,...) custom-call(f32[3,4,16,128]{3,2,1,0:T(8,128)S(1)} %get-tuple-element.81.u_ref, ...), custom_call_target="tpu_custom_call" | custom-call | tf_op jit(solution)/shard_map/stress0/pallas_call | solution.py:682
  12.4 0.9 %collective-permute-start.6 = (f32[152,128]{1,0:T(8,128)S(1)}, f32[152,128]{1,0:T(8,128)S(1)}, u32[]{:S(2)}, u32[]{:S(2)}) collective-permute-start(f32[152,128]{1,0:T(8,128)S(1)} %get-tuple-element.100), channel_id=1, source_target_pairs={{0,5},{1,4},{2,7},{3,6},{4,1},{5,0},{6,3},{7,2},{8,13},{9,12},{10,... | collective-permute-start | bytes 233480 | tf_op jit(solution)/shard_map/ppermute | solution.py:699
  13.3 0.7 %collective-permute-start.7 = (f32[152,128]{1,0:T(8,128)S(1)}, f32[152,128]{1,0:T(8,128)S(1)}, u32[]{:S(2)}, u32[]{:S(2)}) collective-permute-start(f32[152,128]{1,0:T(8,128)S(1)} %get-tuple-element.101), channel_id=1, source_target_pairs={{0,1},{1,0},{2,3},{3,2},{4,9},{5,8},{6,11},{7,10},{8,5},{9,4},{10,... | collective-permute-start | bytes 233480 | tf_op jit(solution)/shard_map/ppermute | solution.py:699
  14.0 1.2 %between0.1 = (f32[3,3,4,16,128]{4,3,2,1,0:T(8,128)S(1)}, f32[3,3,4,16,128]{4,3,2,1,0:T(8,128)S(1)}, f32[3,4,16,128]{3,2,1,0:T(8,128)S(1)}, f32[45,16,256]{2,1,0...) custom-call(f32[3,25,16,128]{3,2,1,0:T(8,128)S(1)} %get-tuple-elemen, ...), custom_call_target="tpu_custom_call" | custom-call | tf_op jit(solution)/shard_map/between0/pallas_call | solution.py:682
  15.2 1.6 %collective-permute-done.6.a_ref = f32[152,128]{1,0:T(8,128)S(1)} collective-permute-done((f32[152,128]{1,0:T(8,128)S(1)}, f32[152,128]{1,0:T(8,128)S(1)}, u32[]{:S(2)}, u32[]{:S(2)}) %collective-permute-start.6) | collective-permute-done | bytes 77856 | tf_op jit(solution)/shard_map/ppermute | solution.py:699
  16.9 1.4 %collective-permute-done.7.b_ref = f32[152,128]{1,0:T(8,128)S(1)} collective-permute-done((f32[152,128]{1,0:T(8,128)S(1)}, f32[152,128]{1,0:T(8,128)S(1)}, u32[]{:S(2)}, u32[]{:S(2)}) %collective-permute-start.7) | collective-permute-done | bytes 77856 | tf_op jit(solution)/shard_map/ppermute | solution.py:699
  18.3 0.8 %stress1.1 = (f32[3,2,4,8,128]{4,3,2,1,0:T(8,128)S(1)}, f32[3,2,4,8,128]{4,3,2,1,0:T(8,128)S(1)}, f32[2,4,8,128]{3,2,1,0:T(8,128)S(1)}, f32[3,25,16,128]{3,2,1,0...) custom-call(f32[3,4,16,128]{3,2,1,0:T(8,128)S(1)} %get-tuple-element, ...), custom_call_target="tpu_custom_call" | custom-call | tf_op jit(solution)/shard_map/stress1/pallas_call | solution.py:682
  19.1 1.1 %collective-permute-start.8 = (f32[88,128]{1,0:T(8,128)S(1)}, f32[88,128]{1,0:T(8,128)S(1)}, u32[]{:S(2)}, u32[]{:S(2)}) collective-permute-start(f32[88,128]{1,0:T(8,128)S(1)} %get-tuple-element.116), channel_id=1, source_target_pairs={{0,5},{1,4},{2,7},{3,6},{4,1},{5,0},{6,3},{7,2},{8,13},{9,12},{10,... | collective-permute-start | bytes 135176 | tf_op jit(solution)/shard_map/ppermute | solution.py:699
  20.3 0.9 %between1.1 = (f32[3,3,4,8,128]{4,3,2,1,0:T(8,128)S(1)}, f32[3,3,4,8,128]{4,3,2,1,0:T(8,128)S(1)}, f32[3,4,8,128]{3,2,1,0:T(8,128)S(1)}, f32[45,8,256]{2,1,0:T(8...) custom-call(f32[3,25,16,128]{3,2,1,0:T(8,128)S(1)} %get-tuple-elemen, ...), custom_call_target="tpu_custom_call" | custom-call | tf_op jit(solution)/shard_map/between1/pallas_call | solution.py:682
  21.2 1.5 %collective-permute-done.8.a_ref = f32[88,128]{1,0:T(8,128)S(1)} collective-permute-done((f32[88,128]{1,0:T(8,128)S(1)}, f32[88,128]{1,0:T(8,128)S(1)}, u32[]{:S(2)}, u32[]{:S(2)}) %collective-permute-start.8) | collective-permute-done | bytes 45088 | tf_op jit(solution)/shard_map/ppermute | solution.py:699
  22.7 2.0 %collective-permute-done.9.b_ref = f32[88,128]{1,0:T(8,128)S(1)} collective-permute-done((f32[88,128]{1,0:T(8,128)S(1)}, f32[88,128]{1,0:T(8,128)S(1)}, u32[]{:S(2)}, u32[]{:S(2)}) %collective-permute-start.9) | collective-permute-done | bytes 45088 | tf_op jit(solution)/shard_map/ppermute | solution.py:699
  24.7 0.5 %stress2.1 = (f32[3,2,4,8,128]{4,3,2,1,0:T(8,128)S(1)}, f32[3,2,4,8,128]{4,3,2,1,0:T(8,128)S(1)}, f32[6,2,10,8,128]{4,3,2,1,0:T(8,128)S(1)}, f32[3,25,8,128]{3,2...) custom-call(f32[3,2,4,8,128]{4,3,2,1,0:T(8,128)S(1)} %get-tuple-elem, ...), custom_call_target="tpu_custom_call" | custom-call | tf_op jit(solution)/shard_map/stress2/pallas_call | solution.py:682
  25.2 0.8 %collective-permute-start.10 = (f32[64,128]{1,0:T(8,128)S(1)}, f32[64,128]{1,0:T(8,128)S(1)}, u32[]{:S(2)}, u32[]{:S(2)}) collective-permute-start(f32[64,128]{1,0:T(8,128)S(1)} %get-tuple-element.132), channel_id=1, source_target_pairs={{0,5},{1,4},{2,7},{3,6},{4,1},{5,0},{6,3},{7,2},{8,13},{9,12},{10,... | collective-permute-start | bytes 98312 | tf_op jit(solution)/shard_map/ppermute | solution.py:699
  26.1 0.7 %collective-permute-start.11 = (f32[64,128]{1,0:T(8,128)S(1)}, f32[64,128]{1,0:T(8,128)S(1)}, u32[]{:S(2)}, u32[]{:S(2)}) collective-permute-start(f32[64,128]{1,0:T(8,128)S(1)} %get-tuple-element.133), channel_id=1, source_target_pairs={{0,1},{1,0},{2,3},{3,2},{4,9},{5,8},{6,11},{7,10},{8,5},{9,4},{10,... | collective-permute-start | bytes 98312 | tf_op jit(solution)/shard_map/ppermute | solution.py:699
  26.7 0.8 %between2.1 = (f32[3,3,4,8,128]{4,3,2,1,0:T(8,128)S(1)}, f32[3,3,4,8,128]{4,3,2,1,0:T(8,128)S(1)}, f32[3,4,8,128]{3,2,1,0:T(8,128)S(1)}, f32[45,8,256]{2,1,0:T(8...) custom-call(f32[3,25,8,128]{3,2,1,0:T(8,128)S(1)} %get-tuple-element, ...), custom_call_target="tpu_custom_call" | custom-call | tf_op jit(solution)/shard_map/between2/pallas_call | solution.py:682
  27.5 1.1 %collective-permute-done.10.a_ref = f32[64,128]{1,0:T(8,128)S(1)} collective-permute-done((f32[64,128]{1,0:T(8,128)S(1)}, f32[64,128]{1,0:T(8,128)S(1)}, u32[]{:S(2)}, u32[]{:S(2)}) %collective-permute-start.10) | collective-permute-done | bytes 32800 | tf_op jit(solution)/shard_map/ppermute | solution.py:699
  28.6 1.7 %collective-permute-done.11.b_ref = f32[64,128]{1,0:T(8,128)S(1)} collective-permute-done((f32[64,128]{1,0:T(8,128)S(1)}, f32[64,128]{1,0:T(8,128)S(1)}, u32[]{:S(2)}, u32[]{:S(2)}) %collective-permute-start.11) | collective-permute-done | bytes 32800 | tf_op jit(solution)/shard_map/ppermute | solution.py:699
  30.3 0.5 %stress3.1 = (f32[3,2,4,8,128]{4,3,2,1,0:T(8,128)S(1)}, f32[3,2,4,8,128]{4,3,2,1,0:T(8,128)S(1)}, f32[3,25,8,128]{3,2,1,0:T(8,128)S(1)}, f32[3,25,8,128]{3,2,1,0...) custom-call(f32[3,2,4,8,128]{4,3,2,1,0:T(8,128)S(1)} %get-tuple-element.129.u_ref, ...), custom_call_target="tpu_custom_call" | custom-call | tf_op jit(solution)/shard_map/stress3/pallas_call | solution.py:682
  30.8 1.1 %collective-permute-start.13 = (f32[48,128]{1,0:T(8,128)S(1)}, f32[48,128]{1,0:T(8,128)S(1)}, u32[]{:S(2)}, u32[]{:S(2)}) collective-permute-start(f32[48,128]{1,0:T(8,128)S(1)} %get-tuple-element.156), channel_id=1, source_target_pairs={{0,4},{1,5},{2,6},{3,7},{4,0},{5,1},{6,2},{7,3},{8,12},{9,13},{10,... | collective-permute-start | bytes 73736 | tf_op jit(solution)/shard_map/ppermute | solution.py:699
  31.9 0.6 %collective-permute-start.14 = (f32[48,128]{1,0:T(8,128)S(1)}, f32[48,128]{1,0:T(8,128)S(1)}, u32[]{:S(2)}, u32[]{:S(2)}) collective-permute-start(f32[48,128]{1,0:T(8,128)S(1)} %get-tuple-element.157), channel_id=1, source_target_pairs={{0,1},{1,0},{2,3},{3,2},{4,9},{5,8},{6,11},{7,10},{8,5},{9,4},{10,... | collective-permute-start | bytes 73736 | tf_op jit(solution)/shard_map/ppermute | solution.py:699
  32.5 0.4 %between3.1.mine = f32[416,128]{1,0:T(8,128)S(1)} custom-call(f32[3,25,8,128]{3,2,1,0:T(8,128)S(1)} %get-tuple-element.145.flux_x, f32[3,25,8,128]{3,2,1,0:T(8,128)S(1)} %get-tuple-element.146.gx, f32[45,8,256]{2,1,0:T(8,128)S(1)} %get-tuple-element.147.gz, f32[3,15,8,128]{3,2,1,0:T(8,128)S(1)} %get-tuple-element.148.gy, ...), custom_call_target="tpu_custom_call" | custom-call | tf_op jit(solution)/shard_map/between3/pallas_call | solution.py:682
  32.9 0.3 collective-permute-start.12
  33.3 1.4 %collective-permute-done.13.a_ref = f32[48,128]{1,0:T(8,128)S(1)} collective-permute-done((f32[48,128]{1,0:T(8,128)S(1)}, f32[48,128]{1,0:T(8,128)S(1)}, u32[]{:S(2)}, u32[]{:S(2)}) %collective-permute-start.13) | collective-permute-done | bytes 24608 | tf_op jit(solution)/shard_map/ppermute | solution.py:699
  34.7 1.4 %collective-permute-done.14.b_ref = f32[48,128]{1,0:T(8,128)S(1)} collective-permute-done((f32[48,128]{1,0:T(8,128)S(1)}, f32[48,128]{1,0:T(8,128)S(1)}, u32[]{:S(2)}, u32[]{:S(2)}) %collective-permute-start.14) | collective-permute-done | bytes 24608 | tf_op jit(solution)/shard_map/ppermute | solution.py:699
  36.1 0.7 %end.1 = (f32[3,4,16,128]{3,2,1,0:T(8,128)}, f32[3,4,16,128]{3,2,1,0:T(8,128)}) custom-call(f32[416,128]{1,0:T(8,128)S(1)} %between3.1.mine, f32[416,128]{1,0:T(8,128)S(1)} %collective-permute-done.12.core, f32[48,128]{1,0:T(8,128)S(1)} %pick.1.force_ref), custom_call_target="tpu_custom_call" | custom-call | tf_op jit(solution)/shard_map/end/pallas_call | solution.py:682
  (16 shorter events, 0.6 us)
Async XLA Ops:
  0.6 4.9 %collective-permute-start.1 = (f32[192,128]{1,0:T(8,128)}, f32[192,128]{1,0:T(8,128)S(1)}, u32[]{:S(2)}, u32[]{:S(2)}) collective-permute-start(f32[192,128]{1,0:T(8,128)} %bitcast.4), channel_id=1, source_target_pairs={{0,8},{1,2},{2,1},{3,11},{4,5},{5,7},{6,4},{7,6},{8,0},{9,10},{10,... | collective-permute-start | bytes 294920 | tf_op jit(solution)/shard_map/ppermute | solution.py:699
  2.3 3.3 %collective-permute-start = (f32[192,128]{1,0:T(8,128)}, f32[192,128]{1,0:T(8,128)S(1)}, u32[]{:S(2)}, u32[]{:S(2)}) collective-permute-start(f32[192,128]{1,0:T(8,128)} %bitcast.5), channel_id=1, source_target_pairs={{0,1},{1,0},{2,3},{3,2},{4,5},{5,4},{6,7},{7,6},{8,9},{9,8},{10,11... | collective-permute-start | bytes 294920 | tf_op jit(solution)/shard_map/ppermute | solution.py:699
  3.6 6.6 %collective-permute-start.3 = (f32[520,128]{1,0:T(8,128)S(1)}, f32[520,128]{1,0:T(8,128)S(1)}, u32[]{:S(2)}, u32[]{:S(2)}) collective-permute-start(f32[520,128]{1,0:T(8,128)S(1)} %pack.1.own.own_ref), channel_id=1, source_target_pairs={{0,8},{1,2},{2,1},{3,11},{4,5},{5,7},{6,4},{7,6},{8,0},{9,10},{10,... | collective-permute-start | bytes 798728 | tf_op jit(solution)/shard_map/ppermute | solution.py:699
  5.3 4.9 %collective-permute-start.2 = (f32[520,128]{1,0:T(8,128)S(1)}, f32[520,128]{1,0:T(8,128)S(1)}, u32[]{:S(2)}, u32[]{:S(2)}) collective-permute-start(f32[520,128]{1,0:T(8,128)S(1)} %pack.1.own.own_ref), channel_id=1, source_target_pairs={{0,1},{1,0},{2,3},{3,2},{4,5},{5,4},{6,7},{7,6},{8,9},{9,8},{10,11... | collective-permute-start | bytes 798728 | tf_op jit(solution)/shard_map/ppermute | solution.py:699
  5.6 6.1 %collective-permute-start.4 = (f32[136,128]{1,0:T(8,128)S(1)}, f32[136,128]{1,0:T(8,128)S(1)}, u32[]{:S(2)}, u32[]{:S(2)}) collective-permute-start(f32[136,128]{1,0:T(8,128)S(1)} %face.1), channel_id=1, source_target_pairs={{0,5},{1,4},{2,7},{3,6},{4,1},{5,0},{6,3},{7,2},{8,13},{9,12},{10,... | collective-permute-start | bytes 208904 | tf_op jit(solution)/shard_map/ppermute | solution.py:699
  5.6 6.0 %collective-permute-start.5 = (f32[136,128]{1,0:T(8,128)S(1)}, f32[136,128]{1,0:T(8,128)S(1)}, u32[]{:S(2)}, u32[]{:S(2)}) collective-permute-start(f32[136,128]{1,0:T(8,128)S(1)} %rim.1.x_ref), channel_id=1, source_target_pairs={{0,1},{1,0},{2,3},{3,2},{4,9},{5,8},{6,11},{7,10},{8,5},{9,4},{10,... | collective-permute-start | bytes 208904 | tf_op jit(solution)/shard_map/ppermute | solution.py:699
  12.4 4.5 %collective-permute-start.6 = (f32[152,128]{1,0:T(8,128)S(1)}, f32[152,128]{1,0:T(8,128)S(1)}, u32[]{:S(2)}, u32[]{:S(2)}) collective-permute-start(f32[152,128]{1,0:T(8,128)S(1)} %get-tuple-element.100), channel_id=1, source_target_pairs={{0,5},{1,4},{2,7},{3,6},{4,1},{5,0},{6,3},{7,2},{8,13},{9,12},{10,... | collective-permute-start | bytes 233480 | tf_op jit(solution)/shard_map/ppermute | solution.py:699
  13.3 5.0 %collective-permute-start.7 = (f32[152,128]{1,0:T(8,128)S(1)}, f32[152,128]{1,0:T(8,128)S(1)}, u32[]{:S(2)}, u32[]{:S(2)}) collective-permute-start(f32[152,128]{1,0:T(8,128)S(1)} %get-tuple-element.101), channel_id=1, source_target_pairs={{0,1},{1,0},{2,3},{3,2},{4,9},{5,8},{6,11},{7,10},{8,5},{9,4},{10,... | collective-permute-start | bytes 233480 | tf_op jit(solution)/shard_map/ppermute | solution.py:699
  19.1 3.6 %collective-permute-start.8 = (f32[88,128]{1,0:T(8,128)S(1)}, f32[88,128]{1,0:T(8,128)S(1)}, u32[]{:S(2)}, u32[]{:S(2)}) collective-permute-start(f32[88,128]{1,0:T(8,128)S(1)} %get-tuple-element.116), channel_id=1, source_target_pairs={{0,5},{1,4},{2,7},{3,6},{4,1},{5,0},{6,3},{7,2},{8,13},{9,12},{10,... | collective-permute-start | bytes 135176 | tf_op jit(solution)/shard_map/ppermute | solution.py:699
  20.2 4.5 %collective-permute-start.9 = (f32[88,128]{1,0:T(8,128)S(1)}, f32[88,128]{1,0:T(8,128)S(1)}, u32[]{:S(2)}, u32[]{:S(2)}) collective-permute-start(f32[88,128]{1,0:T(8,128)S(1)} %get-tuple-element.117), channel_id=1, source_target_pairs={{0,1},{1,0},{2,3},{3,2},{4,9},{5,8},{6,11},{7,10},{8,5},{9,4},{10,... | collective-permute-start | bytes 135176 | tf_op jit(solution)/shard_map/ppermute | solution.py:699
  25.2 3.4 %collective-permute-start.10 = (f32[64,128]{1,0:T(8,128)S(1)}, f32[64,128]{1,0:T(8,128)S(1)}, u32[]{:S(2)}, u32[]{:S(2)}) collective-permute-start(f32[64,128]{1,0:T(8,128)S(1)} %get-tuple-element.132), channel_id=1, source_target_pairs={{0,5},{1,4},{2,7},{3,6},{4,1},{5,0},{6,3},{7,2},{8,13},{9,12},{10,... | collective-permute-start | bytes 98312 | tf_op jit(solution)/shard_map/ppermute | solution.py:699
  26.1 4.2 %collective-permute-start.11 = (f32[64,128]{1,0:T(8,128)S(1)}, f32[64,128]{1,0:T(8,128)S(1)}, u32[]{:S(2)}, u32[]{:S(2)}) collective-permute-start(f32[64,128]{1,0:T(8,128)S(1)} %get-tuple-element.133), channel_id=1, source_target_pairs={{0,1},{1,0},{2,3},{3,2},{4,9},{5,8},{6,11},{7,10},{8,5},{9,4},{10,... | collective-permute-start | bytes 98312 | tf_op jit(solution)/shard_map/ppermute | solution.py:699
  30.8 3.9 %collective-permute-start.13 = (f32[48,128]{1,0:T(8,128)S(1)}, f32[48,128]{1,0:T(8,128)S(1)}, u32[]{:S(2)}, u32[]{:S(2)}) collective-permute-start(f32[48,128]{1,0:T(8,128)S(1)} %get-tuple-element.156), channel_id=1, source_target_pairs={{0,4},{1,5},{2,6},{3,7},{4,0},{5,1},{6,2},{7,3},{8,12},{9,13},{10,... | collective-permute-start | bytes 73736 | tf_op jit(solution)/shard_map/ppermute | solution.py:699
  31.9 4.2 %collective-permute-start.14 = (f32[48,128]{1,0:T(8,128)S(1)}, f32[48,128]{1,0:T(8,128)S(1)}, u32[]{:S(2)}, u32[]{:S(2)}) collective-permute-start(f32[48,128]{1,0:T(8,128)S(1)} %get-tuple-element.157), channel_id=1, source_target_pairs={{0,1},{1,0},{2,3},{3,2},{4,9},{5,8},{6,11},{7,10},{8,5},{9,4},{10,... | collective-permute-start | bytes 73736 | tf_op jit(solution)/shard_map/ppermute | solution.py:699
  32.9 3.2 %collective-permute-start.12 = (f32[416,128]{1,0:T(8,128)S(1)}, f32[416,128]{1,0:T(8,128)S(1)}, u32[]{:S(2)}, u32[]{:S(2)}) collective-permute-start(f32[416,128]{1,0:T(8,128)S(1)} %between3.1.mine), channel_id=1, source_target_pairs={{0,1},{1,0},{2,3},{3,2},{4,5},{5,4},{6,7},{7,6},{8,9},{9,8},{10,11... | collective-permute-start | bytes 638984 | tf_op jit(solution)/shard_map/ppermute | solution.py:699

commit v6 on v4

--- a/solution.py
+++ b/solution.py
@@ -362,16 +362,25 @@
                 scale[n, p, at, :] = sums[0][3 + n] + sums[1][3 + n]
 
 
-def stresses(tall, windows, keep, ends, px, part, scale, lame, level, old, new, flux_x, gx, flux_z, flux_y, us, gz_ends, last_z, qz, grad_ref, div_ref, total):
+def stresses(tall, windows, keep, ends, px, part, scale, lame, level, old, new, flux_x, gx, flux_z, flux_y, us, gz_ends, last_z, qz, grad_ref, div_ref, total, known=None):
     lanes = px.shape[-1]
     points = [[five(ends[c][side]) for side in range(2)] for c in range(3)]
     for c in range(3):
         for side in range(2):
             for j in range(4):
-                us[8 * c + 4 * side + j] = points[c][side][j]
+                if known is None:
+                    us[8 * c + 4 * side + j] = points[c][side][j]
+                elif side == 1:
+                    us[4 * c + j] = points[c][side][j]
     grad_z(us, grad_ref, gz_ends)
+
+    def along_z(c, side, j):
+        if known is None:
+            return gz_ends.at[8 * c + 4 * side + j]
+        return (gz_ends if side else known).at[4 * c + j]
+
     for n in range(6):
-        last_z[n] = rolled(gz_ends[4 * n], -1)
+        last_z[n] = rolled(along_z(n // 2, n % 2, 0)[...], -1)
     for c in range(3):
         for j in range(5):
             y = apply5_ends(D, points[c][0][j], points[c][1][j], [px[c, 5 * i + j] for i in range(5)])
@@ -396,7 +405,7 @@
                 for e in range(2):
                     span = slice(e * lanes, (e + 1) * lanes)
                     if j < 4:
-                        z = [gz_ends[8 * c + 4 * side + j, at, span] for c in range(3)]
+                        z = [along_z(c, side, j)[at, span] for c in range(3)]
                     else:
                         z = [last_z[2 * c + side, at, span] for c in range(3)]
                     if e == 1:
@@ -442,8 +451,12 @@
                 put(c, n, j, z[j])
 
 
-def first_kernel(u_inner, lame, grad_ref, gz, gy, px, part, scale, us):
+def first_kernel(u_ends, u_inner, lame, grad_ref, gz, gy, px, part, scale, gz_ends, us, us_ends):
     tall = u_inner.shape[3]
+    for c in range(3):
+        for j in range(4):
+            us_ends[4 * c + j] = u_ends[c, j]
+    grad_z(us_ends, grad_ref, gz_ends)
     inner = [[[u_inner[c, i, j] for j in range(4)] for i in range(3)] for c in range(3)]
     before(inner, tall, 0, None, lame, None, None, 0, grad_ref, gz, gy, px, part, scale, us)
 
@@ -529,7 +542,7 @@
     return level_of > LEVELS - 2.5
 
 
-def start_kernel(sizes, u_ref, v_ref, m_ref, a_ref, b_ref, px, part, scale, lame, level, grad_ref, div_ref,
+def start_kernel(sizes, known, u_ref, v_ref, m_ref, a_ref, b_ref, px, part, scale, lame, level, grad_ref, div_ref,
                  rim_ref, new, flux_x, gx, total, send_a, send_b, flux_z, flux_y, us, gz_ends, last_z, qz):
     nx, ey, lanes = sizes
     even, _, last = place("px", nx)
@@ -542,7 +555,7 @@
             rim_ref[c, j, 0:count, :] = jnp.where(last, 0.0, jnp.where(even, a_ref[at], b_ref[at]))
     ends = [[[u_ref[c, j] for j in range(4)], [rim_ref[c, j] for j in range(4)]] for c in range(3)]
     stresses(tall, (0, 0), None, ends, px, part, scale, lame, level, None, new, flux_x, gx, flux_z, flux_y, us, gz_ends, last_z, qz,
-             grad_ref, div_ref, total)
+             grad_ref, div_ref, total, known)
     low, high = 1, 3 * ey - 2
     for c in range(3):
 
@@ -728,9 +741,9 @@
         points = functools.partial(shape, rows=rows)
         return [(45, rows, 2 * lanes), points(3, 15), points(3, 25), points(3, 15), points(2, 15)]
 
-    def ends_scratch(rows):
+    def ends_scratch(rows, count=2):
         points = functools.partial(shape, rows=rows)
-        return [points(3, 2, 10), points(3, 10), points(24), (24, rows, 2 * lanes), (6, rows, 2 * lanes), points(3, 8)]
+        return [points(3, 2, 10), points(3, 10), points(12 * count), (12 * count, rows, 2 * lanes), (6, rows, 2 * lanes), points(3, 8)]
 
     def between_scratch(rows, rows_next):
         points = functools.partial(shape, rows=rows)
@@ -743,7 +756,10 @@
         functools.partial(tables_kernel, sizes_y, starts), "tables", [shape(2, 2, 25), shape(2)], [(3, 264, lanes)],
         own, from_e, from_o, weights,
     )
-    gz, gy, *near = call(first_kernel, "before0", near_shapes(tall), [shape(45)], u_inner, lame, gradient)
+    gz, gy, *near, known = call(
+        first_kernel, "before0", near_shapes(tall) + [(12, tall, 2 * lanes)], [shape(45), shape(12)],
+        u_ends, u_inner, lame, gradient,
+    )
     v_ends, v_inner, m_ends, m_inner = call(
         functools.partial(spread_v_kernel, sizes_y, starts[0]), "spread_v",
         [shape(3, 4), shape(3, 3, 4), shape(4), shape(3, 4)], [], own, from_e, from_o,
@@ -754,8 +770,8 @@
     rim_u, old_ends, flux_x, gx, total, send_a, send_b = call(
         functools.partial(start_kernel, sizes_x), "stress0",
         [shape(3, 4), shape(6, 2, 10), shape(3, 25), shape(3, 25), shape(3, 2, 4), message, message],
-        ends_scratch(tall),
-        u_ends, v_ends, m_ends, rim_a, rim_b, *near, *tables,
+        ends_scratch(tall, 1),
+        known, u_ends, v_ends, m_ends, rim_a, rim_b, *near, *tables,
     )
     got_a, got_b = along_x(send_a, send_b)
     every, window, mine = slice(0, tall), slice(ey - 2, 3 * ey - 2), slice(2, 2 + ey)

time: 37.3 us -> 37.2 us (level)
  no operation moved by 1% of the time
where the time goes in v6:
time: 37.2 us; the launch traced here: 36.8 us
  waiting for transfers between devices  15.4 us (41%)
  starting transfers between devices  11.2 us (30%)
  Pallas kernels  9.42 us (25%)
  between operations  0.77 us (2%)
    ppermute x15, waiting for transfers between devices, move(): return lax.ppermute(x, ('px', 'py'), pairs_of(kind, nx, ny))  15.4 us
    ppermute x15, starting transfers between devices, move(): return lax.ppermute(x, ('px', 'py'), pairs_of(kind, nx, ny))  11.2 us
    pallas_call x17, Pallas kernels, call(): pl.pallas_call(kernel, out_shape=shapes, scratch_shapes=[pltpu.VMEM(s, F3...  8.15 us
    pallas_call x1, Pallas kernels, shards(): pl.pallas_call(functools.partial(load_kernel, len(sources)), out_shape=[p...  1.27 us
  transfers between devices with their start and end apart: 15, of which 10 were waited for; matrix products, arithmetic and copies ran while one was open for 0% of the time, Pallas kernels for 17%

profile of v6, /device:TPU:16, one launch (start us, length us, event | category | flops | bytes accessed | tf_op | source)
XLA Modules:
  0.0 36.8 jit_solution(12942707264788102893)
XLA Ops:
  0.6 1.6 %collective-permute-start.1 = (f32[192,128]{1,0:T(8,128)}, f32[192,128]{1,0:T(8,128)S(1)}, u32[]{:S(2)}, u32[]{:S(2)}) collective-permute-start(f32[192,128]{1,0:T(8,128)} %bitcast.4), channel_id=1, source_target_pairs={{0,8},{1,2},{2,1},{3,11},{4,5},{5,7},{6,4},{7,6},{8,0},{9,10},{10,... | collective-permute-start | bytes 294920 | tf_op jit(solution)/shard_map/ppermute | solution.py:708
  2.3 1.3 %load.1 = (f32[192,128]{1,0:T(8,128)S(1)}, f32[192,128]{1,0:T(8,128)S(1)}, f32[64,128]{1,0:T(8,128)S(1)}, f32[5,5,5,1,128]{4,3,2,1,0:T(1,128)S(1)}, f32[5,5,5,1,...) custom-call(f32[192,128]{1,0:T(8,128)} %bitcast.6, ...), custom_call_target="tpu_custom_call" | custom-call | tf_op jit(solution)/shard_map/load/pallas_call | solution.py:721
  3.6 1.6 %collective-permute-start.3 = (f32[520,128]{1,0:T(8,128)S(1)}, f32[520,128]{1,0:T(8,128)S(1)}, u32[]{:S(2)}, u32[]{:S(2)}) collective-permute-start(f32[520,128]{1,0:T(8,128)S(1)} %pack.1.own_ref.own), channel_id=1, source_target_pairs={{0,8},{1,2},{2,1},{3,11},{4,5},{5,7},{6,4},{7,6},{8,0},{9,10},{10,... | collective-permute-start | bytes 798728 | tf_op jit(solution)/shard_map/ppermute | solution.py:708
  5.3 0.2 collective-permute-done.1.o.chip
  5.6 1.6 %collective-permute-start.5 = (f32[136,128]{1,0:T(8,128)S(1)}, f32[136,128]{1,0:T(8,128)S(1)}, u32[]{:S(2)}, u32[]{:S(2)}) collective-permute-start(f32[136,128]{1,0:T(8,128)S(1)} %rim.1.x_ref), channel_id=1, source_target_pairs={{0,1},{1,0},{2,3},{3,2},{4,9},{5,8},{6,11},{7,10},{8,5},{9,4},{10,... | collective-permute-start | bytes 208904 | tf_op jit(solution)/shard_map/ppermute | solution.py:708
  7.4 2.8 %collective-permute-done.3.o_ref.o = f32[520,128]{1,0:T(8,128)S(1)} collective-permute-done((f32[520,128]{1,0:T(8,128)S(1)}, f32[520,128]{1,0:T(8,128)S(1)}, u32[]{:S(2)}, u32[]{:S(2)}) %collective-permute-start.3) | collective-permute-done | bytes 266272 | tf_op jit(solution)/shard_map/ppermute | solution.py:708
  10.2 1.0 %tables.1 = (f32[2,2,25,16,128]{4,3,2,1,0:T(8,128)S(1)}, f32[2,16,128]{2,1,0:T(8,128)S(1)}) custom-call(f32[520,128]{1,0:T(8,128)S(1)} %pack.1.own_ref.own, f32[520,128]{1,0:T(8,128)S(1)} %collective-permute-done.2.e_ref.e, f32[520,128]{1,0:T(8,128)S(1)} %collective-permute-done.3.o_ref.o, f32[50,128]{1,0:T(8,128)S(1)} %get-tuple-element.89.weight_ref), custom_call_target="tpu_custom_call" | custom-call | tf_op jit(solution)/shard_map/tables/pallas_call | solution.py:691
  11.2 0.4 %before0.1 = (f32[45,16,256]{2,1,0:T(8,128)S(1)}, f32[3,15,16,128]{3,2,1,0:T(8,128)S(1)}, f32[3,25,16,128]{3,2,1,0:T(8,128)S(1)}, f32[3,15,16,128]{3,2,1,0:T(8,1...) custom-call(f32[3,4,16,128]{3,2,1,0:T(8,128)S(1)} %get-tuple-element.82.u_ends.u_ref, ...), custom_call_target="tpu_custom_call" | custom-call | tf_op jit(solution)/shard_map/before0/pallas_call | solution.py:691
  11.8 0.7 %stress0.1 = (f32[3,4,16,128]{3,2,1,0:T(8,128)S(1)}, f32[6,2,10,16,128]{4,3,2,1,0:T(8,128)S(1)}, f32[3,25,16,128]{3,2,1,0:T(8,128)S(1)}, f32[3,25,16,128]{3,2,1,...) custom-call(f32[12,16,256]{2,1,0:T(8,128)S(1)} %get-tuple-element.92.known, ...), custom_call_target="tpu_custom_call" | custom-call | tf_op jit(solution)/shard_map/stress0/pallas_call | solution.py:691
  12.4 0.8 %collective-permute-start.6 = (f32[152,128]{1,0:T(8,128)S(1)}, f32[152,128]{1,0:T(8,128)S(1)}, u32[]{:S(2)}, u32[]{:S(2)}) collective-permute-start(f32[152,128]{1,0:T(8,128)S(1)} %get-tuple-element.102), channel_id=1, source_target_pairs={{0,5},{1,4},{2,7},{3,6},{4,1},{5,0},{6,3},{7,2},{8,13},{9,12},{10,... | collective-permute-start | bytes 233480 | tf_op jit(solution)/shard_map/ppermute | solution.py:708
  13.2 0.8 %collective-permute-start.7 = (f32[152,128]{1,0:T(8,128)S(1)}, f32[152,128]{1,0:T(8,128)S(1)}, u32[]{:S(2)}, u32[]{:S(2)}) collective-permute-start(f32[152,128]{1,0:T(8,128)S(1)} %get-tuple-element.103), channel_id=1, source_target_pairs={{0,1},{1,0},{2,3},{3,2},{4,9},{5,8},{6,11},{7,10},{8,5},{9,4},{10,... | collective-permute-start | bytes 233480 | tf_op jit(solution)/shard_map/ppermute | solution.py:708
  14.1 1.2 %between0.1 = (f32[3,3,4,16,128]{4,3,2,1,0:T(8,128)S(1)}, f32[3,3,4,16,128]{4,3,2,1,0:T(8,128)S(1)}, f32[3,4,16,128]{3,2,1,0:T(8,128)S(1)}, f32[45,16,256]{2,1,0...) custom-call(f32[3,25,16,128]{3,2,1,0:T(8,128)S(1)} %get-tuple-elemen, ...), custom_call_target="tpu_custom_call" | custom-call | tf_op jit(solution)/shard_map/between0/pallas_call | solution.py:691
  15.3 1.6 %collective-permute-done.6.a_ref = f32[152,128]{1,0:T(8,128)S(1)} collective-permute-done((f32[152,128]{1,0:T(8,128)S(1)}, f32[152,128]{1,0:T(8,128)S(1)}, u32[]{:S(2)}, u32[]{:S(2)}) %collective-permute-start.6) | collective-permute-done | bytes 77856 | tf_op jit(solution)/shard_map/ppermute | solution.py:708
  16.9 1.4 %collective-permute-done.7.b_ref = f32[152,128]{1,0:T(8,128)S(1)} collective-permute-done((f32[152,128]{1,0:T(8,128)S(1)}, f32[152,128]{1,0:T(8,128)S(1)}, u32[]{:S(2)}, u32[]{:S(2)}) %collective-permute-start.7) | collective-permute-done | bytes 77856 | tf_op jit(solution)/shard_map/ppermute | solution.py:708
  18.3 0.8 %stress1.1 = (f32[3,2,4,8,128]{4,3,2,1,0:T(8,128)S(1)}, f32[3,2,4,8,128]{4,3,2,1,0:T(8,128)S(1)}, f32[2,4,8,128]{3,2,1,0:T(8,128)S(1)}, f32[3,25,16,128]{3,2,1,0...) custom-call(f32[3,4,16,128]{3,2,1,0:T(8,128)S(1)} %get-tuple-element, ...), custom_call_target="tpu_custom_call" | custom-call | tf_op jit(solution)/shard_map/stress1/pallas_call | solution.py:691
  19.1 1.0 %collective-permute-start.8 = (f32[88,128]{1,0:T(8,128)S(1)}, f32[88,128]{1,0:T(8,128)S(1)}, u32[]{:S(2)}, u32[]{:S(2)}) collective-permute-start(f32[88,128]{1,0:T(8,128)S(1)} %get-tuple-element.118), channel_id=1, source_target_pairs={{0,5},{1,4},{2,7},{3,6},{4,1},{5,0},{6,3},{7,2},{8,13},{9,12},{10,... | collective-permute-start | bytes 135176 | tf_op jit(solution)/shard_map/ppermute | solution.py:708
  20.2 0.9 %between1.1 = (f32[3,3,4,8,128]{4,3,2,1,0:T(8,128)S(1)}, f32[3,3,4,8,128]{4,3,2,1,0:T(8,128)S(1)}, f32[3,4,8,128]{3,2,1,0:T(8,128)S(1)}, f32[45,8,256]{2,1,0:T(8...) custom-call(f32[3,25,16,128]{3,2,1,0:T(8,128)S(1)} %get-tuple-elemen, ...), custom_call_target="tpu_custom_call" | custom-call | tf_op jit(solution)/shard_map/between1/pallas_call | solution.py:691
  21.1 1.6 %collective-permute-done.8.a_ref = f32[88,128]{1,0:T(8,128)S(1)} collective-permute-done((f32[88,128]{1,0:T(8,128)S(1)}, f32[88,128]{1,0:T(8,128)S(1)}, u32[]{:S(2)}, u32[]{:S(2)}) %collective-permute-start.8) | collective-permute-done | bytes 45088 | tf_op jit(solution)/shard_map/ppermute | solution.py:708
  22.7 2.0 %collective-permute-done.9.b_ref = f32[88,128]{1,0:T(8,128)S(1)} collective-permute-done((f32[88,128]{1,0:T(8,128)S(1)}, f32[88,128]{1,0:T(8,128)S(1)}, u32[]{:S(2)}, u32[]{:S(2)}) %collective-permute-start.9) | collective-permute-done | bytes 45088 | tf_op jit(solution)/shard_map/ppermute | solution.py:708
  24.7 0.5 %stress2.1 = (f32[3,2,4,8,128]{4,3,2,1,0:T(8,128)S(1)}, f32[3,2,4,8,128]{4,3,2,1,0:T(8,128)S(1)}, f32[6,2,10,8,128]{4,3,2,1,0:T(8,128)S(1)}, f32[3,25,8,128]{3,2...) custom-call(f32[3,2,4,8,128]{4,3,2,1,0:T(8,128)S(1)} %get-tuple-elem, ...), custom_call_target="tpu_custom_call" | custom-call | tf_op jit(solution)/shard_map/stress2/pallas_call | solution.py:691
  25.2 0.9 %collective-permute-start.10 = (f32[64,128]{1,0:T(8,128)S(1)}, f32[64,128]{1,0:T(8,128)S(1)}, u32[]{:S(2)}, u32[]{:S(2)}) collective-permute-start(f32[64,128]{1,0:T(8,128)S(1)} %get-tuple-element.134), channel_id=1, source_target_pairs={{0,5},{1,4},{2,7},{3,6},{4,1},{5,0},{6,3},{7,2},{8,13},{9,12},{10,... | collective-permute-start | bytes 98312 | tf_op jit(solution)/shard_map/ppermute | solution.py:708
  26.0 0.8 %collective-permute-start.11 = (f32[64,128]{1,0:T(8,128)S(1)}, f32[64,128]{1,0:T(8,128)S(1)}, u32[]{:S(2)}, u32[]{:S(2)}) collective-permute-start(f32[64,128]{1,0:T(8,128)S(1)} %get-tuple-element.135), channel_id=1, source_target_pairs={{0,1},{1,0},{2,3},{3,2},{4,9},{5,8},{6,11},{7,10},{8,5},{9,4},{10,... | collective-permute-start | bytes 98312 | tf_op jit(solution)/shard_map/ppermute | solution.py:708
  26.8 0.8 %between2.1 = (f32[3,3,4,8,128]{4,3,2,1,0:T(8,128)S(1)}, f32[3,3,4,8,128]{4,3,2,1,0:T(8,128)S(1)}, f32[3,4,8,128]{3,2,1,0:T(8,128)S(1)}, f32[45,8,256]{2,1,0:T(8...) custom-call(f32[3,25,8,128]{3,2,1,0:T(8,128)S(1)} %get-tuple-element, ...), custom_call_target="tpu_custom_call" | custom-call | tf_op jit(solution)/shard_map/between2/pallas_call | solution.py:691
  27.6 1.0 %collective-permute-done.10.a_ref = f32[64,128]{1,0:T(8,128)S(1)} collective-permute-done((f32[64,128]{1,0:T(8,128)S(1)}, f32[64,128]{1,0:T(8,128)S(1)}, u32[]{:S(2)}, u32[]{:S(2)}) %collective-permute-start.10) | collective-permute-done | bytes 32800 | tf_op jit(solution)/shard_map/ppermute | solution.py:708
  28.6 1.7 %collective-permute-done.11.b_ref = f32[64,128]{1,0:T(8,128)S(1)} collective-permute-done((f32[64,128]{1,0:T(8,128)S(1)}, f32[64,128]{1,0:T(8,128)S(1)}, u32[]{:S(2)}, u32[]{:S(2)}) %collective-permute-start.11) | collective-permute-done | bytes 32800 | tf_op jit(solution)/shard_map/ppermute | solution.py:708
  30.3 0.5 %stress3.1 = (f32[3,2,4,8,128]{4,3,2,1,0:T(8,128)S(1)}, f32[3,2,4,8,128]{4,3,2,1,0:T(8,128)S(1)}, f32[3,25,8,128]{3,2,1,0:T(8,128)S(1)}, f32[3,25,8,128]{3,2,1,0...) custom-call(f32[3,2,4,8,128]{4,3,2,1,0:T(8,128)S(1)} %get-tuple-element.131.u_ref, ...), custom_call_target="tpu_custom_call" | custom-call | tf_op jit(solution)/shard_map/stress3/pallas_call | solution.py:691
  30.8 1.1 %collective-permute-start.13 = (f32[48,128]{1,0:T(8,128)S(1)}, f32[48,128]{1,0:T(8,128)S(1)}, u32[]{:S(2)}, u32[]{:S(2)}) collective-permute-start(f32[48,128]{1,0:T(8,128)S(1)} %get-tuple-element.158), channel_id=1, source_target_pairs={{0,4},{1,5},{2,6},{3,7},{4,0},{5,1},{6,2},{7,3},{8,12},{9,13},{10,... | collective-permute-start | bytes 73736 | tf_op jit(solution)/shard_map/ppermute | solution.py:708
  31.8 0.6 %collective-permute-start.14 = (f32[48,128]{1,0:T(8,128)S(1)}, f32[48,128]{1,0:T(8,128)S(1)}, u32[]{:S(2)}, u32[]{:S(2)}) collective-permute-start(f32[48,128]{1,0:T(8,128)S(1)} %get-tuple-element.159), channel_id=1, source_target_pairs={{0,1},{1,0},{2,3},{3,2},{4,9},{5,8},{6,11},{7,10},{8,5},{9,4},{10,... | collective-permute-start | bytes 73736 | tf_op jit(solution)/shard_map/ppermute | solution.py:708
  32.4 0.4 %between3.1.mine = f32[400,128]{1,0:T(8,128)S(1)} custom-call(f32[3,25,8,128]{3,2,1,0:T(8,128)S(1)} %get-tuple-element.147.flux_x, f32[3,25,8,128]{3,2,1,0:T(8,128)S(1)} %get-tuple-element.148.gx, f32[45,8,256]{2,1,0:T(8,128)S(1)} %get-tuple-element.149.gz, f32[3,15,8,128]{3,2,1,0:T(8,128)S(1)} %get-tuple-element.150.gy, ...), custom_call_target="tpu_custom_call" | custom-call | tf_op jit(solution)/shard_map/between3/pallas_call | solution.py:691
  33.0 1.7 %collective-permute-done.13.a_ref = f32[48,128]{1,0:T(8,128)S(1)} collective-permute-done((f32[48,128]{1,0:T(8,128)S(1)}, f32[48,128]{1,0:T(8,128)S(1)}, u32[]{:S(2)}, u32[]{:S(2)}) %collective-permute-start.13) | collective-permute-done | bytes 24608 | tf_op jit(solution)/shard_map/ppermute | solution.py:708
  34.7 1.3 %collective-permute-done.14.b_ref = f32[48,128]{1,0:T(8,128)S(1)} collective-permute-done((f32[48,128]{1,0:T(8,128)S(1)}, f32[48,128]{1,0:T(8,128)S(1)}, u32[]{:S(2)}, u32[]{:S(2)}) %collective-permute-start.14) | collective-permute-done | bytes 24608 | tf_op jit(solution)/shard_map/ppermute | solution.py:708
  36.0 0.7 %end.1 = (f32[3,4,16,128]{3,2,1,0:T(8,128)}, f32[3,4,16,128]{3,2,1,0:T(8,128)}) custom-call(f32[400,128]{1,0:T(8,128)S(1)} %between3.1.mine, f32[400,128]{1,0:T(8,128)S(1)} %collective-permute-done.12.core, f32[48,128]{1,0:T(8,128)S(1)} %pick.1.force_ref), custom_call_target="tpu_custom_call" | custom-call | tf_op jit(solution)/shard_map/end/pallas_call | solution.py:691
  (16 shorter events, 0.6 us)
Async XLA Ops:
  0.6 4.9 %collective-permute-start.1 = (f32[192,128]{1,0:T(8,128)}, f32[192,128]{1,0:T(8,128)S(1)}, u32[]{:S(2)}, u32[]{:S(2)}) collective-permute-start(f32[192,128]{1,0:T(8,128)} %bitcast.4), channel_id=1, source_target_pairs={{0,8},{1,2},{2,1},{3,11},{4,5},{5,7},{6,4},{7,6},{8,0},{9,10},{10,... | collective-permute-start | bytes 294920 | tf_op jit(solution)/shard_map/ppermute | solution.py:708
  2.3 3.3 %collective-permute-start = (f32[192,128]{1,0:T(8,128)}, f32[192,128]{1,0:T(8,128)S(1)}, u32[]{:S(2)}, u32[]{:S(2)}) collective-permute-start(f32[192,128]{1,0:T(8,128)} %bitcast.5), channel_id=1, source_target_pairs={{0,1},{1,0},{2,3},{3,2},{4,5},{5,4},{6,7},{7,6},{8,9},{9,8},{10,11... | collective-permute-start | bytes 294920 | tf_op jit(solution)/shard_map/ppermute | solution.py:708
  3.6 6.6 %collective-permute-start.3 = (f32[520,128]{1,0:T(8,128)S(1)}, f32[520,128]{1,0:T(8,128)S(1)}, u32[]{:S(2)}, u32[]{:S(2)}) collective-permute-start(f32[520,128]{1,0:T(8,128)S(1)} %pack.1.own_ref.own), channel_id=1, source_target_pairs={{0,8},{1,2},{2,1},{3,11},{4,5},{5,7},{6,4},{7,6},{8,0},{9,10},{10,... | collective-permute-start | bytes 798728 | tf_op jit(solution)/shard_map/ppermute | solution.py:708
  5.3 4.9 %collective-permute-start.2 = (f32[520,128]{1,0:T(8,128)S(1)}, f32[520,128]{1,0:T(8,128)S(1)}, u32[]{:S(2)}, u32[]{:S(2)}) collective-permute-start(f32[520,128]{1,0:T(8,128)S(1)} %pack.1.own_ref.own), channel_id=1, source_target_pairs={{0,1},{1,0},{2,3},{3,2},{4,5},{5,4},{6,7},{7,6},{8,9},{9,8},{10,11... | collective-permute-start | bytes 798728 | tf_op jit(solution)/shard_map/ppermute | solution.py:708
  5.6 6.2 %collective-permute-start.4 = (f32[136,128]{1,0:T(8,128)S(1)}, f32[136,128]{1,0:T(8,128)S(1)}, u32[]{:S(2)}, u32[]{:S(2)}) collective-permute-start(f32[136,128]{1,0:T(8,128)S(1)} %face.1), channel_id=1, source_target_pairs={{0,5},{1,4},{2,7},{3,6},{4,1},{5,0},{6,3},{7,2},{8,13},{9,12},{10,... | collective-permute-start | bytes 208904 | tf_op jit(solution)/shard_map/ppermute | solution.py:708
  5.6 6.1 %collective-permute-start.5 = (f32[136,128]{1,0:T(8,128)S(1)}, f32[136,128]{1,0:T(8,128)S(1)}, u32[]{:S(2)}, u32[]{:S(2)}) collective-permute-start(f32[136,128]{1,0:T(8,128)S(1)} %rim.1.x_ref), channel_id=1, source_target_pairs={{0,1},{1,0},{2,3},{3,2},{4,9},{5,8},{6,11},{7,10},{8,5},{9,4},{10,... | collective-permute-start | bytes 208904 | tf_op jit(solution)/shard_map/ppermute | solution.py:708
  12.4 4.5 %collective-permute-start.6 = (f32[152,128]{1,0:T(8,128)S(1)}, f32[152,128]{1,0:T(8,128)S(1)}, u32[]{:S(2)}, u32[]{:S(2)}) collective-permute-start(f32[152,128]{1,0:T(8,128)S(1)} %get-tuple-element.102), channel_id=1, source_target_pairs={{0,5},{1,4},{2,7},{3,6},{4,1},{5,0},{6,3},{7,2},{8,13},{9,12},{10,... | collective-permute-start | bytes 233480 | tf_op jit(solution)/shard_map/ppermute | solution.py:708
  13.2 5.1 %collective-permute-start.7 = (f32[152,128]{1,0:T(8,128)S(1)}, f32[152,128]{1,0:T(8,128)S(1)}, u32[]{:S(2)}, u32[]{:S(2)}) collective-permute-start(f32[152,128]{1,0:T(8,128)S(1)} %get-tuple-element.103), channel_id=1, source_target_pairs={{0,1},{1,0},{2,3},{3,2},{4,9},{5,8},{6,11},{7,10},{8,5},{9,4},{10,... | collective-permute-start | bytes 233480 | tf_op jit(solution)/shard_map/ppermute | solution.py:708
  19.1 3.6 %collective-permute-start.8 = (f32[88,128]{1,0:T(8,128)S(1)}, f32[88,128]{1,0:T(8,128)S(1)}, u32[]{:S(2)}, u32[]{:S(2)}) collective-permute-start(f32[88,128]{1,0:T(8,128)S(1)} %get-tuple-element.118), channel_id=1, source_target_pairs={{0,5},{1,4},{2,7},{3,6},{4,1},{5,0},{6,3},{7,2},{8,13},{9,12},{10,... | collective-permute-start | bytes 135176 | tf_op jit(solution)/shard_map/ppermute | solution.py:708
  20.2 4.5 %collective-permute-start.9 = (f32[88,128]{1,0:T(8,128)S(1)}, f32[88,128]{1,0:T(8,128)S(1)}, u32[]{:S(2)}, u32[]{:S(2)}) collective-permute-start(f32[88,128]{1,0:T(8,128)S(1)} %get-tuple-element.119), channel_id=1, source_target_pairs={{0,1},{1,0},{2,3},{3,2},{4,9},{5,8},{6,11},{7,10},{8,5},{9,4},{10,... | collective-permute-start | bytes 135176 | tf_op jit(solution)/shard_map/ppermute | solution.py:708
  25.2 3.4 %collective-permute-start.10 = (f32[64,128]{1,0:T(8,128)S(1)}, f32[64,128]{1,0:T(8,128)S(1)}, u32[]{:S(2)}, u32[]{:S(2)}) collective-permute-start(f32[64,128]{1,0:T(8,128)S(1)} %get-tuple-element.134), channel_id=1, source_target_pairs={{0,5},{1,4},{2,7},{3,6},{4,1},{5,0},{6,3},{7,2},{8,13},{9,12},{10,... | collective-permute-start | bytes 98312 | tf_op jit(solution)/shard_map/ppermute | solution.py:708
  26.0 4.3 %collective-permute-start.11 = (f32[64,128]{1,0:T(8,128)S(1)}, f32[64,128]{1,0:T(8,128)S(1)}, u32[]{:S(2)}, u32[]{:S(2)}) collective-permute-start(f32[64,128]{1,0:T(8,128)S(1)} %get-tuple-element.135), channel_id=1, source_target_pairs={{0,1},{1,0},{2,3},{3,2},{4,9},{5,8},{6,11},{7,10},{8,5},{9,4},{10,... | collective-permute-start | bytes 98312 | tf_op jit(solution)/shard_map/ppermute | solution.py:708
  30.8 3.9 %collective-permute-start.13 = (f32[48,128]{1,0:T(8,128)S(1)}, f32[48,128]{1,0:T(8,128)S(1)}, u32[]{:S(2)}, u32[]{:S(2)}) collective-permute-start(f32[48,128]{1,0:T(8,128)S(1)} %get-tuple-element.158), channel_id=1, source_target_pairs={{0,4},{1,5},{2,6},{3,7},{4,0},{5,1},{6,2},{7,3},{8,12},{9,13},{10,... | collective-permute-start | bytes 73736 | tf_op jit(solution)/shard_map/ppermute | solution.py:708
  31.8 4.2 %collective-permute-start.14 = (f32[48,128]{1,0:T(8,128)S(1)}, f32[48,128]{1,0:T(8,128)S(1)}, u32[]{:S(2)}, u32[]{:S(2)}) collective-permute-start(f32[48,128]{1,0:T(8,128)S(1)} %get-tuple-element.159), channel_id=1, source_target_pairs={{0,1},{1,0},{2,3},{3,2},{4,9},{5,8},{6,11},{7,10},{8,5},{9,4},{10,... | collective-permute-start | bytes 73736 | tf_op jit(solution)/shard_map/ppermute | solution.py:708
  32.8 3.2 %collective-permute-start.12 = (f32[400,128]{1,0:T(8,128)S(1)}, f32[400,128]{1,0:T(8,128)S(1)}, u32[]{:S(2)}, u32[]{:S(2)}) collective-permute-start(f32[400,128]{1,0:T(8,128)S(1)} %between3.1.mine), channel_id=1, source_target_pairs={{0,1},{1,0},{2,3},{3,2},{4,5},{5,4},{6,7},{7,6},{8,9},{9,8},{10,11... | collective-permute-start | bytes 614408 | tf_op jit(solution)/shard_map/ppermute | solution.py:708

commit v7 on v6

--- a/solution.py
+++ b/solution.py
@@ -386,8 +386,6 @@
             y = apply5_ends(D, points[c][0][j], points[c][1][j], [px[c, 5 * i + j] for i in range(5)])
             for i in range(5):
                 gx[c, 5 * i + j] = y[i]
-                if 0 < i < 4:
-                    flux_x[c, 5 * i + j] = scale[min(c, 1), 5 * i + j - 5] * y[i] + part[c, 5 * i + j - 5]
     mask = inside(lanes)
     for h in range(tall // 8):
         at = slice(8 * h, 8 * h + 8)
@@ -433,6 +431,9 @@
                 rows.append(flux_z[c, e, first + 1 : first + 4].reshape(3 * tall, lanes))
         parts.append(jnp.concatenate(rows, axis=0))
     qz[...] = div_z(*parts, div_ref).reshape(qz.shape)
+    for c in range(3):
+        for p in range(5, 20):
+            flux_x[c, p] = scale[min(c, 1), p - 5] * gx[c, p] + part[c, p - 5]
     assemble((0, 4), flux_x, flux_y, qz, lambda c, side, j, value: total.__setitem__((c, side, j), value))
 
 

time: 37.2 us -> 37.2 us (level)
  no operation moved by 1% of the time
where the time goes in v7:
time: 37.2 us; the launch traced here: 36.7 us
  waiting for transfers between devices  15.5 us (42%)
  starting transfers between devices  11.1 us (30%)
  Pallas kernels  9.42 us (25%)
  between operations  0.77 us (2%)
    ppermute x15, waiting for transfers between devices, move(): return lax.ppermute(x, ('px', 'py'), pairs_of(kind, nx, ny))  15.5 us
    ppermute x15, starting transfers between devices, move(): return lax.ppermute(x, ('px', 'py'), pairs_of(kind, nx, ny))  11.1 us
    pallas_call x17, Pallas kernels, call(): pl.pallas_call(kernel, out_shape=shapes, scratch_shapes=[pltpu.VMEM(s, F3...  8.14 us
    pallas_call x1, Pallas kernels, shards(): pl.pallas_call(functools.partial(load_kernel, len(sources)), out_shape=[p...  1.27 us
  transfers between devices with their start and end apart: 15, of which 10 were waited for; matrix products, arithmetic and copies ran while one was open for 0% of the time, Pallas kernels for 17%

profile of v7, /device:TPU:16, one launch (start us, length us, event | category | flops | bytes accessed | tf_op | source)
XLA Modules:
  0.0 36.7 jit_solution(290143543494445535)
XLA Ops:
  0.6 1.6 %collective-permute-start.1 = (f32[192,128]{1,0:T(8,128)}, f32[192,128]{1,0:T(8,128)S(1)}, u32[]{:S(2)}, u32[]{:S(2)}) collective-permute-start(f32[192,128]{1,0:T(8,128)} %bitcast.4), channel_id=1, source_target_pairs={{0,8},{1,2},{2,1},{3,11},{4,5},{5,7},{6,4},{7,6},{8,0},{9,10},{10,... | collective-permute-start | bytes 294920 | tf_op jit(solution)/shard_map/ppermute | solution.py:709
  2.3 1.3 %load.1 = (f32[192,128]{1,0:T(8,128)S(1)}, f32[192,128]{1,0:T(8,128)S(1)}, f32[64,128]{1,0:T(8,128)S(1)}, f32[5,5,5,1,128]{4,3,2,1,0:T(1,128)S(1)}, f32[5,5,5,1,...) custom-call(f32[192,128]{1,0:T(8,128)} %bitcast.6, ...), custom_call_target="tpu_custom_call" | custom-call | tf_op jit(solution)/shard_map/load/pallas_call | solution.py:722
  3.6 1.6 %collective-permute-start.3 = (f32[520,128]{1,0:T(8,128)S(1)}, f32[520,128]{1,0:T(8,128)S(1)}, u32[]{:S(2)}, u32[]{:S(2)}) collective-permute-start(f32[520,128]{1,0:T(8,128)S(1)} %pack.1.own_ref.own), channel_id=1, source_target_pairs={{0,8},{1,2},{2,1},{3,11},{4,5},{5,7},{6,4},{7,6},{8,0},{9,10},{10,... | collective-permute-start | bytes 798728 | tf_op jit(solution)/shard_map/ppermute | solution.py:709
  5.3 0.2 collective-permute-done.1.o.chip
  5.6 1.6 %collective-permute-start.5 = (f32[136,128]{1,0:T(8,128)S(1)}, f32[136,128]{1,0:T(8,128)S(1)}, u32[]{:S(2)}, u32[]{:S(2)}) collective-permute-start(f32[136,128]{1,0:T(8,128)S(1)} %rim.1.x_ref), channel_id=1, source_target_pairs={{0,1},{1,0},{2,3},{3,2},{4,9},{5,8},{6,11},{7,10},{8,5},{9,4},{10,... | collective-permute-start | bytes 208904 | tf_op jit(solution)/shard_map/ppermute | solution.py:709
  7.4 2.8 %collective-permute-done.3.o_ref.o = f32[520,128]{1,0:T(8,128)S(1)} collective-permute-done((f32[520,128]{1,0:T(8,128)S(1)}, f32[520,128]{1,0:T(8,128)S(1)}, u32[]{:S(2)}, u32[]{:S(2)}) %collective-permute-start.3) | collective-permute-done | bytes 266272 | tf_op jit(solution)/shard_map/ppermute | solution.py:709
  10.2 1.0 %tables.1 = (f32[2,2,25,16,128]{4,3,2,1,0:T(8,128)S(1)}, f32[2,16,128]{2,1,0:T(8,128)S(1)}) custom-call(f32[520,128]{1,0:T(8,128)S(1)} %pack.1.own_ref.own, f32[520,128]{1,0:T(8,128)S(1)} %collective-permute-done.2.e_ref.e, f32[520,128]{1,0:T(8,128)S(1)} %collective-permute-done.3.o_ref.o, f32[50,128]{1,0:T(8,128)S(1)} %get-tuple-element.89.weight_ref), custom_call_target="tpu_custom_call" | custom-call | tf_op jit(solution)/shard_map/tables/pallas_call | solution.py:692
  11.2 0.4 %before0.1 = (f32[45,16,256]{2,1,0:T(8,128)S(1)}, f32[3,15,16,128]{3,2,1,0:T(8,128)S(1)}, f32[3,25,16,128]{3,2,1,0:T(8,128)S(1)}, f32[3,15,16,128]{3,2,1,0:T(8,1...) custom-call(f32[3,4,16,128]{3,2,1,0:T(8,128)S(1)} %get-tuple-element.82.u_ends.u_ref, ...), custom_call_target="tpu_custom_call" | custom-call | tf_op jit(solution)/shard_map/before0/pallas_call | solution.py:692
  11.8 0.6 %stress0.1 = (f32[3,4,16,128]{3,2,1,0:T(8,128)S(1)}, f32[6,2,10,16,128]{4,3,2,1,0:T(8,128)S(1)}, f32[3,25,16,128]{3,2,1,0:T(8,128)S(1)}, f32[3,25,16,128]{3,2,1,...) custom-call(f32[12,16,256]{2,1,0:T(8,128)S(1)} %get-tuple-element.92.known, ...), custom_call_target="tpu_custom_call" | custom-call | tf_op jit(solution)/shard_map/stress0/pallas_call | solution.py:692
  12.4 0.8 %collective-permute-start.6 = (f32[152,128]{1,0:T(8,128)S(1)}, f32[152,128]{1,0:T(8,128)S(1)}, u32[]{:S(2)}, u32[]{:S(2)}) collective-permute-start(f32[152,128]{1,0:T(8,128)S(1)} %get-tuple-element.102), channel_id=1, source_target_pairs={{0,5},{1,4},{2,7},{3,6},{4,1},{5,0},{6,3},{7,2},{8,13},{9,12},{10,... | collective-permute-start | bytes 233480 | tf_op jit(solution)/shard_map/ppermute | solution.py:709
  13.2 0.8 %collective-permute-start.7 = (f32[152,128]{1,0:T(8,128)S(1)}, f32[152,128]{1,0:T(8,128)S(1)}, u32[]{:S(2)}, u32[]{:S(2)}) collective-permute-start(f32[152,128]{1,0:T(8,128)S(1)} %get-tuple-element.103), channel_id=1, source_target_pairs={{0,1},{1,0},{2,3},{3,2},{4,9},{5,8},{6,11},{7,10},{8,5},{9,4},{10,... | collective-permute-start | bytes 233480 | tf_op jit(solution)/shard_map/ppermute | solution.py:709
  14.0 1.2 %between0.1 = (f32[3,3,4,16,128]{4,3,2,1,0:T(8,128)S(1)}, f32[3,3,4,16,128]{4,3,2,1,0:T(8,128)S(1)}, f32[3,4,16,128]{3,2,1,0:T(8,128)S(1)}, f32[45,16,256]{2,1,0...) custom-call(f32[3,25,16,128]{3,2,1,0:T(8,128)S(1)} %get-tuple-elemen, ...), custom_call_target="tpu_custom_call" | custom-call | tf_op jit(solution)/shard_map/between0/pallas_call | solution.py:692
  15.2 1.6 %collective-permute-done.6.a_ref = f32[152,128]{1,0:T(8,128)S(1)} collective-permute-done((f32[152,128]{1,0:T(8,128)S(1)}, f32[152,128]{1,0:T(8,128)S(1)}, u32[]{:S(2)}, u32[]{:S(2)}) %collective-permute-start.6) | collective-permute-done | bytes 77856 | tf_op jit(solution)/shard_map/ppermute | solution.py:709
  16.9 1.5 %collective-permute-done.7.b_ref = f32[152,128]{1,0:T(8,128)S(1)} collective-permute-done((f32[152,128]{1,0:T(8,128)S(1)}, f32[152,128]{1,0:T(8,128)S(1)}, u32[]{:S(2)}, u32[]{:S(2)}) %collective-permute-start.7) | collective-permute-done | bytes 77856 | tf_op jit(solution)/shard_map/ppermute | solution.py:709
  18.3 0.9 %stress1.1 = (f32[3,2,4,8,128]{4,3,2,1,0:T(8,128)S(1)}, f32[3,2,4,8,128]{4,3,2,1,0:T(8,128)S(1)}, f32[2,4,8,128]{3,2,1,0:T(8,128)S(1)}, f32[3,25,16,128]{3,2,1,0...) custom-call(f32[3,4,16,128]{3,2,1,0:T(8,128)S(1)} %get-tuple-element, ...), custom_call_target="tpu_custom_call" | custom-call | tf_op jit(solution)/shard_map/stress1/pallas_call | solution.py:692
  19.2 1.0 %collective-permute-start.8 = (f32[88,128]{1,0:T(8,128)S(1)}, f32[88,128]{1,0:T(8,128)S(1)}, u32[]{:S(2)}, u32[]{:S(2)}) collective-permute-start(f32[88,128]{1,0:T(8,128)S(1)} %get-tuple-element.118), channel_id=1, source_target_pairs={{0,5},{1,4},{2,7},{3,6},{4,1},{5,0},{6,3},{7,2},{8,13},{9,12},{10,... | collective-permute-start | bytes 135176 | tf_op jit(solution)/shard_map/ppermute | solution.py:709
  20.2 0.9 %between1.1 = (f32[3,3,4,8,128]{4,3,2,1,0:T(8,128)S(1)}, f32[3,3,4,8,128]{4,3,2,1,0:T(8,128)S(1)}, f32[3,4,8,128]{3,2,1,0:T(8,128)S(1)}, f32[45,8,256]{2,1,0:T(8...) custom-call(f32[3,25,16,128]{3,2,1,0:T(8,128)S(1)} %get-tuple-elemen, ...), custom_call_target="tpu_custom_call" | custom-call | tf_op jit(solution)/shard_map/between1/pallas_call | solution.py:692
  21.1 1.6 %collective-permute-done.8.a_ref = f32[88,128]{1,0:T(8,128)S(1)} collective-permute-done((f32[88,128]{1,0:T(8,128)S(1)}, f32[88,128]{1,0:T(8,128)S(1)}, u32[]{:S(2)}, u32[]{:S(2)}) %collective-permute-start.8) | collective-permute-done | bytes 45088 | tf_op jit(solution)/shard_map/ppermute | solution.py:709
  22.7 1.9 %collective-permute-done.9.b_ref = f32[88,128]{1,0:T(8,128)S(1)} collective-permute-done((f32[88,128]{1,0:T(8,128)S(1)}, f32[88,128]{1,0:T(8,128)S(1)}, u32[]{:S(2)}, u32[]{:S(2)}) %collective-permute-start.9) | collective-permute-done | bytes 45088 | tf_op jit(solution)/shard_map/ppermute | solution.py:709
  24.7 0.5 %stress2.1 = (f32[3,2,4,8,128]{4,3,2,1,0:T(8,128)S(1)}, f32[3,2,4,8,128]{4,3,2,1,0:T(8,128)S(1)}, f32[6,2,10,8,128]{4,3,2,1,0:T(8,128)S(1)}, f32[3,25,8,128]{3,2...) custom-call(f32[3,2,4,8,128]{4,3,2,1,0:T(8,128)S(1)} %get-tuple-elem, ...), custom_call_target="tpu_custom_call" | custom-call | tf_op jit(solution)/shard_map/stress2/pallas_call | solution.py:692
  25.2 0.9 %collective-permute-start.10 = (f32[64,128]{1,0:T(8,128)S(1)}, f32[64,128]{1,0:T(8,128)S(1)}, u32[]{:S(2)}, u32[]{:S(2)}) collective-permute-start(f32[64,128]{1,0:T(8,128)S(1)} %get-tuple-element.134), channel_id=1, source_target_pairs={{0,5},{1,4},{2,7},{3,6},{4,1},{5,0},{6,3},{7,2},{8,13},{9,12},{10,... | collective-permute-start | bytes 98312 | tf_op jit(solution)/shard_map/ppermute | solution.py:709
  26.0 0.8 %collective-permute-start.11 = (f32[64,128]{1,0:T(8,128)S(1)}, f32[64,128]{1,0:T(8,128)S(1)}, u32[]{:S(2)}, u32[]{:S(2)}) collective-permute-start(f32[64,128]{1,0:T(8,128)S(1)} %get-tuple-element.135), channel_id=1, source_target_pairs={{0,1},{1,0},{2,3},{3,2},{4,9},{5,8},{6,11},{7,10},{8,5},{9,4},{10,... | collective-permute-start | bytes 98312 | tf_op jit(solution)/shard_map/ppermute | solution.py:709
  26.8 0.8 %between2.1 = (f32[3,3,4,8,128]{4,3,2,1,0:T(8,128)S(1)}, f32[3,3,4,8,128]{4,3,2,1,0:T(8,128)S(1)}, f32[3,4,8,128]{3,2,1,0:T(8,128)S(1)}, f32[45,8,256]{2,1,0:T(8...) custom-call(f32[3,25,8,128]{3,2,1,0:T(8,128)S(1)} %get-tuple-element, ...), custom_call_target="tpu_custom_call" | custom-call | tf_op jit(solution)/shard_map/between2/pallas_call | solution.py:692
  27.6 1.0 %collective-permute-done.10.a_ref = f32[64,128]{1,0:T(8,128)S(1)} collective-permute-done((f32[64,128]{1,0:T(8,128)S(1)}, f32[64,128]{1,0:T(8,128)S(1)}, u32[]{:S(2)}, u32[]{:S(2)}) %collective-permute-start.10) | collective-permute-done | bytes 32800 | tf_op jit(solution)/shard_map/ppermute | solution.py:709
  28.6 1.7 %collective-permute-done.11.b_ref = f32[64,128]{1,0:T(8,128)S(1)} collective-permute-done((f32[64,128]{1,0:T(8,128)S(1)}, f32[64,128]{1,0:T(8,128)S(1)}, u32[]{:S(2)}, u32[]{:S(2)}) %collective-permute-start.11) | collective-permute-done | bytes 32800 | tf_op jit(solution)/shard_map/ppermute | solution.py:709
  30.3 0.5 %stress3.1 = (f32[3,2,4,8,128]{4,3,2,1,0:T(8,128)S(1)}, f32[3,2,4,8,128]{4,3,2,1,0:T(8,128)S(1)}, f32[3,25,8,128]{3,2,1,0:T(8,128)S(1)}, f32[3,25,8,128]{3,2,1,0...) custom-call(f32[3,2,4,8,128]{4,3,2,1,0:T(8,128)S(1)} %get-tuple-element.131.u_ref, ...), custom_call_target="tpu_custom_call" | custom-call | tf_op jit(solution)/shard_map/stress3/pallas_call | solution.py:692
  30.8 1.1 %collective-permute-start.13 = (f32[48,128]{1,0:T(8,128)S(1)}, f32[48,128]{1,0:T(8,128)S(1)}, u32[]{:S(2)}, u32[]{:S(2)}) collective-permute-start(f32[48,128]{1,0:T(8,128)S(1)} %get-tuple-element.158), channel_id=1, source_target_pairs={{0,4},{1,5},{2,6},{3,7},{4,0},{5,1},{6,2},{7,3},{8,12},{9,13},{10,... | collective-permute-start | bytes 73736 | tf_op jit(solution)/shard_map/ppermute | solution.py:709
  31.8 0.6 %collective-permute-start.14 = (f32[48,128]{1,0:T(8,128)S(1)}, f32[48,128]{1,0:T(8,128)S(1)}, u32[]{:S(2)}, u32[]{:S(2)}) collective-permute-start(f32[48,128]{1,0:T(8,128)S(1)} %get-tuple-element.159), channel_id=1, source_target_pairs={{0,1},{1,0},{2,3},{3,2},{4,9},{5,8},{6,11},{7,10},{8,5},{9,4},{10,... | collective-permute-start | bytes 73736 | tf_op jit(solution)/shard_map/ppermute | solution.py:709
  32.4 0.4 %between3.1.mine = f32[400,128]{1,0:T(8,128)S(1)} custom-call(f32[3,25,8,128]{3,2,1,0:T(8,128)S(1)} %get-tuple-element.147.flux_x, f32[3,25,8,128]{3,2,1,0:T(8,128)S(1)} %get-tuple-element.148.gx, f32[45,8,256]{2,1,0:T(8,128)S(1)} %get-tuple-element.149.gz, f32[3,15,8,128]{3,2,1,0:T(8,128)S(1)} %get-tuple-element.150.gy, ...), custom_call_target="tpu_custom_call" | custom-call | tf_op jit(solution)/shard_map/between3/pallas_call | solution.py:692
  33.0 1.7 %collective-permute-done.13.a_ref = f32[48,128]{1,0:T(8,128)S(1)} collective-permute-done((f32[48,128]{1,0:T(8,128)S(1)}, f32[48,128]{1,0:T(8,128)S(1)}, u32[]{:S(2)}, u32[]{:S(2)}) %collective-permute-start.13) | collective-permute-done | bytes 24608 | tf_op jit(solution)/shard_map/ppermute | solution.py:709
  34.7 1.3 %collective-permute-done.14.b_ref = f32[48,128]{1,0:T(8,128)S(1)} collective-permute-done((f32[48,128]{1,0:T(8,128)S(1)}, f32[48,128]{1,0:T(8,128)S(1)}, u32[]{:S(2)}, u32[]{:S(2)}) %collective-permute-start.14) | collective-permute-done | bytes 24608 | tf_op jit(solution)/shard_map/ppermute | solution.py:709
  36.0 0.7 %end.1 = (f32[3,4,16,128]{3,2,1,0:T(8,128)}, f32[3,4,16,128]{3,2,1,0:T(8,128)}) custom-call(f32[400,128]{1,0:T(8,128)S(1)} %between3.1.mine, f32[400,128]{1,0:T(8,128)S(1)} %collective-permute-done.12.core, f32[48,128]{1,0:T(8,128)S(1)} %pick.1.force_ref), custom_call_target="tpu_custom_call" | custom-call | tf_op jit(solution)/shard_map/end/pallas_call | solution.py:692
  (16 shorter events, 0.6 us)
Async XLA Ops:
  0.6 4.9 %collective-permute-start.1 = (f32[192,128]{1,0:T(8,128)}, f32[192,128]{1,0:T(8,128)S(1)}, u32[]{:S(2)}, u32[]{:S(2)}) collective-permute-start(f32[192,128]{1,0:T(8,128)} %bitcast.4), channel_id=1, source_target_pairs={{0,8},{1,2},{2,1},{3,11},{4,5},{5,7},{6,4},{7,6},{8,0},{9,10},{10,... | collective-permute-start | bytes 294920 | tf_op jit(solution)/shard_map/ppermute | solution.py:709
  2.3 3.3 %collective-permute-start = (f32[192,128]{1,0:T(8,128)}, f32[192,128]{1,0:T(8,128)S(1)}, u32[]{:S(2)}, u32[]{:S(2)}) collective-permute-start(f32[192,128]{1,0:T(8,128)} %bitcast.5), channel_id=1, source_target_pairs={{0,1},{1,0},{2,3},{3,2},{4,5},{5,4},{6,7},{7,6},{8,9},{9,8},{10,11... | collective-permute-start | bytes 294920 | tf_op jit(solution)/shard_map/ppermute | solution.py:709
  3.6 6.6 %collective-permute-start.3 = (f32[520,128]{1,0:T(8,128)S(1)}, f32[520,128]{1,0:T(8,128)S(1)}, u32[]{:S(2)}, u32[]{:S(2)}) collective-permute-start(f32[520,128]{1,0:T(8,128)S(1)} %pack.1.own_ref.own), channel_id=1, source_target_pairs={{0,8},{1,2},{2,1},{3,11},{4,5},{5,7},{6,4},{7,6},{8,0},{9,10},{10,... | collective-permute-start | bytes 798728 | tf_op jit(solution)/shard_map/ppermute | solution.py:709
  5.3 4.9 %collective-permute-start.2 = (f32[520,128]{1,0:T(8,128)S(1)}, f32[520,128]{1,0:T(8,128)S(1)}, u32[]{:S(2)}, u32[]{:S(2)}) collective-permute-start(f32[520,128]{1,0:T(8,128)S(1)} %pack.1.own_ref.own), channel_id=1, source_target_pairs={{0,1},{1,0},{2,3},{3,2},{4,5},{5,4},{6,7},{7,6},{8,9},{9,8},{10,11... | collective-permute-start | bytes 798728 | tf_op jit(solution)/shard_map/ppermute | solution.py:709
  5.6 6.2 %collective-permute-start.4 = (f32[136,128]{1,0:T(8,128)S(1)}, f32[136,128]{1,0:T(8,128)S(1)}, u32[]{:S(2)}, u32[]{:S(2)}) collective-permute-start(f32[136,128]{1,0:T(8,128)S(1)} %face.1), channel_id=1, source_target_pairs={{0,5},{1,4},{2,7},{3,6},{4,1},{5,0},{6,3},{7,2},{8,13},{9,12},{10,... | collective-permute-start | bytes 208904 | tf_op jit(solution)/shard_map/ppermute | solution.py:709
  5.6 6.1 %collective-permute-start.5 = (f32[136,128]{1,0:T(8,128)S(1)}, f32[136,128]{1,0:T(8,128)S(1)}, u32[]{:S(2)}, u32[]{:S(2)}) collective-permute-start(f32[136,128]{1,0:T(8,128)S(1)} %rim.1.x_ref), channel_id=1, source_target_pairs={{0,1},{1,0},{2,3},{3,2},{4,9},{5,8},{6,11},{7,10},{8,5},{9,4},{10,... | collective-permute-start | bytes 208904 | tf_op jit(solution)/shard_map/ppermute | solution.py:709
  12.4 4.5 %collective-permute-start.6 = (f32[152,128]{1,0:T(8,128)S(1)}, f32[152,128]{1,0:T(8,128)S(1)}, u32[]{:S(2)}, u32[]{:S(2)}) collective-permute-start(f32[152,128]{1,0:T(8,128)S(1)} %get-tuple-element.102), channel_id=1, source_target_pairs={{0,5},{1,4},{2,7},{3,6},{4,1},{5,0},{6,3},{7,2},{8,13},{9,12},{10,... | collective-permute-start | bytes 233480 | tf_op jit(solution)/shard_map/ppermute | solution.py:709
  13.2 5.1 %collective-permute-start.7 = (f32[152,128]{1,0:T(8,128)S(1)}, f32[152,128]{1,0:T(8,128)S(1)}, u32[]{:S(2)}, u32[]{:S(2)}) collective-permute-start(f32[152,128]{1,0:T(8,128)S(1)} %get-tuple-element.103), channel_id=1, source_target_pairs={{0,1},{1,0},{2,3},{3,2},{4,9},{5,8},{6,11},{7,10},{8,5},{9,4},{10,... | collective-permute-start | bytes 233480 | tf_op jit(solution)/shard_map/ppermute | solution.py:709
  19.2 3.5 %collective-permute-start.8 = (f32[88,128]{1,0:T(8,128)S(1)}, f32[88,128]{1,0:T(8,128)S(1)}, u32[]{:S(2)}, u32[]{:S(2)}) collective-permute-start(f32[88,128]{1,0:T(8,128)S(1)} %get-tuple-element.118), channel_id=1, source_target_pairs={{0,5},{1,4},{2,7},{3,6},{4,1},{5,0},{6,3},{7,2},{8,13},{9,12},{10,... | collective-permute-start | bytes 135176 | tf_op jit(solution)/shard_map/ppermute | solution.py:709
  20.2 4.5 %collective-permute-start.9 = (f32[88,128]{1,0:T(8,128)S(1)}, f32[88,128]{1,0:T(8,128)S(1)}, u32[]{:S(2)}, u32[]{:S(2)}) collective-permute-start(f32[88,128]{1,0:T(8,128)S(1)} %get-tuple-element.119), channel_id=1, source_target_pairs={{0,1},{1,0},{2,3},{3,2},{4,9},{5,8},{6,11},{7,10},{8,5},{9,4},{10,... | collective-permute-start | bytes 135176 | tf_op jit(solution)/shard_map/ppermute | solution.py:709
  25.2 3.4 %collective-permute-start.10 = (f32[64,128]{1,0:T(8,128)S(1)}, f32[64,128]{1,0:T(8,128)S(1)}, u32[]{:S(2)}, u32[]{:S(2)}) collective-permute-start(f32[64,128]{1,0:T(8,128)S(1)} %get-tuple-element.134), channel_id=1, source_target_pairs={{0,5},{1,4},{2,7},{3,6},{4,1},{5,0},{6,3},{7,2},{8,13},{9,12},{10,... | collective-permute-start | bytes 98312 | tf_op jit(solution)/shard_map/ppermute | solution.py:709
  26.0 4.3 %collective-permute-start.11 = (f32[64,128]{1,0:T(8,128)S(1)}, f32[64,128]{1,0:T(8,128)S(1)}, u32[]{:S(2)}, u32[]{:S(2)}) collective-permute-start(f32[64,128]{1,0:T(8,128)S(1)} %get-tuple-element.135), channel_id=1, source_target_pairs={{0,1},{1,0},{2,3},{3,2},{4,9},{5,8},{6,11},{7,10},{8,5},{9,4},{10,... | collective-permute-start | bytes 98312 | tf_op jit(solution)/shard_map/ppermute | solution.py:709
  30.8 3.9 %collective-permute-start.13 = (f32[48,128]{1,0:T(8,128)S(1)}, f32[48,128]{1,0:T(8,128)S(1)}, u32[]{:S(2)}, u32[]{:S(2)}) collective-permute-start(f32[48,128]{1,0:T(8,128)S(1)} %get-tuple-element.158), channel_id=1, source_target_pairs={{0,4},{1,5},{2,6},{3,7},{4,0},{5,1},{6,2},{7,3},{8,12},{9,13},{10,... | collective-permute-start | bytes 73736 | tf_op jit(solution)/shard_map/ppermute | solution.py:709
  31.8 4.2 %collective-permute-start.14 = (f32[48,128]{1,0:T(8,128)S(1)}, f32[48,128]{1,0:T(8,128)S(1)}, u32[]{:S(2)}, u32[]{:S(2)}) collective-permute-start(f32[48,128]{1,0:T(8,128)S(1)} %get-tuple-element.159), channel_id=1, source_target_pairs={{0,1},{1,0},{2,3},{3,2},{4,9},{5,8},{6,11},{7,10},{8,5},{9,4},{10,... | collective-permute-start | bytes 73736 | tf_op jit(solution)/shard_map/ppermute | solution.py:709
  32.8 3.2 %collective-permute-start.12 = (f32[400,128]{1,0:T(8,128)S(1)}, f32[400,128]{1,0:T(8,128)S(1)}, u32[]{:S(2)}, u32[]{:S(2)}) collective-permute-start(f32[400,128]{1,0:T(8,128)S(1)} %between3.1.mine), channel_id=1, source_target_pairs={{0,1},{1,0},{2,3},{3,2},{4,5},{5,4},{6,7},{7,6},{8,9},{9,8},{10,11... | collective-permute-start | bytes 614408 | tf_op jit(solution)/shard_map/ppermute | solution.py:709
